TPU v7x, 512 devices: a whole 4x4x16 slice. The times are simulated.
512 devices in a mesh: ctx: 64 (over z, y_lo, core), tp: 8 (over y_hi, x).
Axes of the slice: x: 4, y: 4 (y_hi: 2, y_lo: 2; y = y_hi * 2 + y_lo), z: 16, core: 2. Of those that a mesh axis runs over, the one named last changes fastest.
Arguments:
- queries: bfloat16 [8192, 32, 128], P('ctx', 'tp'), may hold values from -20 to 20
- prompt_kv: bfloat16 [16384, 2, 8, 128], P('ctx', None, 'tp'), may hold values from -20 to 20
- response_kv: bfloat16 [8192, 2, 8, 128], P('ctx', None, 'tp'), may hold values from -6 to 6
- logits: bfloat16 [8192, 76800], P('ctx', 'tp'), may hold values from -330 to 330
- token_ids: int32 [8192], P('ctx'), may hold values from 0 to 76799
- lengths: int32 [16], replicated, may hold values from 1 to 2048, as said below
- rewards: float32 [16], replicated, may hold values from -4 to 4
Outputs:
- context: bfloat16 [8192, 32, 128], P('ctx', 'tp')
- token_logprob: float32 [8192], P('ctx')
- response_objective: float32 [16], replicated
Inputs may be any that keep to these rules, and one draw needn't show every extreme that they name: The lengths sum to 8128; the last response has exactly 2048 rows.
All inputs are finite; a program needn't handle non-finite values.
Results may differ from a plain program's by a relative error of at most 0.01.
Values may be sent and summed in bfloat16 or wider, within the bound.
No kernel may reach another device: no remote copies, remote signals or barrier semaphores. Data moves between devices by JAX's collectives and lax.ppermute only.
A program may use at most 64 MiB of HBM per device.

v0:
```python
import math

import jax
import jax.numpy as jnp
from jax import lax
from jax.sharding import PartitionSpec as P

NEGATIVE = -1e30


def from_behind(block, axis, distance):
    devices = range(lax.axis_size(axis))
    route = [(i - distance, i) for i in devices if i - distance in devices]
    return lax.ppermute(block, axis, route)


def segment_of(row_index, ends_at):
    return jnp.sum((row_index[:, None] >= ends_at[None, :]).astype(jnp.int32), axis=1)


def absorb(carried, keys_part, values_part, key_rows, setting):
    grouped, score_scale, query_rows, query_seg, ends_at, responses, masked = setting
    highest, denominator, weighted = carried
    scores = (
        jnp.einsum("rkgd,nkd->rkgn", grouped, keys_part, preferred_element_type=jnp.float32)
        * score_scale
    )
    if masked:
        key_seg = segment_of(key_rows, ends_at)
        allowed = (key_seg[None, :] == query_seg[:, None]) & (query_seg[:, None] < responses) & (
            key_rows[None, :] <= query_rows[:, None]
        ) & (key_rows[None, :] >= 0) | (key_rows[None, :] == query_rows[:, None])
        allowed = allowed[:, None, None, :]
        scores = jnp.where(allowed, scores, NEGATIVE)
    raised = jnp.maximum(highest, scores.max(-1))
    shrink = jnp.exp(highest - raised)
    weights = jnp.exp(scores - raised[..., None])
    if masked:
        weights = jnp.where(allowed, weights, 0.0)
    denominator = denominator * shrink + weights.sum(-1)
    weighted = weighted * shrink[..., None] + jnp.einsum(
        "rkgn,nkd->rkgd",
        weights.astype(jnp.bfloat16),
        values_part,
        preferred_element_type=jnp.float32,
    )
    return (raised, denominator, weighted)


def absorb_blocks(carried, block_data, first_index, setting):
    length_rows = block_data.shape[0]
    block_size = math.gcd(length_rows, 512)

    def advance(block_number, running):
        offset = block_number * block_size
        section = lax.dynamic_slice_in_dim(block_data, offset, block_size, 0)
        rows_here = first_index + offset + jnp.arange(block_size, dtype=jnp.int32)
        return absorb(running, section[:, 0], section[:, 1], rows_here, setting)

    return lax.fori_loop(0, length_rows // block_size, advance, carried)


def shards(queries, prompt_kv, response_kv, logits, token_ids, lengths, rewards):
    rows_dev, heads_here, head_dim = queries.shape
    kv_here = prompt_kv.shape[2]
    cycle_size = lax.axis_size("ctx")
    position = lax.axis_index("ctx")
    responses = lengths.shape[0]
    ends_at = jnp.cumsum(lengths)
    first_row = position * rows_dev
    query_rows = first_row + jnp.arange(rows_dev, dtype=jnp.int32)
    query_seg = segment_of(query_rows, ends_at)
    grouped = queries.reshape(rows_dev, kv_here, heads_here // kv_here, head_dim)
    score_scale = 1.0 / math.sqrt(head_dim)
    open_setting = (grouped, score_scale, query_rows, query_seg, ends_at, responses, False)
    causal_setting = (grouped, score_scale, query_rows, query_seg, ends_at, responses, True)
    running = (
        jnp.full(grouped.shape[:3], NEGATIVE, jnp.float32),
        jnp.zeros(grouped.shape[:3], jnp.float32),
        jnp.zeros(grouped.shape, jnp.float32),
    )
    running = absorb_blocks(
        running, lax.all_gather(prompt_kv, "ctx", axis=0, tiled=True), jnp.int32(0), open_setting
    )
    longest = min(2048, rows_dev * cycle_size // 4)
    hop_count = min(cycle_size - 1, (longest - 2 + rows_dev) // rows_dev)
    running = absorb_blocks(running, response_kv, first_row, causal_setting)

    def hop(hop_index, carried):
        inner, moving = carried
        moving = from_behind(moving, "ctx", 1)
        inner = absorb_blocks(inner, moving, first_row - hop_index * rows_dev, causal_setting)
        return (inner, moving)

    running, unused_block = lax.fori_loop(1, hop_count + 1, hop, (running, response_kv))
    highest, denominator, weighted = running
    context = (
        (weighted / denominator[..., None])
        .astype(jnp.bfloat16)
        .reshape(rows_dev, heads_here, head_dim)
    )
    vocab_here = logits.shape[1]
    vocab_base = lax.axis_index("tp") * vocab_here
    local_peak = jnp.max(logits, axis=1).astype(jnp.float32)
    widened = logits.astype(jnp.float32)
    local_sum = jnp.sum(jnp.exp(widened - local_peak[:, None]), axis=1)
    columns = jnp.arange(vocab_here, dtype=jnp.int32)
    matches = columns[None, :] == (token_ids - vocab_base)[:, None]
    picked = jnp.sum(jnp.where(matches, widened, 0.0), axis=1)
    global_peak = lax.pmax(local_peak, "tp")
    global_sum, chosen = lax.psum((local_sum * jnp.exp(local_peak - global_peak), picked), "tp")
    logprob = chosen - global_peak - jnp.log(global_sum)
    is_valid = query_seg < responses
    token_logprob = jnp.where(is_valid, logprob, 0.0)
    members = query_seg[:, None] == jnp.arange(responses, dtype=jnp.int32)[None, :]
    partial_sums = jnp.sum(jnp.where(members, token_logprob[:, None], 0.0), axis=0)
    response_sum = lax.psum(partial_sums, "ctx")
    length_float = lengths.astype(jnp.float32)
    adjusted = rewards - 0.5 * length_float / longest
    advantage = adjusted - jnp.mean(adjusted)
    response_objective = -advantage * response_sum / length_float
    return (context, token_logprob, response_objective)


def solution(mesh):
    return jax.shard_map(
        shards,
        mesh=mesh,
        in_specs=(
            P("ctx", "tp", None),
            P("ctx", None, "tp", None),
            P("ctx", None, "tp", None),
            P("ctx", "tp"),
            P("ctx"),
            P(),
            P(),
        ),
        out_specs=(P("ctx", "tp", None), P("ctx"), P()),
        check_vma=False,
    )
```

profile of v0, /device:TPU:258, one launch (start us, length us, event | category | flops | bytes accessed | tf_op | source)
XLA Modules:
  0.0 398.8 jit_solution(3632918570719847902)
XLA Ops:
  7.2 1.6 copy.41
  11.6 2.1 reduce_max.50
  13.7 1.3 fusion.43
  15.6 20.1 %pmax.7 = f32[128]{0:T(128)S(1)} all-reduce(bf16[128]{0:T(256)(128)(2,1)S(1)} %reduce_max.50), channel_id=1, replica_groups=mesh['ctx'=64,'tp'=8] {'tp'}, use_global_device_ids=true, to_apply=%region_16.17 | all-reduce | flops 128 | bytes 768 | tf_op jit(solution)/shard_map/pmax | solution.py:110
  36.3 3.4 fusion.26
  39.8 23.7 %all-reduce = (f32[128]{0:T(128)S(1)}, f32[128]{0:T(128)S(1)}) all-reduce(f32[128]{0:T(128)S(1)} %exponential_multiply_fusion, f32[128]{0:T(128)S(1)} %get-tuple-element.470), channel_id=1, replica_groups=mesh['ctx'=64,'tp'=8] {'tp'}, use_global_device_ids=true, to_apply=%region_18.19 | all-reduce | flops 256 | bytes 2048 | tf_op jit(solution)/shard_map/psum | solution.py:111
  63.7 104.9 %psum.23 = f32[16]{0:T(128)S(1)} all-reduce(f32[16]{0:T(128)S(1)} %select_reduce_fusion), channel_id=1, replica_groups=mesh['ctx'=64,'tp'=8] {'ctx'}, use_global_device_ids=true, to_apply=%region_21.22 | all-reduce | flops 16 | bytes 128 | tf_op jit(solution)/shard_map/psum | solution.py:117
  169.6 87.6 %while.61 = (s32[]{:T(128)}, f32[128,1,4]{0,2,1:T(4,128)S(1)}, f32[128,1,4]{0,2,1:T(4,128)S(1)}, f32[128,1,4,128]{0,3,2,1:T(8,128)S(1)}, bf16[16384,2,1,128]{3,0...) while((s32[]{:T(128)}, f32[128,1,4]{0,2,1:T(4,128)S(1)}, ...), condition=%wide.region_3.4_spmd.clone, body=%wide.region_0.3_spmd.clone.sunk | while | flops 135990272 | bytes 4096199 | solution.py:60
  171.0 1.3 fusion.62
  173.7 1.3 fusion.62
  176.5 1.3 fusion.62
  179.2 1.3 fusion.62
  182.0 1.3 fusion.62
  184.7 1.3 fusion.62
  187.4 1.3 fusion.62
  190.2 1.3 fusion.62
  192.9 1.3 fusion.62
  201.1 1.3 fusion.62
  206.6 1.3 fusion.62
  209.3 1.3 fusion.62
  212.1 1.3 fusion.62
  217.5 1.3 fusion.62
  220.3 1.3 fusion.62
  225.7 1.3 fusion.62
  231.2 1.3 fusion.62
  234.0 1.3 fusion.62
  236.7 1.3 fusion.62
  242.2 1.3 fusion.62
  244.9 1.3 fusion.62
  250.4 1.3 fusion.62
  255.9 1.3 fusion.62
  257.7 133.2 %while.62 = (s32[]{:T(128)}, f32[128,1,4]{0,2,1:T(4,128)S(1)}, f32[128,1,4]{0,2,1:T(4,128)S(1)}, f32[128,1,4,128]{3,0,2,1:T(8,128)S(1)}, bf16[128,2,1,128]{3,0,2...) while((s32[]{:T(128)}, f32[128,1,4]{0,2,1:T(4,128)S(1)}, ...), condition=%wide.region_12.13_spmd.clone.clone, body=%wide.region_8.12_spmd.clone.clone.sunk | while | flops 34398212 | bytes 2004217 | solution.py:95
  257.7 1.9 collective-permute-start
  259.9 5.5 %collective-permute-done = bf16[128,2,1,128]{3,0,2,1:T(8,128)(2,1)S(1)} collective-permute-done((bf16[128,2,1,128]{3,0,2,1:T(8,128)(2,1)S(1)}, bf16[128,2,1,128]{3,0,2,1:T(8,128)(2,1)S(1)}, u32[]{:S(2)}, u32[]{:S(2)}) %collective-permute-start) | collective-permute-done | bytes 65568 | tf_op jit(solution)/shard_map/while/body/eval_jaxpr/ppermute | solution.py:14
  266.0 1.9 collective-permute-start
  268.2 5.5 %collective-permute-done = bf16[128,2,1,128]{3,0,2,1:T(8,128)(2,1)S(1)} collective-permute-done((bf16[128,2,1,128]{3,0,2,1:T(8,128)(2,1)S(1)}, bf16[128,2,1,128]{3,0,2,1:T(8,128)(2,1)S(1)}, u32[]{:S(2)}, u32[]{:S(2)}) %collective-permute-start) | collective-permute-done | bytes 65568 | tf_op jit(solution)/shard_map/while/body/eval_jaxpr/ppermute | solution.py:14
  274.3 1.9 collective-permute-start
  276.5 5.5 %collective-permute-done = bf16[128,2,1,128]{3,0,2,1:T(8,128)(2,1)S(1)} collective-permute-done((bf16[128,2,1,128]{3,0,2,1:T(8,128)(2,1)S(1)}, bf16[128,2,1,128]{3,0,2,1:T(8,128)(2,1)S(1)}, u32[]{:S(2)}, u32[]{:S(2)}) %collective-permute-start) | collective-permute-done | bytes 65568 | tf_op jit(solution)/shard_map/while/body/eval_jaxpr/ppermute | solution.py:14
  282.7 1.9 collective-permute-start
  284.8 5.5 %collective-permute-done = bf16[128,2,1,128]{3,0,2,1:T(8,128)(2,1)S(1)} collective-permute-done((bf16[128,2,1,128]{3,0,2,1:T(8,128)(2,1)S(1)}, bf16[128,2,1,128]{3,0,2,1:T(8,128)(2,1)S(1)}, u32[]{:S(2)}, u32[]{:S(2)}) %collective-permute-start) | collective-permute-done | bytes 65568 | tf_op jit(solution)/shard_map/while/body/eval_jaxpr/ppermute | solution.py:14
  291.0 1.9 collective-permute-start
  293.2 5.5 %collective-permute-done = bf16[128,2,1,128]{3,0,2,1:T(8,128)(2,1)S(1)} collective-permute-done((bf16[128,2,1,128]{3,0,2,1:T(8,128)(2,1)S(1)}, bf16[128,2,1,128]{3,0,2,1:T(8,128)(2,1)S(1)}, u32[]{:S(2)}, u32[]{:S(2)}) %collective-permute-start) | collective-permute-done | bytes 65568 | tf_op jit(solution)/shard_map/while/body/eval_jaxpr/ppermute | solution.py:14
  299.3 1.9 collective-permute-start
  301.5 5.5 %collective-permute-done = bf16[128,2,1,128]{3,0,2,1:T(8,128)(2,1)S(1)} collective-permute-done((bf16[128,2,1,128]{3,0,2,1:T(8,128)(2,1)S(1)}, bf16[128,2,1,128]{3,0,2,1:T(8,128)(2,1)S(1)}, u32[]{:S(2)}, u32[]{:S(2)}) %collective-permute-start) | collective-permute-done | bytes 65568 | tf_op jit(solution)/shard_map/while/body/eval_jaxpr/ppermute | solution.py:14
  307.6 1.9 collective-permute-start
  309.8 5.5 %collective-permute-done = bf16[128,2,1,128]{3,0,2,1:T(8,128)(2,1)S(1)} collective-permute-done((bf16[128,2,1,128]{3,0,2,1:T(8,128)(2,1)S(1)}, bf16[128,2,1,128]{3,0,2,1:T(8,128)(2,1)S(1)}, u32[]{:S(2)}, u32[]{:S(2)}) %collective-permute-start) | collective-permute-done | bytes 65568 | tf_op jit(solution)/shard_map/while/body/eval_jaxpr/ppermute | solution.py:14
  316.0 1.9 collective-permute-start
  318.2 5.5 %collective-permute-done = bf16[128,2,1,128]{3,0,2,1:T(8,128)(2,1)S(1)} collective-permute-done((bf16[128,2,1,128]{3,0,2,1:T(8,128)(2,1)S(1)}, bf16[128,2,1,128]{3,0,2,1:T(8,128)(2,1)S(1)}, u32[]{:S(2)}, u32[]{:S(2)}) %collective-permute-start) | collective-permute-done | bytes 65568 | tf_op jit(solution)/shard_map/while/body/eval_jaxpr/ppermute | solution.py:14
  324.3 1.9 collective-permute-start
  326.5 5.5 %collective-permute-done = bf16[128,2,1,128]{3,0,2,1:T(8,128)(2,1)S(1)} collective-permute-done((bf16[128,2,1,128]{3,0,2,1:T(8,128)(2,1)S(1)}, bf16[128,2,1,128]{3,0,2,1:T(8,128)(2,1)S(1)}, u32[]{:S(2)}, u32[]{:S(2)}) %collective-permute-start) | collective-permute-done | bytes 65568 | tf_op jit(solution)/shard_map/while/body/eval_jaxpr/ppermute | solution.py:14
  332.6 1.9 collective-permute-start
  334.8 5.5 %collective-permute-done = bf16[128,2,1,128]{3,0,2,1:T(8,128)(2,1)S(1)} collective-permute-done((bf16[128,2,1,128]{3,0,2,1:T(8,128)(2,1)S(1)}, bf16[128,2,1,128]{3,0,2,1:T(8,128)(2,1)S(1)}, u32[]{:S(2)}, u32[]{:S(2)}) %collective-permute-start) | collective-permute-done | bytes 65568 | tf_op jit(solution)/shard_map/while/body/eval_jaxpr/ppermute | solution.py:14
  341.0 1.9 collective-permute-start
  343.1 5.5 %collective-permute-done = bf16[128,2,1,128]{3,0,2,1:T(8,128)(2,1)S(1)} collective-permute-done((bf16[128,2,1,128]{3,0,2,1:T(8,128)(2,1)S(1)}, bf16[128,2,1,128]{3,0,2,1:T(8,128)(2,1)S(1)}, u32[]{:S(2)}, u32[]{:S(2)}) %collective-permute-start) | collective-permute-done | bytes 65568 | tf_op jit(solution)/shard_map/while/body/eval_jaxpr/ppermute | solution.py:14
  349.3 1.9 collective-permute-start
  351.5 5.5 %collective-permute-done = bf16[128,2,1,128]{3,0,2,1:T(8,128)(2,1)S(1)} collective-permute-done((bf16[128,2,1,128]{3,0,2,1:T(8,128)(2,1)S(1)}, bf16[128,2,1,128]{3,0,2,1:T(8,128)(2,1)S(1)}, u32[]{:S(2)}, u32[]{:S(2)}) %collective-permute-start) | collective-permute-done | bytes 65568 | tf_op jit(solution)/shard_map/while/body/eval_jaxpr/ppermute | solution.py:14
  357.6 1.9 collective-permute-start
  359.8 5.5 %collective-permute-done = bf16[128,2,1,128]{3,0,2,1:T(8,128)(2,1)S(1)} collective-permute-done((bf16[128,2,1,128]{3,0,2,1:T(8,128)(2,1)S(1)}, bf16[128,2,1,128]{3,0,2,1:T(8,128)(2,1)S(1)}, u32[]{:S(2)}, u32[]{:S(2)}) %collective-permute-start) | collective-permute-done | bytes 65568 | tf_op jit(solution)/shard_map/while/body/eval_jaxpr/ppermute | solution.py:14
  365.9 1.9 collective-permute-start
  368.1 5.5 %collective-permute-done = bf16[128,2,1,128]{3,0,2,1:T(8,128)(2,1)S(1)} collective-permute-done((bf16[128,2,1,128]{3,0,2,1:T(8,128)(2,1)S(1)}, bf16[128,2,1,128]{3,0,2,1:T(8,128)(2,1)S(1)}, u32[]{:S(2)}, u32[]{:S(2)}) %collective-permute-start) | collective-permute-done | bytes 65568 | tf_op jit(solution)/shard_map/while/body/eval_jaxpr/ppermute | solution.py:14
  374.3 1.9 collective-permute-start
  376.5 5.5 %collective-permute-done = bf16[128,2,1,128]{3,0,2,1:T(8,128)(2,1)S(1)} collective-permute-done((bf16[128,2,1,128]{3,0,2,1:T(8,128)(2,1)S(1)}, bf16[128,2,1,128]{3,0,2,1:T(8,128)(2,1)S(1)}, u32[]{:S(2)}, u32[]{:S(2)}) %collective-permute-start) | collective-permute-done | bytes 65568 | tf_op jit(solution)/shard_map/while/body/eval_jaxpr/ppermute | solution.py:14
  382.6 1.9 collective-permute-start
  384.8 5.5 %collective-permute-done = bf16[128,2,1,128]{3,0,2,1:T(8,128)(2,1)S(1)} collective-permute-done((bf16[128,2,1,128]{3,0,2,1:T(8,128)(2,1)S(1)}, bf16[128,2,1,128]{3,0,2,1:T(8,128)(2,1)S(1)}, u32[]{:S(2)}, u32[]{:S(2)}) %collective-permute-start) | collective-permute-done | bytes 65568 | tf_op jit(solution)/shard_map/while/body/eval_jaxpr/ppermute | solution.py:14
  (383 shorter events, 75.3 us)
Async XLA Ops:
  7.2 162.1 %copy-start = (bf16[128,4,128]{2,1,0:T(4,128)(2,1)S(1)}, bf16[128,4,128]{2,1,0:T(4,128)(2,1)}, u32[]{:S(2)}) copy-start(bf16[128,4,128]{2,1,0:T(4,128)(2,1)} %param.11) | copy-start | bytes 393220
  7.2 161.5 %copy-start.1 = (s32[16]{0:T(128)S(1)}, s32[16]{0:T(128)}, u32[]{:S(2)}) copy-start(s32[16]{0:T(128)} %param.16) | copy-start | bytes 196
  7.2 161.5 %copy-start.2 = (f32[16]{0:T(128)S(1)}, f32[16]{0:T(128)}, u32[]{:S(2)}) copy-start(f32[16]{0:T(128)} %param.17) | copy-start | bytes 196
  7.2 162.3 %all-gather.2.cloned.1.call-start = ((), (), s32[]{:S(2)}) async-start(), calls=%async_computation | async-start | bytes 8519680 | tf_op jit(solution)/shard_map/all_gather | solution.py:83
  63.6 106.0 %copy-start.3 = (f32[128]{0:T(128)}, f32[128]{0:T(128)S(1)}, u32[]{:S(2)}) copy-start(f32[128]{0:T(128)S(1)} %subtract_select_fusion) | copy-start | bytes 1540
  257.7 7.7 %collective-permute-start = (bf16[128,2,1,128]{3,0,2,1:T(8,128)(2,1)S(1)}, bf16[128,2,1,128]{3,0,2,1:T(8,128)(2,1)S(1)}, u32[]{:S(2)}, u32[]{:S(2)}) collective-permute-start(bf16[128,2,1,128]{3,0,2,1:T(8,128)(2,1)S(1)} %get-tuple-element.684), channel_id=1, source_target_pairs={{0,8},{8,16},{16,24},{24,32},{32,40},{40,48},{48,56},{56,64},{64,7... | collective-permute-start | bytes 196616 | tf_op jit(solution)/shard_map/while/body/eval_jaxpr/ppermute | solution.py:14
  266.0 7.7 %collective-permute-start = (bf16[128,2,1,128]{3,0,2,1:T(8,128)(2,1)S(1)}, bf16[128,2,1,128]{3,0,2,1:T(8,128)(2,1)S(1)}, u32[]{:S(2)}, u32[]{:S(2)}) collective-permute-start(bf16[128,2,1,128]{3,0,2,1:T(8,128)(2,1)S(1)} %get-tuple-element.684), channel_id=1, source_target_pairs={{0,8},{8,16},{16,24},{24,32},{32,40},{40,48},{48,56},{56,64},{64,7... | collective-permute-start | bytes 196616 | tf_op jit(solution)/shard_map/while/body/eval_jaxpr/ppermute | solution.py:14
  274.3 7.7 %collective-permute-start = (bf16[128,2,1,128]{3,0,2,1:T(8,128)(2,1)S(1)}, bf16[128,2,1,128]{3,0,2,1:T(8,128)(2,1)S(1)}, u32[]{:S(2)}, u32[]{:S(2)}) collective-permute-start(bf16[128,2,1,128]{3,0,2,1:T(8,128)(2,1)S(1)} %get-tuple-element.684), channel_id=1, source_target_pairs={{0,8},{8,16},{16,24},{24,32},{32,40},{40,48},{48,56},{56,64},{64,7... | collective-permute-start | bytes 196616 | tf_op jit(solution)/shard_map/while/body/eval_jaxpr/ppermute | solution.py:14
  282.7 7.7 %collective-permute-start = (bf16[128,2,1,128]{3,0,2,1:T(8,128)(2,1)S(1)}, bf16[128,2,1,128]{3,0,2,1:T(8,128)(2,1)S(1)}, u32[]{:S(2)}, u32[]{:S(2)}) collective-permute-start(bf16[128,2,1,128]{3,0,2,1:T(8,128)(2,1)S(1)} %get-tuple-element.684), channel_id=1, source_target_pairs={{0,8},{8,16},{16,24},{24,32},{32,40},{40,48},{48,56},{56,64},{64,7... | collective-permute-start | bytes 196616 | tf_op jit(solution)/shard_map/while/body/eval_jaxpr/ppermute | solution.py:14
  291.0 7.7 %collective-permute-start = (bf16[128,2,1,128]{3,0,2,1:T(8,128)(2,1)S(1)}, bf16[128,2,1,128]{3,0,2,1:T(8,128)(2,1)S(1)}, u32[]{:S(2)}, u32[]{:S(2)}) collective-permute-start(bf16[128,2,1,128]{3,0,2,1:T(8,128)(2,1)S(1)} %get-tuple-element.684), channel_id=1, source_target_pairs={{0,8},{8,16},{16,24},{24,32},{32,40},{40,48},{48,56},{56,64},{64,7... | collective-permute-start | bytes 196616 | tf_op jit(solution)/shard_map/while/body/eval_jaxpr/ppermute | solution.py:14
  299.3 7.7 %collective-permute-start = (bf16[128,2,1,128]{3,0,2,1:T(8,128)(2,1)S(1)}, bf16[128,2,1,128]{3,0,2,1:T(8,128)(2,1)S(1)}, u32[]{:S(2)}, u32[]{:S(2)}) collective-permute-start(bf16[128,2,1,128]{3,0,2,1:T(8,128)(2,1)S(1)} %get-tuple-element.684), channel_id=1, source_target_pairs={{0,8},{8,16},{16,24},{24,32},{32,40},{40,48},{48,56},{56,64},{64,7... | collective-permute-start | bytes 196616 | tf_op jit(solution)/shard_map/while/body/eval_jaxpr/ppermute | solution.py:14
  307.6 7.7 %collective-permute-start = (bf16[128,2,1,128]{3,0,2,1:T(8,128)(2,1)S(1)}, bf16[128,2,1,128]{3,0,2,1:T(8,128)(2,1)S(1)}, u32[]{:S(2)}, u32[]{:S(2)}) collective-permute-start(bf16[128,2,1,128]{3,0,2,1:T(8,128)(2,1)S(1)} %get-tuple-element.684), channel_id=1, source_target_pairs={{0,8},{8,16},{16,24},{24,32},{32,40},{40,48},{48,56},{56,64},{64,7... | collective-permute-start | bytes 196616 | tf_op jit(solution)/shard_map/while/body/eval_jaxpr/ppermute | solution.py:14
  316.0 7.7 %collective-permute-start = (bf16[128,2,1,128]{3,0,2,1:T(8,128)(2,1)S(1)}, bf16[128,2,1,128]{3,0,2,1:T(8,128)(2,1)S(1)}, u32[]{:S(2)}, u32[]{:S(2)}) collective-permute-start(bf16[128,2,1,128]{3,0,2,1:T(8,128)(2,1)S(1)} %get-tuple-element.684), channel_id=1, source_target_pairs={{0,8},{8,16},{16,24},{24,32},{32,40},{40,48},{48,56},{56,64},{64,7... | collective-permute-start | bytes 196616 | tf_op jit(solution)/shard_map/while/body/eval_jaxpr/ppermute | solution.py:14
  324.3 7.7 %collective-permute-start = (bf16[128,2,1,128]{3,0,2,1:T(8,128)(2,1)S(1)}, bf16[128,2,1,128]{3,0,2,1:T(8,128)(2,1)S(1)}, u32[]{:S(2)}, u32[]{:S(2)}) collective-permute-start(bf16[128,2,1,128]{3,0,2,1:T(8,128)(2,1)S(1)} %get-tuple-element.684), channel_id=1, source_target_pairs={{0,8},{8,16},{16,24},{24,32},{32,40},{40,48},{48,56},{56,64},{64,7... | collective-permute-start | bytes 196616 | tf_op jit(solution)/shard_map/while/body/eval_jaxpr/ppermute | solution.py:14
  332.6 7.7 %collective-permute-start = (bf16[128,2,1,128]{3,0,2,1:T(8,128)(2,1)S(1)}, bf16[128,2,1,128]{3,0,2,1:T(8,128)(2,1)S(1)}, u32[]{:S(2)}, u32[]{:S(2)}) collective-permute-start(bf16[128,2,1,128]{3,0,2,1:T(8,128)(2,1)S(1)} %get-tuple-element.684), channel_id=1, source_target_pairs={{0,8},{8,16},{16,24},{24,32},{32,40},{40,48},{48,56},{56,64},{64,7... | collective-permute-start | bytes 196616 | tf_op jit(solution)/shard_map/while/body/eval_jaxpr/ppermute | solution.py:14
  341.0 7.7 %collective-permute-start = (bf16[128,2,1,128]{3,0,2,1:T(8,128)(2,1)S(1)}, bf16[128,2,1,128]{3,0,2,1:T(8,128)(2,1)S(1)}, u32[]{:S(2)}, u32[]{:S(2)}) collective-permute-start(bf16[128,2,1,128]{3,0,2,1:T(8,128)(2,1)S(1)} %get-tuple-element.684), channel_id=1, source_target_pairs={{0,8},{8,16},{16,24},{24,32},{32,40},{40,48},{48,56},{56,64},{64,7... | collective-permute-start | bytes 196616 | tf_op jit(solution)/shard_map/while/body/eval_jaxpr/ppermute | solution.py:14
  349.3 7.7 %collective-permute-start = (bf16[128,2,1,128]{3,0,2,1:T(8,128)(2,1)S(1)}, bf16[128,2,1,128]{3,0,2,1:T(8,128)(2,1)S(1)}, u32[]{:S(2)}, u32[]{:S(2)}) collective-permute-start(bf16[128,2,1,128]{3,0,2,1:T(8,128)(2,1)S(1)} %get-tuple-element.684), channel_id=1, source_target_pairs={{0,8},{8,16},{16,24},{24,32},{32,40},{40,48},{48,56},{56,64},{64,7... | collective-permute-start | bytes 196616 | tf_op jit(solution)/shard_map/while/body/eval_jaxpr/ppermute | solution.py:14
  357.6 7.7 %collective-permute-start = (bf16[128,2,1,128]{3,0,2,1:T(8,128)(2,1)S(1)}, bf16[128,2,1,128]{3,0,2,1:T(8,128)(2,1)S(1)}, u32[]{:S(2)}, u32[]{:S(2)}) collective-permute-start(bf16[128,2,1,128]{3,0,2,1:T(8,128)(2,1)S(1)} %get-tuple-element.684), channel_id=1, source_target_pairs={{0,8},{8,16},{16,24},{24,32},{32,40},{40,48},{48,56},{56,64},{64,7... | collective-permute-start | bytes 196616 | tf_op jit(solution)/shard_map/while/body/eval_jaxpr/ppermute | solution.py:14
  365.9 7.7 %collective-permute-start = (bf16[128,2,1,128]{3,0,2,1:T(8,128)(2,1)S(1)}, bf16[128,2,1,128]{3,0,2,1:T(8,128)(2,1)S(1)}, u32[]{:S(2)}, u32[]{:S(2)}) collective-permute-start(bf16[128,2,1,128]{3,0,2,1:T(8,128)(2,1)S(1)} %get-tuple-element.684), channel_id=1, source_target_pairs={{0,8},{8,16},{16,24},{24,32},{32,40},{40,48},{48,56},{56,64},{64,7... | collective-permute-start | bytes 196616 | tf_op jit(solution)/shard_map/while/body/eval_jaxpr/ppermute | solution.py:14
  374.3 7.7 %collective-permute-start = (bf16[128,2,1,128]{3,0,2,1:T(8,128)(2,1)S(1)}, bf16[128,2,1,128]{3,0,2,1:T(8,128)(2,1)S(1)}, u32[]{:S(2)}, u32[]{:S(2)}) collective-permute-start(bf16[128,2,1,128]{3,0,2,1:T(8,128)(2,1)S(1)} %get-tuple-element.684), channel_id=1, source_target_pairs={{0,8},{8,16},{16,24},{24,32},{32,40},{40,48},{48,56},{56,64},{64,7... | collective-permute-start | bytes 196616 | tf_op jit(solution)/shard_map/while/body/eval_jaxpr/ppermute | solution.py:14
  382.6 7.7 %collective-permute-start = (bf16[128,2,1,128]{3,0,2,1:T(8,128)(2,1)S(1)}, bf16[128,2,1,128]{3,0,2,1:T(8,128)(2,1)S(1)}, u32[]{:S(2)}, u32[]{:S(2)}) collective-permute-start(bf16[128,2,1,128]{3,0,2,1:T(8,128)(2,1)S(1)} %get-tuple-element.684), channel_id=1, source_target_pairs={{0,8},{8,16},{16,24},{24,32},{32,40},{40,48},{48,56},{56,64},{64,7... | collective-permute-start | bytes 196616 | tf_op jit(solution)/shard_map/while/body/eval_jaxpr/ppermute | solution.py:14
Sparse Core Ops, SparseCore 0:
  10.8 125.3 all-gather.1
where the time goes:
time: 401 us; the launch traced here: 399 us
  blocking collectives  149 us (37%)
  waiting for transfers between devices  88.3 us (22%)
  matrix products  88 us (22%)
  starting transfers between devices  30.8 us (8%)
  other arithmetic  20.5 us (5%)
  between operations  14.9 us (4%)
  local copies, waits for them, and re-layouts  4.58 us (1%)
    psum x1, blocking collectives, shards(): response_sum = lax.psum(partial_sums, 'ctx')  105 us
    ppermute x16, waiting for transfers between devices, from_behind(): return lax.ppermute(block, axis, route)  88.2 us
    dot_general x49, matrix products, absorb(): jnp.einsum('rkgn,nkd->rkgd', weights.astype(jnp.bfloat16), values_part, p...  45.6 us
    dot_general x49, matrix products, absorb(): jnp.einsum('rkgd,nkd->rkgn', grouped, keys_part, preferred_element_type=j...  42.4 us
    ppermute x16, starting transfers between devices, from_behind(): return lax.ppermute(block, axis, route)  30.7 us
    psum x1, blocking collectives, shards(): lax.psum((local_sum * jnp.exp(local_peak - global_peak), picked), 'tp')  23.7 us
    pmax x1, blocking collectives, shards(): global_peak = lax.pmax(local_peak, 'tp')  20.1 us
  transfers between devices with their start and end apart: 17, of which 16 were waited for; matrix products, arithmetic and copies ran while one was open for 4% of the time, Pallas kernels for 0%

commit v1 on v0

v1 whole, which is shorter than its diff:
```python
import functools
import math

import jax
import jax.numpy as jnp
from jax import lax
from jax.experimental import pallas as pl
from jax.experimental.pallas import tpu as pltpu
from jax.sharding import Mesh, PartitionSpec as P

HD = 128
HEADS = 4
ROWS_DEV = 128
PLANE = 4
TILE = 256
SCALE = 1.0 / math.sqrt(HD)
LOG2E = 1.4426950408889634
CTX = ("z", "yl", "core")
PLANE_AXES = ("yl", "core")
MIB = 1 << 20


def logit_kernel(token_ref, base_ref, logits_ref, out_ref, stat_ref):
    step = pl.program_id(0)
    rows = logits_ref.shape[0]
    width = logits_ref.shape[1]
    here = pl.ds(pl.multiple_of(step * rows, rows), rows)
    wide = logits_ref[...].astype(jnp.float32)
    peak = jnp.max(wide, axis=1, keepdims=True)
    total = jnp.sum(jnp.exp(wide - peak), axis=1, keepdims=True)
    target = token_ref[...] - base_ref[0]
    columns = lax.broadcasted_iota(jnp.int32, (rows, width), 1)
    picked = jnp.sum(jnp.where(columns == target, wide, 0.0), axis=1, keepdims=True)
    lane = lax.broadcasted_iota(jnp.int32, (rows, 128), 1)
    stat_ref[here, :] = jnp.where(
        lane == 0, peak, jnp.where(lane == 1, total, picked)
    )

    @pl.when(step == pl.num_programs(0) - 1)
    def _():
        out_ref[...] = stat_ref[...].T[:8]


def logit_stats(logits, token_ids, vocab_base):
    rows, width = logits.shape
    block = 32
    return pl.pallas_call(
        logit_kernel,
        grid=(rows // block,),
        in_specs=[
            pl.BlockSpec((block, 1), lambda i: (i, 0)),
            pl.BlockSpec(memory_space=pltpu.SMEM),
            pl.BlockSpec((block, width), lambda i: (i, 0)),
        ],
        out_specs=pl.BlockSpec((8, 128), lambda i: (0, 0)),
        out_shape=jax.ShapeDtypeStruct((8, 128), jnp.float32),
        scratch_shapes=[pltpu.VMEM((rows, 128), jnp.float32)],
        compiler_params=pltpu.CompilerParams(vmem_limit_bytes=32 * MIB),
        cost_estimate=pl.CostEstimate(
            flops=8 * rows * width, bytes_accessed=2 * rows * width, transcendentals=rows * width
        ),
        name="logit_stats",
    )(token_ids.reshape(rows, 1), vocab_base, logits)


def nt(a, b):
    return lax.dot_general(a, b, (((1,), (1,)), ((), ())), preferred_element_type=jnp.float32)


def attend_kernel(lengths_ref, place_ref, q_ref, prompt_ref, own_ref, out_ref, pv_ref, ov_ref):
    prompt_rows = prompt_ref.shape[0]
    own_rows = own_ref.shape[0]
    pv_ref[:, :HD] = prompt_ref[:, HD:]
    pv_ref[:, HD:] = jnp.ones((prompt_rows, HD), jnp.bfloat16)
    ov_ref[:, :HD] = own_ref[:, HD:]
    ov_ref[:, HD:] = jnp.ones((own_rows, HD), jnp.bfloat16)
    first_row = place_ref[0]
    first_key = place_ref[1]
    lane = lax.broadcasted_iota(jnp.int32, (TILE, HD), 1)
    key_block = lax.broadcasted_iota(jnp.int32, (TILE, own_rows), 1)
    keys = first_key + (key_block // ROWS_DEV) * (PLANE * ROWS_DEV) + key_block % ROWS_DEV
    per = TILE // ROWS_DEV

    def row_tile(t, carry):
        rows = first_row + t * TILE + lax.broadcasted_iota(jnp.int32, (TILE, 1), 0)
        start = jnp.zeros((TILE, 1), jnp.int32)
        edge = jnp.int32(0)
        for r in range(lengths_ref.shape[0]):
            edge = edge + lengths_ref[r]
            start = jnp.where(rows >= edge, edge, start)
        start = jnp.where(rows >= edge, rows, start)
        allowed = (keys >= start) & (keys <= rows)
        packed = jnp.zeros((TILE, HD), jnp.float32)
        devs = pl.ds(t * per, per)
        for h in range(HEADS):
            lanes = slice(h * HD, (h + 1) * HD)
            q = q_ref[devs, :, lanes].reshape(TILE, HD)
            s1 = nt(q, prompt_ref[:, :HD])
            s2 = jnp.where(allowed, nt(q, own_ref[:, :HD]), -1e30)
            m = jnp.maximum(
                jnp.max(s1, axis=1, keepdims=True), jnp.max(s2, axis=1, keepdims=True)
            )
            p1 = jnp.exp2((s1 - m) * (SCALE * LOG2E)).astype(jnp.bfloat16)
            p2 = jnp.exp2((s2 - m) * (SCALE * LOG2E)).astype(jnp.bfloat16)
            acc = jnp.dot(p1, pv_ref[...], preferred_element_type=jnp.float32)
            acc = acc + jnp.dot(p2, ov_ref[...], preferred_element_type=jnp.float32)
            denominator = acc[:, HD:]
            out_ref[devs, :, lanes] = (
                (acc[:, :HD] / denominator).astype(jnp.bfloat16).reshape(per, ROWS_DEV, HD)
            )
            lse = m * SCALE + jnp.log(denominator)
            high = lse.astype(jnp.bfloat16).astype(jnp.float32)
            middle = (lse - high).astype(jnp.bfloat16).astype(jnp.float32)
            low = lse - high - middle
            packed = jnp.where(lane == 3 * h, high, packed)
            packed = jnp.where(lane == 3 * h + 1, middle, packed)
            packed = jnp.where(lane == 3 * h + 2, low, packed)
        out_ref[devs, :, HEADS * HD :] = packed.astype(jnp.bfloat16).reshape(per, ROWS_DEV, HD)
        return carry

    lax.fori_loop(0, PLANE * ROWS_DEV // TILE, row_tile, 0)


def attend(lengths, place, q, prompt, own):
    vmem = pl.BlockSpec(memory_space=pltpu.VMEM)
    smem = pl.BlockSpec(memory_space=pltpu.SMEM)
    keys = prompt.shape[0] + own.shape[0]
    pairs = PLANE * ROWS_DEV * HEADS * keys
    return pl.pallas_call(
        attend_kernel,
        in_specs=[smem, smem, vmem, vmem, vmem],
        out_specs=vmem,
        out_shape=jax.ShapeDtypeStruct((PLANE, ROWS_DEV, HEADS * HD + HD), jnp.bfloat16),
        scratch_shapes=[
            pltpu.VMEM((prompt.shape[0], 2 * HD), jnp.bfloat16),
            pltpu.VMEM((own.shape[0], 2 * HD), jnp.bfloat16),
        ],
        compiler_params=pltpu.CompilerParams(vmem_limit_bytes=48 * MIB),
        cost_estimate=pl.CostEstimate(
            flops=4 * HD * pairs, bytes_accessed=512 * keys + 2 * MIB, transcendentals=pairs
        ),
        name="attend",
    )(lengths, place, q, prompt, own)


def combine_kernel(parts_ref, out_ref):
    for h in range(HEADS):
        lanes = slice(h * HD, (h + 1) * HD)
        lse = []
        for j in range(PLANE):
            base = HEADS * HD + 3 * h
            bits = parts_ref[j, :, HEADS * HD :].astype(jnp.float32)
            lse.append(
                bits[:, 3 * h : 3 * h + 1] + bits[:, 3 * h + 1 : 3 * h + 2] + bits[:, 3 * h + 2 : 3 * h + 3]
            )
        top = jnp.maximum(jnp.maximum(lse[0], lse[1]), jnp.maximum(lse[2], lse[3]))
        weights = [jnp.exp(x - top) for x in lse]
        share = 1.0 / (weights[0] + weights[1] + weights[2] + weights[3])
        total = sum(
            (weights[j] * share) * parts_ref[j, :, lanes].astype(jnp.float32) for j in range(PLANE)
        )
        out_ref[:, lanes] = total.astype(jnp.bfloat16)


def combine(parts):
    vmem = pl.BlockSpec(memory_space=pltpu.VMEM)
    return pl.pallas_call(
        combine_kernel,
        in_specs=[vmem],
        out_specs=vmem,
        out_shape=jax.ShapeDtypeStruct((ROWS_DEV, HEADS * HD), jnp.bfloat16),
        name="combine",
    )(parts)


def to_all(x, axes, count):
    return lax.all_to_all(jnp.broadcast_to(x[None], (count,) + x.shape), axes, 0, 0)


def shards(queries, prompt_kv, response_kv, logits, token_ids, lengths, rewards):
    z = lax.axis_index("z")
    spot = lax.axis_index(PLANE_AXES)
    depth = lax.axis_size("z")
    responses = lengths.shape[0]
    prompt_dev = prompt_kv.shape[0]

    kv_here = jnp.concatenate(
        [prompt_kv.reshape(prompt_dev, 2 * HD), response_kv.reshape(ROWS_DEV, 2 * HD)], axis=0
    )
    gathered = lax.all_gather(kv_here, "z", axis=0)
    q = lax.all_gather(queries.reshape(ROWS_DEV, HEADS * HD), PLANE_AXES, axis=0)

    vocab_base = (lax.axis_index("tp") * logits.shape[1]).astype(jnp.int32).reshape(1)
    stats = to_all(logit_stats(logits, token_ids, vocab_base), "tp", lax.axis_size("tp"))
    peaks, sums, picks = stats[:, 0], stats[:, 1], stats[:, 2]
    peak = jnp.max(peaks, axis=0)
    spread = jnp.sum(sums * jnp.exp(peaks - peak), axis=0)
    logprob = jnp.sum(picks, axis=0) - peak - jnp.log(spread)
    ends_at = jnp.cumsum(lengths)
    rows = (z * PLANE + spot) * ROWS_DEV + jnp.arange(ROWS_DEV, dtype=jnp.int32)
    segment = jnp.sum((rows[:, None] >= ends_at[None, :]).astype(jnp.int32), axis=1)
    token_logprob = jnp.where(segment < responses, logprob, 0.0)
    members = segment[:, None] == jnp.arange(128, dtype=jnp.int32)[None, :]
    part = jnp.sum(jnp.where(members, token_logprob[:, None], 0.0), axis=0)
    parts = to_all(part[None], CTX, depth * PLANE)
    response_sum = jnp.sum(parts[:, 0], axis=0)[:responses]
    length_float = lengths.astype(jnp.float32)
    adjusted = rewards - 0.5 * length_float / 2048
    advantage = adjusted - jnp.mean(adjusted)
    response_objective = -advantage * response_sum / length_float

    prompt = gathered[:, :prompt_dev].reshape(depth * prompt_dev, 2 * HD)
    reach = 5
    low = jnp.maximum(z - (reach - 1), 0)
    own = lax.dynamic_slice_in_dim(gathered[:, prompt_dev:], low, reach, 0)
    own = own.reshape(reach * ROWS_DEV, 2 * HD)
    place = jnp.stack(
        [z * PLANE * ROWS_DEV, (low * PLANE + spot) * ROWS_DEV]
    ).astype(jnp.int32)
    partial = attend(lengths, place, q, prompt, own)
    exchanged = lax.all_to_all(partial, PLANE_AXES, 0, 0)
    context = combine(exchanged).reshape(ROWS_DEV, HEADS, HD)
    return (context, token_logprob, response_objective)


def solution(mesh):
    fine = Mesh(mesh.devices.reshape(16, 2, 2, 8), ("z", "yl", "core", "tp"))
    return jax.shard_map(
        shards,
        mesh=fine,
        in_specs=(
            P(CTX, "tp", None),
            P(CTX, None, "tp", None),
            P(CTX, None, "tp", None),
            P(CTX, "tp"),
            P(CTX),
            P(),
            P(),
        ),
        out_specs=(P(CTX, "tp", None), P(CTX), P()),
        check_vma=False,
    )
```

time: 401 us -> 140 us (0.35)
  the two profiles are of different devices: /device:TPU:258 before, /device:TPU:1 now
where the time goes in v1:
time: 140 us
  waiting for transfers between devices  43.6 us (31%)
  starting transfers between devices  35.3 us (25%)
  Pallas kernels  23.4 us (17%)
  between operations  14.8 us (11%)
  local copies, waits for them, and re-layouts  11.3 us (8%)
  blocking collectives  9.09 us (6%)
  other arithmetic  2.35 us (2%)
    all_gather x1, waiting for transfers between devices, shards(): gathered = lax.all_gather(kv_here, 'z', axis=0)  36 us
    all_to_all x2, starting transfers between devices, to_all(): lax.all_to_all(jnp.broadcast_to(x[None], (count,) + x.shape), axes, 0, 0)  22.4 us
    pallas_call x1, Pallas kernels, attend(): pl.pallas_call(attend_kernel, in_specs=[smem, smem, vmem, vmem, vmem], ou...  18.3 us
    all_to_all x1, starting transfers between devices, shards(): exchanged = lax.all_to_all(partial, PLANE_AXES, 0, 0)  12.9 us
    all_gather x1, blocking collectives, shards(): lax.all_gather(queries.reshape(ROWS_DEV, HEADS * HD), PLANE_AXES, axis=0)  9.09 us
    all_to_all x1, waiting for transfers between devices, shards(): exchanged = lax.all_to_all(partial, PLANE_AXES, 0, 0)  7.58 us
    unnamed x14, local copies, waits for them, and re-layouts  4.35 us
  transfers between devices with their start and end apart: 4, of which 2 were waited for; matrix products, arithmetic and copies ran while one was open for 5% of the time, Pallas kernels for 15%

profile of v1, /device:TPU:1, one launch (start us, length us, event | category | flops | bytes accessed | tf_op | source)
XLA Modules:
  0.0 139.9 jit_solution(17265251540514065509)
XLA Ops:
  7.2 0.0 copy-start.1
  7.2 0.0 copy-start.3
  7.2 0.0 all-gather.3.cloned.1.call-start
  7.2 1.0 copy.31
  8.2 0.9 copy.32
  9.0 0.7 pad_maximum_fusion
  9.7 0.0 all-gather.3.cloned.1.call-update
  9.8 0.8 copy.22.token_ref
  10.5 0.0 copy-start
  10.5 1.7 %copy-done = bf16[128,9600]{1,0:T(8,128)(2,1)S(1)} copy-done((bf16[128,9600]{1,0:T(8,128)(2,1)S(1)}, bf16[128,9600]{1,0:T(8,128)(2,1)}, u32[]{:S(2)}) %copy-start) | copy-done | bytes 2457624
  12.2 2.3 %logit_stats.1 = f32[8,128]{1,0:T(8,128)S(1)} custom-call(s32[128,1]{1,0:T(8,128)S(1)} %copy.22.token_ref, s32[1]{0:T(128)} %bitcast.7.base_ref, bf16[128,9600]{1,0:T(8,128)(2,1)S(1)} %copy-done), custom_call_target="tpu_custom_call" | custom-call | flops 9830400 | bytes 2457600 | tf_op jit(solution)/shard_map/logit_stats/pallas_call | solution.py:47
  14.6 0.6 broadcast_in_dim.20
  15.2 7.5 %all-to-all-start.1 = ((f32[8,8,128]{2,1,0:T(8,128)}), f32[8,8,128]{2,1,0:T(8,128)S(1)}, u32[]{:S(2)}, u32[]{:S(2)}) async-start(f32[8,8,128]{2,1,0:T(8,128)} %broadcast_in_dim.20), calls=%async_computation.1 | async-start | bytes 65536 | tf_op jit(solution)/shard_map/all_to_all | solution.py:177
  22.7 0.0 copy-done.1
  22.7 0.1 copy.21
  22.8 0.1 reduce.3
  22.9 0.0 copy-done.3
  22.9 0.1 all_gather_reshape.3
  23.0 0.1 convert_reduce_fusion
  23.1 9.1 %all_gather.9.q_ref = bf16[4,128,512]{2,1,0:T(8,128)(2,1)S(1)} all-gather(bf16[1,128,512]{2,1,0:T(8,128)(2,1)S(1)} %all_gather_reshape.3), channel_id=1, replica_groups=mesh['z'=16,'yl'=2,'core'=2,'tp'=8] {'yl','core'}, dimensions={0}, use_global_device_ids=true | all-gather | bytes 655360 | tf_op jit(solution)/shard_map/all_gather | solution.py:191
  32.2 0.1 pad_add_fusion.place_ref
  32.3 0.0 all-to-all-done.1
  32.4 0.0 copy-start.5
  32.4 0.1 select_reduce_fusion
  32.5 0.6 broadcast_in_dim.37
  33.1 14.9 %all-to-all-start.2 = ((f32[64,1,128]{2,1,0:T(1,128)}), f32[64,1,128]{2,1,0:T(1,128)S(1)}, u32[]{:S(2)}, u32[]{:S(2)}) async-start(f32[64,1,128]{2,1,0:T(1,128)} %broadcast_in_dim.37), calls=%async_computation.2 | async-start | bytes 65536 | tf_op jit(solution)/shard_map/all_to_all | solution.py:177
  48.0 36.0 %all-gather.3.cloned.1.call-done = bf16[6144,256]{1,0:T(8,128)(2,1)} async-done(((bf16[384,256]{1,0:T(8,128)(2,1)}), bf16[6144,256]{1,0:T(8,128)(2,1)}) %all-gather.3.cloned.1.call-update) | async-done | bytes 3145744 | tf_op jit(solution)/shard_map/all_gather | solution.py:190
  84.1 1.3 slice.25
  85.4 1.8 %slice.24 = bf16[16,256,256]{2,1,0:T(8,128)(2,1)S(1)} slice(bf16[16,384,256]{2,1,0:T(8,128)(2,1)} %bitcast.30), slice={[0:16], [0:256], [0:256]} | slice | bytes 4194304 | tf_op jit(solution)/shard_map/slice | solution.py:212
  87.2 0.0 copy-done.5
  87.2 0.0 copy-start.4
  87.2 18.3 %attend.1 = bf16[4,128,640]{2,1,0:T(8,128)(2,1)} custom-call(s32[16]{0:T(128)S(1)} %copy-done.1, s32[2]{0:T(128)S(1)} %pad_add_fusion.place_ref, bf16[4,128,512]{2,1,0:T(8,128)(2,1)S(1)} %all_gather.9.q_ref, bf16[4096,256]{1,0:T(8,128)(2,1)S(1)} %bitcast.26, bf16[640,256]{1,0:T(8,128)(2,1)S(1)} %bitcast.27), custom_call_target="tpu_custom_call" | custom-call | flops 4966055936 | bytes 4521984 | tf_op jit(solution)/shard_map/attend/pallas_call | solution.py:129
  105.5 0.0 all-to-all-done.2
  105.5 12.9 %all-to-all-start = ((bf16[4,128,640]{2,1,0:T(8,128)(2,1)}), bf16[4,128,640]{2,1,0:T(8,128)(2,1)S(1)}, u32[]{:S(2)}, u32[]{:S(2)}) async-start(bf16[4,128,640]{2,1,0:T(8,128)(2,1)} %attend.1), calls=%async_computation | async-start | bytes 1310720 | tf_op jit(solution)/shard_map/all_to_all | solution.py:221
  118.5 0.0 copy-done.4
  118.5 0.6 fusion
  119.7 0.5 multiply_divide_fusion
  120.3 7.6 %all-to-all-done.parts_ref = bf16[4,128,640]{2,1,0:T(8,128)(2,1)S(1)} async-done(((bf16[4,128,640]{2,1,0:T(8,128)(2,1)}), bf16[4,128,640]{2,1,0:T(8,128)(2,1)S(1)}, u32[]{:S(2)}, u32[]{:S(2)}) %all-to-all-start) | async-done | bytes 655392 | tf_op jit(solution)/shard_map/all_to_all | solution.py:221
  127.8 0.0 copy-start.2
  127.8 0.8 copy-done.2
  128.7 2.8 %combine.1 = bf16[128,512]{1,0:T(8,128)(2,1)} custom-call(bf16[4,128,640]{2,1,0:T(8,128)(2,1)} %copy-done.2), custom_call_target="tpu_custom_call" | custom-call | tf_op jit(solution)/shard_map/combine/pallas_call | solution.py:167
  131.4 1.6 %reshape.78 = bf16[128,4,128]{2,1,0:T(4,128)(2,1)} reshape(bf16[128,512]{1,0:T(8,128)(2,1)} %combine.1) | data formatting | bytes 262144 | tf_op jit(solution)/shard_map/reshape | solution.py:222
  (9 shorter events, 0.2 us)
Async XLA Ops:
  7.2 15.5 %copy-start.1 = (s32[16]{0:T(128)S(1)}, s32[16]{0:T(128)}, u32[]{:S(2)}) copy-start(s32[16]{0:T(128)} %lengths_ref.1) | copy-start | bytes 196
  7.2 15.8 %copy-start.3 = (bf16[128,4,128]{2,1,0:T(4,128)(2,1)S(1)}, bf16[128,4,128]{2,1,0:T(4,128)(2,1)}, u32[]{:S(2)}) copy-start(bf16[128,4,128]{2,1,0:T(4,128)(2,1)} %param.7) | copy-start | bytes 393220
  7.2 76.9 %all-gather.3.cloned.1.call-start = ((), (), s32[]{:S(2)}) async-start(), calls=%async_computation.3 | async-start | bytes 3342336 | tf_op jit(solution)/shard_map/all_gather | solution.py:190
  10.5 1.7 %copy-start = (bf16[128,9600]{1,0:T(8,128)(2,1)S(1)}, bf16[128,9600]{1,0:T(8,128)(2,1)}, u32[]{:S(2)}) copy-start(bf16[128,9600]{1,0:T(8,128)(2,1)} %logits_ref.1) | copy-start | bytes 7372804
  15.2 17.1 %all-to-all-start.1 = ((f32[8,8,128]{2,1,0:T(8,128)}), f32[8,8,128]{2,1,0:T(8,128)S(1)}, u32[]{:S(2)}, u32[]{:S(2)}) async-start(f32[8,8,128]{2,1,0:T(8,128)} %broadcast_in_dim.20), calls=%async_computation.1 | async-start | bytes 65536 | tf_op jit(solution)/shard_map/all_to_all | solution.py:177
  32.4 54.8 %copy-start.5 = (f32[128]{0:T(128)}, f32[128]{0:T(128)S(1)}, u32[]{:S(2)}) copy-start(f32[128]{0:T(128)S(1)} %compare_select_fusion) | copy-start | bytes 1540
  33.1 72.4 %all-to-all-start.2 = ((f32[64,1,128]{2,1,0:T(1,128)}), f32[64,1,128]{2,1,0:T(1,128)S(1)}, u32[]{:S(2)}, u32[]{:S(2)}) async-start(f32[64,1,128]{2,1,0:T(1,128)} %broadcast_in_dim.37), calls=%async_computation.2 | async-start | bytes 65536 | tf_op jit(solution)/shard_map/all_to_all | solution.py:177
  87.2 31.3 %copy-start.4 = (f32[16]{0:T(128)S(1)}, f32[16]{0:T(128)}, u32[]{:S(2)}) copy-start(f32[16]{0:T(128)} %param.13) | copy-start | bytes 196
  105.5 22.3 %all-to-all-start = ((bf16[4,128,640]{2,1,0:T(8,128)(2,1)}), bf16[4,128,640]{2,1,0:T(8,128)(2,1)S(1)}, u32[]{:S(2)}, u32[]{:S(2)}) async-start(bf16[4,128,640]{2,1,0:T(8,128)(2,1)} %attend.1), calls=%async_computation | async-start | bytes 1310720 | tf_op jit(solution)/shard_map/all_to_all | solution.py:221
  127.8 0.8 copy-start.2
Sparse Core Ops, SparseCore 0:
  10.1 73.9 all-gather.2

commit v2 on v1

v2 whole, which is shorter than its diff:
```python
import functools
import math

import jax
import jax.numpy as jnp
from jax import lax
from jax.experimental import pallas as pl
from jax.experimental.pallas import tpu as pltpu
from jax.sharding import Mesh, PartitionSpec as P

HD = 128
HEADS = 4
ROWS_DEV = 128
PLANE = 4
TILE = 256
SCALE = 1.0 / math.sqrt(HD)
LOG2E = 1.4426950408889634
Z = ("zh", "zl")
CTX = Z + ("yl", "core")
PLANE_AXES = ("yl", "core")
MIB = 1 << 20


def logit_kernel(token_ref, base_ref, logits_ref, out_ref, stat_ref):
    step = pl.program_id(0)
    rows = logits_ref.shape[0]
    width = logits_ref.shape[1]
    here = pl.ds(pl.multiple_of(step * rows, rows), rows)
    wide = logits_ref[...].astype(jnp.float32)
    peak = jnp.max(wide, axis=1, keepdims=True)
    total = jnp.sum(jnp.exp(wide - peak), axis=1, keepdims=True)
    target = token_ref[...] - base_ref[0]
    columns = lax.broadcasted_iota(jnp.int32, (rows, width), 1)
    picked = jnp.sum(jnp.where(columns == target, wide, 0.0), axis=1, keepdims=True)
    lane = lax.broadcasted_iota(jnp.int32, (rows, 128), 1)
    stat_ref[here, :] = jnp.where(
        lane == 0, peak, jnp.where(lane == 1, total, picked)
    )

    @pl.when(step == pl.num_programs(0) - 1)
    def _():
        out_ref[...] = stat_ref[...].T[:8]


def logit_stats(logits, token_ids, vocab_base):
    rows, width = logits.shape
    block = 32
    return pl.pallas_call(
        logit_kernel,
        grid=(rows // block,),
        in_specs=[
            pl.BlockSpec((block, 1), lambda i: (i, 0)),
            pl.BlockSpec(memory_space=pltpu.SMEM),
            pl.BlockSpec((block, width), lambda i: (i, 0)),
        ],
        out_specs=pl.BlockSpec((8, 128), lambda i: (0, 0)),
        out_shape=jax.ShapeDtypeStruct((8, 128), jnp.float32),
        scratch_shapes=[pltpu.VMEM((rows, 128), jnp.float32)],
        compiler_params=pltpu.CompilerParams(vmem_limit_bytes=32 * MIB),
        cost_estimate=pl.CostEstimate(
            flops=8 * rows * width, bytes_accessed=2 * rows * width, transcendentals=rows * width
        ),
        name="logit_stats",
    )(token_ids.reshape(rows, 1), vocab_base, logits)


def nt(a, b):
    return lax.dot_general(a, b, (((1,), (1,)), ((), ())), preferred_element_type=jnp.float32)


def attend_kernel(pieces, first, last, *refs):
    lengths_ref, place_ref, q_ref = refs[:3]
    count = len(pieces)
    kv_refs = refs[3 : 3 + count]
    refs = refs[3 + count :]
    if not first:
        acc_in, stat_in = refs[:2]
        refs = refs[2:]
    if last:
        out_ref = refs[0]
        refs = refs[1:]
    else:
        acc_out, stat_out = refs[:2]
        refs = refs[2:]
    v_refs = refs
    for kv_ref, v_ref in zip(kv_refs, v_refs):
        v_ref[:, :HD] = kv_ref[:, HD:]
        v_ref[:, HD:] = jnp.ones((kv_ref.shape[0], HD), jnp.bfloat16)
    lane = lax.broadcasted_iota(jnp.int32, (TILE, HD), 1)
    per = TILE // ROWS_DEV

    def row_tile(t, carry):
        rows = place_ref[0] + t * TILE + lax.broadcasted_iota(jnp.int32, (TILE, 1), 0)
        start = jnp.zeros((TILE, 1), jnp.int32)
        edge = jnp.int32(0)
        for r in range(lengths_ref.shape[0]):
            edge = edge + lengths_ref[r]
            start = jnp.where(rows >= edge, edge, start)
        start = jnp.where(rows >= edge, rows, start)
        devs = pl.ds(t * per, per)
        packed = jnp.zeros((TILE, HD), jnp.float32)
        if not first:
            stat = stat_in[devs].reshape(TILE, HD)
        for h in range(HEADS):
            lanes = slice(h * HD, (h + 1) * HD)
            q = q_ref[devs, :, lanes].reshape(TILE, HD)
            tops = [] if first else [stat[:, h : h + 1]]
            scores = []
            answer = 0
            for kv_ref, v_ref, spans in zip(kv_refs, v_refs, pieces):
                for low, high, masked in spans:
                    s = nt(q, kv_ref[low:high, :HD])
                    if masked:
                        answer += 1
                        keys = place_ref[answer] + lax.broadcasted_iota(
                            jnp.int32, (TILE, high - low), 1
                        )
                        s = jnp.where((keys >= start) & (keys <= rows), s, -1e30)
                    tops.append(jnp.max(s, axis=1, keepdims=True))
                    scores.append((s, v_ref, low, high))
            m = tops[0]
            for top in tops[1:]:
                m = jnp.maximum(m, top)
            acc = 0.0
            for s, v_ref, low, high in scores:
                p = jnp.exp2((s - m) * (SCALE * LOG2E)).astype(jnp.bfloat16)
                acc = acc + jnp.dot(p, v_ref[low:high, :], preferred_element_type=jnp.float32)
            weighted, denominator = acc[:, :HD], acc[:, HD:]
            if not first:
                shrink = jnp.exp2((tops[0] - m) * (SCALE * LOG2E))
                weighted = weighted + shrink * acc_in[devs, :, lanes].reshape(TILE, HD)
                denominator = denominator + shrink * stat[:, HEADS + h : HEADS + h + 1]
            if last:
                out_ref[devs, :, lanes] = (
                    (weighted / denominator).astype(jnp.bfloat16).reshape(per, ROWS_DEV, HD)
                )
                lse = m * SCALE + jnp.log(denominator)
                high_part = lse.astype(jnp.bfloat16).astype(jnp.float32)
                middle = (lse - high_part).astype(jnp.bfloat16).astype(jnp.float32)
                low_part = lse - high_part - middle
                packed = jnp.where(lane == 3 * h, high_part, packed)
                packed = jnp.where(lane == 3 * h + 1, middle, packed)
                packed = jnp.where(lane == 3 * h + 2, low_part, packed)
            else:
                acc_out[devs, :, lanes] = weighted.reshape(per, ROWS_DEV, HD)
                packed = jnp.where(lane == h, m, packed)
                packed = jnp.where(lane == HEADS + h, denominator, packed)
        if last:
            out_ref[devs, :, HEADS * HD :] = packed.astype(jnp.bfloat16).reshape(
                per, ROWS_DEV, HD
            )
        else:
            stat_out[devs] = packed.reshape(per, ROWS_DEV, HD)
        return carry

    lax.fori_loop(0, PLANE * ROWS_DEV // TILE, row_tile, 0)


def attend(lengths, place, q, blocks, pieces, state, last):
    vmem = pl.BlockSpec(memory_space=pltpu.VMEM)
    smem = pl.BlockSpec(memory_space=pltpu.SMEM)
    keys = sum(high - low for spans in pieces for low, high, masked in spans)
    pairs = PLANE * ROWS_DEV * HEADS * keys
    if last:
        out_shape = jax.ShapeDtypeStruct((PLANE, ROWS_DEV, HEADS * HD + HD), jnp.bfloat16)
        out_specs = vmem
    else:
        out_shape = (
            jax.ShapeDtypeStruct((PLANE, ROWS_DEV, HEADS * HD), jnp.float32),
            jax.ShapeDtypeStruct((PLANE, ROWS_DEV, HD), jnp.float32),
        )
        out_specs = (vmem, vmem)
    return pl.pallas_call(
        functools.partial(attend_kernel, pieces, not state, last),
        in_specs=[smem, smem] + [vmem] * (1 + len(blocks) + len(state)),
        out_specs=out_specs,
        out_shape=out_shape,
        scratch_shapes=[pltpu.VMEM((block.shape[0], 2 * HD), jnp.bfloat16) for block in blocks],
        compiler_params=pltpu.CompilerParams(vmem_limit_bytes=40 * MIB),
        cost_estimate=pl.CostEstimate(
            flops=8 * HD * pairs, bytes_accessed=512 * keys + 2 * MIB, transcendentals=pairs
        ),
        name="attend",
    )(lengths, place, q, *blocks, *state)


def combine_kernel(parts_ref, out_ref):
    for h in range(HEADS):
        lanes = slice(h * HD, (h + 1) * HD)
        lse = []
        for j in range(PLANE):
            base = HEADS * HD + 3 * h
            bits = parts_ref[j, :, HEADS * HD :].astype(jnp.float32)
            lse.append(
                bits[:, 3 * h : 3 * h + 1] + bits[:, 3 * h + 1 : 3 * h + 2] + bits[:, 3 * h + 2 : 3 * h + 3]
            )
        top = jnp.maximum(jnp.maximum(lse[0], lse[1]), jnp.maximum(lse[2], lse[3]))
        weights = [jnp.exp(x - top) for x in lse]
        share = 1.0 / (weights[0] + weights[1] + weights[2] + weights[3])
        total = sum(
            (weights[j] * share) * parts_ref[j, :, lanes].astype(jnp.float32) for j in range(PLANE)
        )
        out_ref[:, lanes] = total.astype(jnp.bfloat16)


def combine(parts):
    vmem = pl.BlockSpec(memory_space=pltpu.VMEM)
    return pl.pallas_call(
        combine_kernel,
        in_specs=[vmem],
        out_specs=vmem,
        out_shape=jax.ShapeDtypeStruct((ROWS_DEV, HEADS * HD), jnp.bfloat16),
        name="combine",
    )(parts)


def to_all(x, axes, count):
    return lax.all_to_all(jnp.broadcast_to(x[None], (count,) + x.shape), axes, 0, 0)


def shift(x, distance):
    depth = lax.axis_size("zh") * lax.axis_size("zl")
    return lax.ppermute(x, Z, [(i, (i + distance) % depth) for i in range(depth)])


def shards(queries, prompt_kv, response_kv, logits, token_ids, lengths, rewards):
    z = lax.axis_index(Z)
    spot = lax.axis_index(PLANE_AXES)
    depth = lax.axis_size("zh") * lax.axis_size("zl")
    responses = lengths.shape[0]
    pb = prompt_kv.shape[0]
    rb = response_kv.shape[0]

    own = jnp.concatenate(
        [prompt_kv.reshape(pb, 2 * HD), response_kv.reshape(rb, 2 * HD)], axis=0
    )
    plus4 = shift(own, 4)
    minus4 = shift(own[:pb], -4)
    q = lax.all_gather(queries.reshape(ROWS_DEV, HEADS * HD), PLANE_AXES, axis=0)
    eight_a = shift(minus4[: pb // 2], -4)
    eight_b = shift(plus4[pb // 2 : pb], 4)

    vocab_base = (lax.axis_index("tp") * logits.shape[1]).astype(jnp.int32).reshape(1)
    stats = to_all(logit_stats(logits, token_ids, vocab_base), "tp", lax.axis_size("tp"))
    peaks, sums, picks = stats[:, 0], stats[:, 1], stats[:, 2]
    peak = jnp.max(peaks, axis=0)
    spread = jnp.sum(sums * jnp.exp(peaks - peak), axis=0)
    logprob = jnp.sum(picks, axis=0) - peak - jnp.log(spread)
    ends_at = jnp.cumsum(lengths)
    rows = (z * PLANE + spot) * ROWS_DEV + jnp.arange(ROWS_DEV, dtype=jnp.int32)
    segment = jnp.sum((rows[:, None] >= ends_at[None, :]).astype(jnp.int32), axis=1)
    token_logprob = jnp.where(segment < responses, logprob, 0.0)
    members = segment[:, None] == jnp.arange(128, dtype=jnp.int32)[None, :]
    part = jnp.sum(jnp.where(members, token_logprob[:, None], 0.0), axis=0)
    part = jnp.sum(to_all(part[None], ("zl",) + PLANE_AXES, 8)[:, 0], axis=0)
    part = jnp.sum(to_all(part[None], "zh", 8)[:, 0], axis=0)
    response_sum = part[:responses]
    length_float = lengths.astype(jnp.float32)
    adjusted = rewards - 0.5 * length_float / 2048
    advantage = adjusted - jnp.mean(adjusted)
    response_objective = -advantage * response_sum / length_float

    def place(*planes):
        first_keys = [((p + depth) % depth * PLANE + spot) * rb for p in planes]
        return jnp.stack([z * PLANE * ROWS_DEV] + first_keys).astype(jnp.int32)

    send_right = jnp.concatenate(
        [own[:pb], plus4[:pb], own[pb:], minus4, eight_a, eight_b], axis=0
    )
    send_left = jnp.concatenate(
        [own[:pb], minus4, plus4[pb:], plus4[:pb], eight_a, eight_b], axis=0
    )
    right = shift(send_right, 1)
    left = shift(send_left, -1)
    whole = ((0, 2 * pb, False), (2 * pb, 2 * pb + rb, True), (2 * pb + rb, 4 * pb + rb, False))
    state = attend(
        lengths, place(z, z - 4), q, [send_right, plus4], [whole, ((pb, pb + rb, True),)], (), False
    )
    right2 = shift(right[: 2 * pb + rb], 1)
    left2 = shift(left[: 2 * pb], -1)
    state = attend(
        lengths, place(z - 1, z - 3), q, [right, left], [whole, whole], state, False
    )
    partial = attend(
        lengths, place(z - 2), q, [right2, left2], [whole[:2], whole[:1]], state, True
    )
    exchanged = lax.all_to_all(partial, PLANE_AXES, 0, 0)
    context = combine(exchanged).reshape(ROWS_DEV, HEADS, HD)
    return (context, token_logprob, response_objective)


def solution(mesh):
    fine = Mesh(mesh.devices.reshape(8, 2, 2, 2, 8), ("zh", "zl", "yl", "core", "tp"))
    return jax.shard_map(
        shards,
        mesh=fine,
        in_specs=(
            P(CTX, "tp", None),
            P(CTX, None, "tp", None),
            P(CTX, None, "tp", None),
            P(CTX, "tp"),
            P(CTX),
            P(),
            P(),
        ),
        out_specs=(P(CTX, "tp", None), P(CTX), P()),
        check_vma=False,
    )
```

time: 140 us -> 131 us (0.936)
  starting transfers between devices: 35.3 us -> 63.3 us
  waiting for transfers between devices: 43.6 us -> 22.8 us
  between operations: 14.8 us -> 1.69 us
  local copies, waits for them, and re-layouts: 11.3 us -> 8.92 us
  blocking collectives: 9.09 us -> 7.67 us
    ppermute x0 -> x8, starting transfers between devices: none -> 38.7 us  [shift(): lax.ppermute(x, Z, [(i, (i + distance) % depth) for i in range(depth)])]
    all_gather x1 -> x0, waiting for transfers between devices: 36 us -> none  [shards(): gathered = lax.all_gather(kv_here, 'z', axis=0)]
    all_to_all x1, starting transfers between devices: 12.9 us -> 4.98 us  [shards(): exchanged = lax.all_to_all(partial, PLANE_AXES, 0, 0)]
    all_to_all x2 -> x3, waiting for transfers between devices: 0.01 us -> 7.92 us  [to_all(): lax.all_to_all(jnp.broadcast_to(x[None], (count,) + x.shape), axes, 0, 0)]
    ppermute x0 -> x8, waiting for transfers between devices: none -> 7.27 us  [shift(): lax.ppermute(x, Z, [(i, (i + distance) % depth) for i in range(depth)])]
    slice x2 -> x3, local copies, waits for them, and re-layouts: 3.09 us -> 0.05 us  [the longest x1 0.02 us: shards(): right2 = shift(right[:2 * pb + rb], 1)]
    all_to_all x2 -> x3, starting transfers between devices: 22.4 us -> 19.6 us  [to_all(): lax.all_to_all(jnp.broadcast_to(x[None], (count,) + x.shape), axes, 0, 0)]
    all_gather x1, blocking collectives: 9.09 us -> 7.67 us  [shards(): lax.all_gather(queries.reshape(ROWS_DEV, HEADS * HD), PLANE_AXES, axis=0)]
  transfers between devices with their start and end apart: 4 -> 12, of which waited for: 2 -> 4; matrix products, arithmetic and copies ran while one was open for 5% -> 4% of each run, Pallas kernels for 15% -> 17%
where the time goes in v2:
time: 131 us
  starting transfers between devices  63.3 us (48%)
  Pallas kernels  24.5 us (19%)
  waiting for transfers between devices  22.8 us (17%)
  local copies, waits for them, and re-layouts  8.92 us (7%)
  blocking collectives  7.67 us (6%)
  other arithmetic  1.82 us (1%)
  between operations  1.69 us (1%)
    ppermute x8, starting transfers between devices, shift(): lax.ppermute(x, Z, [(i, (i + distance) % depth) for i in range(depth)])  38.7 us
    all_to_all x3, starting transfers between devices, to_all(): lax.all_to_all(jnp.broadcast_to(x[None], (count,) + x.shape), axes, 0, 0)  19.6 us
    pallas_call x3, Pallas kernels, attend(): pl.pallas_call(functools.partial(attend_kernel, pieces, not state, last),...  19.4 us
    all_to_all x3, waiting for transfers between devices, to_all(): lax.all_to_all(jnp.broadcast_to(x[None], (count,) + x.shape), axes, 0, 0)  7.92 us
    all_gather x1, blocking collectives, shards(): lax.all_gather(queries.reshape(ROWS_DEV, HEADS * HD), PLANE_AXES, axis=0)  7.67 us
    all_to_all x1, waiting for transfers between devices, shards(): exchanged = lax.all_to_all(partial, PLANE_AXES, 0, 0)  7.59 us
    ppermute x8, waiting for transfers between devices, shift(): lax.ppermute(x, Z, [(i, (i + distance) % depth) for i in range(depth)])  7.27 us
    all_to_all x1, starting transfers between devices, shards(): exchanged = lax.all_to_all(partial, PLANE_AXES, 0, 0)  4.98 us
  transfers between devices with their start and end apart: 12, of which 4 were waited for; matrix products, arithmetic and copies ran while one was open for 4% of the time, Pallas kernels for 17%

profile of v2, /device:TPU:1, one launch (start us, length us, event | category | flops | bytes accessed | tf_op | source)
XLA Modules:
  0.0 130.7 jit_solution(13881335098597020472)
XLA Ops:
  0.6 0.0 copy-start.3
  0.6 0.0 copy-start.5
  0.7 0.0 copy-start.1
  0.7 1.0 copy.38
  1.6 13.3 %collective-permute-start.1 = (bf16[256,256]{1,0:T(8,128)(2,1)S(1)}, bf16[256,256]{1,0:T(8,128)(2,1)S(1)}, u32[]{:S(2)}, u32[]{:S(2)}) collective-permute-start(bf16[256,256]{1,0:T(8,128)(2,1)S(1)} %bitcast.35), channel_id=1, source_target_pairs={{0,384},{32,416},{64,448},{96,480},{128,0},{160,32},{192,64},{224,... | collective-permute-start | bytes 393224 | tf_op jit(solution)/shard_map/ppermute | solution.py:223
  14.9 0.9 copy.39
  15.8 1.9 %collective-permute-start = (bf16[384,256]{1,0:T(8,128)(2,1)S(1)}, bf16[384,256]{1,0:T(8,128)(2,1)S(1)}, u32[]{:S(2)}, u32[]{:S(2)}) collective-permute-start(bf16[384,256]{1,0:T(8,128)(2,1)S(1)} %pad_maximum_fusion), channel_id=1, source_target_pairs={{0,128},{32,160},{64,192},{96,224},{128,256},{160,288},{192,320},{... | collective-permute-start | bytes 589832 | tf_op jit(solution)/shard_map/ppermute | solution.py:223
  17.7 0.8 copy.22.token_ref
  18.5 0.0 copy-start
  18.5 1.7 %copy-done = bf16[128,9600]{1,0:T(8,128)(2,1)S(1)} copy-done((bf16[128,9600]{1,0:T(8,128)(2,1)S(1)}, bf16[128,9600]{1,0:T(8,128)(2,1)}, u32[]{:S(2)}) %copy-start) | copy-done | bytes 2457624
  20.2 2.3 %logit_stats.1 = f32[8,128]{1,0:T(8,128)S(1)} custom-call(s32[128,1]{1,0:T(8,128)S(1)} %copy.22.token_ref, s32[1]{0:T(128)} %bitcast.8.base_ref, bf16[128,9600]{1,0:T(8,128)(2,1)S(1)} %copy-done), custom_call_target="tpu_custom_call" | custom-call | flops 9830400 | bytes 2457600 | tf_op jit(solution)/shard_map/logit_stats/pallas_call | solution.py:48
  22.5 0.0 copy-start.4
  22.5 0.6 broadcast_in_dim.22
  23.2 6.7 %all-to-all-start.1 = ((f32[8,8,128]{2,1,0:T(8,128)}), f32[8,8,128]{2,1,0:T(8,128)S(1)}, u32[]{:S(2)}, u32[]{:S(2)}) async-start(f32[8,8,128]{2,1,0:T(8,128)} %broadcast_in_dim.22), calls=%async_computation.1 | async-start | bytes 65536 | tf_op jit(solution)/shard_map/all_to_all | solution.py:218
  29.8 0.0 copy-done.3
  29.9 0.0 copy-done.5
  29.9 0.1 all_gather_reshape.3
  30.0 7.7 %all_gather.3.refs_2_ = bf16[4,128,512]{2,1,0:T(8,128)(2,1)S(1)} all-gather(bf16[1,128,512]{2,1,0:T(8,128)(2,1)S(1)} %all_gather_reshape.3), channel_id=1, replica_groups=mesh['zh'=8,'zl'=2,'yl'=2,'core'=2,'tp'=8] {'yl','core'}, dimensions={0}, use_global_device_ids=true | all-gather | bytes 655360 | tf_op jit(solution)/shard_map/all_gather | solution.py:239
  37.6 0.0 copy-done.1
  37.6 0.1 copy.21
  37.8 0.1 reduce.4
  37.9 0.1 pad_add_fusion.refs_1_
  38.0 0.1 convert_reduce_fusion
  38.0 0.1 pad_add_fusion.2.refs_1_
  38.2 0.0 all-to-all-done.1
  38.3 0.0 collective-permute-done.1
  38.3 7.5 %collective-permute-start.2 = (bf16[128,256]{1,0:T(8,128)(2,1)S(1)}, bf16[128,256]{1,0:T(8,128)(2,1)S(1)}, u32[]{:S(2)}, u32[]{:S(2)}) collective-permute-start(bf16[128,256]{1,0:T(8,128)(2,1)S(1)} %slice.42), channel_id=1, source_target_pairs={{0,384},{32,416},{64,448},{96,480},{128,0},{160,32},{192,64},{224,... | collective-permute-start | bytes 196616 | tf_op jit(solution)/shard_map/ppermute | solution.py:223
  45.9 0.0 collective-permute-done.refs_4_
  45.9 0.0 copy-done.4
  46.0 1.9 %collective-permute-start.3 = (bf16[128,256]{1,0:T(8,128)(2,1)S(1)}, bf16[128,256]{1,0:T(8,128)(2,1)S(1)}, u32[]{:S(2)}, u32[]{:S(2)}) collective-permute-start(bf16[128,256]{1,0:T(8,128)(2,1)S(1)} %get-tuple-element.14), channel_id=1, source_target_pairs={{0,128},{32,160},{64,192},{96,224},{128,256},{160,288},{192,320},{... | collective-permute-start | bytes 196616 | tf_op jit(solution)/shard_map/ppermute | solution.py:223
  47.9 2.6 %collective-permute-done.2 = bf16[128,256]{1,0:T(8,128)(2,1)S(1)} collective-permute-done((bf16[128,256]{1,0:T(8,128)(2,1)S(1)}, bf16[128,256]{1,0:T(8,128)(2,1)S(1)}, u32[]{:S(2)}, u32[]{:S(2)}) %collective-permute-start.2) | collective-permute-done | bytes 65568 | tf_op jit(solution)/shard_map/ppermute | solution.py:223
  50.5 4.7 %collective-permute-done.3 = bf16[128,256]{1,0:T(8,128)(2,1)S(1)} collective-permute-done((bf16[128,256]{1,0:T(8,128)(2,1)S(1)}, bf16[128,256]{1,0:T(8,128)(2,1)S(1)}, u32[]{:S(2)}, u32[]{:S(2)}) %collective-permute-start.3) | collective-permute-done | bytes 65568 | tf_op jit(solution)/shard_map/ppermute | solution.py:223
  55.2 3.5 %collective-permute-start.4 = (bf16[1152,256]{1,0:T(8,128)(2,1)S(1)}, bf16[1152,256]{1,0:T(8,128)(2,1)S(1)}, u32[]{:S(2)}, u32[]{:S(2)}) collective-permute-start(bf16[1152,256]{1,0:T(8,128)(2,1)S(1)} %get-tuple-element.16.refs_3_), channel_id=1, source_target_pairs={{0,32},{32,64},{64,96},{96,128},{128,160},{160,192},{192,224},{224... | collective-permute-start | bytes 1769480 | tf_op jit(solution)/shard_map/ppermute | solution.py:223
  58.7 4.1 %collective-permute-start.6 = (bf16[1152,256]{1,0:T(8,128)(2,1)S(1)}, bf16[1152,256]{1,0:T(8,128)(2,1)S(1)}, u32[]{:S(2)}, u32[]{:S(2)}) collective-permute-start(bf16[1152,256]{1,0:T(8,128)(2,1)S(1)} %get-tuple-element.15), channel_id=1, source_target_pairs={{0,480},{32,0},{64,32},{96,64},{128,96},{160,128},{192,160},{224,1... | collective-permute-start | bytes 1769480 | tf_op jit(solution)/shard_map/ppermute | solution.py:223
  62.8 0.0 copy-start.7
  62.8 0.1 select_reduce_fusion
  62.9 0.6 broadcast_in_dim.42
  63.5 6.8 %all-to-all-start.2 = ((f32[8,1,128]{2,1,0:T(1,128)}), f32[8,1,128]{2,1,0:T(1,128)S(1)}, u32[]{:S(2)}, u32[]{:S(2)}) async-start(f32[8,1,128]{2,1,0:T(1,128)} %broadcast_in_dim.42), calls=%async_computation.2 | async-start | bytes 8192 | tf_op jit(solution)/shard_map/all_to_all | solution.py:218
  70.3 0.1 pad_add_fusion.1.refs_1_
  70.4 7.9 %all-to-all-done.2 = f32[8,1,128]{2,1,0:T(1,128)S(1)} async-done(((f32[8,1,128]{2,1,0:T(1,128)}), f32[8,1,128]{2,1,0:T(1,128)S(1)}, u32[]{:S(2)}, u32[]{:S(2)}) %all-to-all-start.2) | async-done | bytes 4128 | tf_op jit(solution)/shard_map/all_to_all | solution.py:218
  78.3 0.6 broadcast_in_dim.43
  78.9 6.2 %all-to-all-start.3 = ((f32[8,1,128]{2,1,0:T(1,128)}), f32[8,1,128]{2,1,0:T(1,128)S(1)}, u32[]{:S(2)}, u32[]{:S(2)}) async-start(f32[8,1,128]{2,1,0:T(1,128)} %broadcast_in_dim.43), calls=%async_computation.3 | async-start | bytes 8192 | tf_op jit(solution)/shard_map/all_to_all | solution.py:218
  85.1 5.0 %attend.3 = (f32[4,128,512]{2,1,0:T(8,128)S(1)}, f32[4,128,128]{2,1,0:T(8,128)S(1)}) custom-call(s32[16]{0:T(128)S(1)} %copy-done.1, s32[3]{0:T(128)S(1)} %pad_add_fusion.2.refs_1_, bf16[4,128,512]{2,1,0:T(8,128)(2,1)S(1)} %all_gather.3.refs_2_, bf16[1152,256]{1,0:T(8,128)(2,1)S(1)} %get-tuple-element.16.refs_3_, ...), custom_call_target="tpu_custom_call" | custom-call | flops 2684354560 | bytes 2752512 | tf_op jit(solution)/shard_map/attend/pallas_call | solution.py:173
  90.1 0.0 copy-done.7
  90.1 0.0 collective-permute-done.4.refs_3_
  90.1 1.9 %collective-permute-start.5 = (bf16[640,256]{1,0:T(8,128)(2,1)S(1)}, bf16[640,256]{1,0:T(8,128)(2,1)S(1)}, u32[]{:S(2)}, u32[]{:S(2)}) collective-permute-start(bf16[640,256]{1,0:T(8,128)(2,1)S(1)} %slice.44), channel_id=1, source_target_pairs={{0,32},{32,64},{64,96},{96,128},{128,160},{160,192},{192,224},{224... | collective-permute-start | bytes 983048 | tf_op jit(solution)/shard_map/ppermute | solution.py:223
  92.0 0.0 collective-permute-done.6.refs_4_
  92.1 4.6 %collective-permute-start.7 = (bf16[512,256]{1,0:T(8,128)(2,1)S(1)}, bf16[512,256]{1,0:T(8,128)(2,1)S(1)}, u32[]{:S(2)}, u32[]{:S(2)}) collective-permute-start(bf16[512,256]{1,0:T(8,128)(2,1)S(1)} %slice.46), channel_id=1, source_target_pairs={{0,480},{32,0},{64,32},{96,64},{128,96},{160,128},{192,160},{224,1... | collective-permute-start | bytes 786440 | tf_op jit(solution)/shard_map/ppermute | solution.py:223
  96.7 8.0 %attend.4 = (f32[4,128,512]{2,1,0:T(8,128)S(1)}, f32[4,128,128]{2,1,0:T(8,128)S(1)}) custom-call(s32[16]{0:T(128)S(1)} %copy-done.1, s32[3]{0:T(128)S(1)} %pad_add_fusion.1.refs_1_, bf16[4,128,512]{2,1,0:T(8,128)(2,1)S(1)} %all_gather.3.refs_2_, bf16[1152,256]{1,0:T(8,128)(2,1)S(1)} %collective-permute-done.4.refs_3_, ...), custom_call_target="tpu_custom_call" | custom-call | flops 4831838208 | bytes 3276800 | tf_op jit(solution)/shard_map/attend/pallas_call | solution.py:173
  104.7 0.0 collective-permute-done.7.refs_4_
  104.7 0.0 collective-permute-done.5.refs_3_
  104.7 0.0 copy-start.6
  104.7 6.4 %attend.5 = bf16[4,128,640]{2,1,0:T(8,128)(2,1)} custom-call(s32[16]{0:T(128)S(1)} %copy-done.1, s32[2]{0:T(128)S(1)} %pad_add_fusion.refs_1_, bf16[4,128,512]{2,1,0:T(8,128)(2,1)S(1)} %all_gather.3.refs_2_, bf16[640,256]{1,0:T(8,128)(2,1)S(1)} %collective-permute-done.5.refs_3_, bf16[512,256]{1,0:T(8,128)(2,1)S(1)} %collective-permute-done.7.refs_4_, ...), custom_call_target="tpu_custom_call" | custom-call | flops 2415919104 | bytes 2686976 | tf_op jit(solution)/shard_map/attend/pallas_call | solution.py:173
  111.1 0.0 all-to-all-done.3
  111.1 5.0 %all-to-all-start = ((bf16[4,128,640]{2,1,0:T(8,128)(2,1)}), bf16[4,128,640]{2,1,0:T(8,128)(2,1)S(1)}, u32[]{:S(2)}, u32[]{:S(2)}) async-start(bf16[4,128,640]{2,1,0:T(8,128)(2,1)} %attend.5), calls=%async_computation | async-start | bytes 1310720 | tf_op jit(solution)/shard_map/all_to_all | solution.py:287
  116.1 0.0 copy-done.6
  116.1 0.6 fusion
  117.4 0.5 multiply_divide_fusion
  117.9 7.6 %all-to-all-done.parts_ref = bf16[4,128,640]{2,1,0:T(8,128)(2,1)S(1)} async-done(((bf16[4,128,640]{2,1,0:T(8,128)(2,1)}), bf16[4,128,640]{2,1,0:T(8,128)(2,1)S(1)}, u32[]{:S(2)}, u32[]{:S(2)}) %all-to-all-start) | async-done | bytes 655392 | tf_op jit(solution)/shard_map/all_to_all | solution.py:287
  125.5 0.0 copy-start.2
  125.5 0.8 copy-done.2
  126.3 2.8 %combine.1 = bf16[128,512]{1,0:T(8,128)(2,1)} custom-call(bf16[4,128,640]{2,1,0:T(8,128)(2,1)} %copy-done.2), custom_call_target="tpu_custom_call" | custom-call | tf_op jit(solution)/shard_map/combine/pallas_call | solution.py:208
  129.1 1.6 %reshape.73 = bf16[128,4,128]{2,1,0:T(4,128)(2,1)} reshape(bf16[128,512]{1,0:T(8,128)(2,1)} %combine.1) | data formatting | bytes 262144 | tf_op jit(solution)/shard_map/reshape | solution.py:288
  (22 shorter events, 0.4 us)
Async XLA Ops:
  0.6 29.2 %copy-start.3 = (bf16[256,2,1,128]{3,1,2,0:T(2,128)(2,1)S(1)}, bf16[256,2,1,128]{3,1,2,0:T(2,128)(2,1)}, u32[]{:S(2)}) copy-start(bf16[256,2,1,128]{3,1,2,0:T(2,128)(2,1)} %param.8) | copy-start | bytes 393220
  0.6 29.3 %copy-start.5 = (bf16[128,4,128]{2,1,0:T(4,128)(2,1)S(1)}, bf16[128,4,128]{2,1,0:T(4,128)(2,1)}, u32[]{:S(2)}) copy-start(bf16[128,4,128]{2,1,0:T(4,128)(2,1)} %param.7) | copy-start | bytes 393220
  0.7 37.0 %copy-start.1 = (s32[16]{0:T(128)S(1)}, s32[16]{0:T(128)}, u32[]{:S(2)}) copy-start(s32[16]{0:T(128)} %refs_0_.5) | copy-start | bytes 196
  1.6 36.7 %collective-permute-start.1 = (bf16[256,256]{1,0:T(8,128)(2,1)S(1)}, bf16[256,256]{1,0:T(8,128)(2,1)S(1)}, u32[]{:S(2)}, u32[]{:S(2)}) collective-permute-start(bf16[256,256]{1,0:T(8,128)(2,1)S(1)} %bitcast.35), channel_id=1, source_target_pairs={{0,384},{32,416},{64,448},{96,480},{128,0},{160,32},{192,64},{224,... | collective-permute-start | bytes 393224 | tf_op jit(solution)/shard_map/ppermute | solution.py:223
  15.8 30.1 %collective-permute-start = (bf16[384,256]{1,0:T(8,128)(2,1)S(1)}, bf16[384,256]{1,0:T(8,128)(2,1)S(1)}, u32[]{:S(2)}, u32[]{:S(2)}) collective-permute-start(bf16[384,256]{1,0:T(8,128)(2,1)S(1)} %pad_maximum_fusion), channel_id=1, source_target_pairs={{0,128},{32,160},{64,192},{96,224},{128,256},{160,288},{192,320},{... | collective-permute-start | bytes 589832 | tf_op jit(solution)/shard_map/ppermute | solution.py:223
  18.5 1.7 %copy-start = (bf16[128,9600]{1,0:T(8,128)(2,1)S(1)}, bf16[128,9600]{1,0:T(8,128)(2,1)}, u32[]{:S(2)}) copy-start(bf16[128,9600]{1,0:T(8,128)(2,1)} %logits_ref.1) | copy-start | bytes 7372804
  22.5 23.4 %copy-start.4 = (bf16[128,2,1,128]{3,1,2,0:T(2,128)(2,1)S(1)}, bf16[128,2,1,128]{3,1,2,0:T(2,128)(2,1)}, u32[]{:S(2)}) copy-start(bf16[128,2,1,128]{3,1,2,0:T(2,128)(2,1)} %param.9) | copy-start | bytes 196612
  23.2 15.0 %all-to-all-start.1 = ((f32[8,8,128]{2,1,0:T(8,128)}), f32[8,8,128]{2,1,0:T(8,128)S(1)}, u32[]{:S(2)}, u32[]{:S(2)}) async-start(f32[8,8,128]{2,1,0:T(8,128)} %broadcast_in_dim.22), calls=%async_computation.1 | async-start | bytes 65536 | tf_op jit(solution)/shard_map/all_to_all | solution.py:218
  38.3 12.2 %collective-permute-start.2 = (bf16[128,256]{1,0:T(8,128)(2,1)S(1)}, bf16[128,256]{1,0:T(8,128)(2,1)S(1)}, u32[]{:S(2)}, u32[]{:S(2)}) collective-permute-start(bf16[128,256]{1,0:T(8,128)(2,1)S(1)} %slice.42), channel_id=1, source_target_pairs={{0,384},{32,416},{64,448},{96,480},{128,0},{160,32},{192,64},{224,... | collective-permute-start | bytes 196616 | tf_op jit(solution)/shard_map/ppermute | solution.py:223
  46.0 9.2 %collective-permute-start.3 = (bf16[128,256]{1,0:T(8,128)(2,1)S(1)}, bf16[128,256]{1,0:T(8,128)(2,1)S(1)}, u32[]{:S(2)}, u32[]{:S(2)}) collective-permute-start(bf16[128,256]{1,0:T(8,128)(2,1)S(1)} %get-tuple-element.14), channel_id=1, source_target_pairs={{0,128},{32,160},{64,192},{96,224},{128,256},{160,288},{192,320},{... | collective-permute-start | bytes 196616 | tf_op jit(solution)/shard_map/ppermute | solution.py:223
  55.2 34.9 %collective-permute-start.4 = (bf16[1152,256]{1,0:T(8,128)(2,1)S(1)}, bf16[1152,256]{1,0:T(8,128)(2,1)S(1)}, u32[]{:S(2)}, u32[]{:S(2)}) collective-permute-start(bf16[1152,256]{1,0:T(8,128)(2,1)S(1)} %get-tuple-element.16.refs_3_), channel_id=1, source_target_pairs={{0,32},{32,64},{64,96},{96,128},{128,160},{160,192},{192,224},{224... | collective-permute-start | bytes 1769480 | tf_op jit(solution)/shard_map/ppermute | solution.py:223
  58.7 33.4 %collective-permute-start.6 = (bf16[1152,256]{1,0:T(8,128)(2,1)S(1)}, bf16[1152,256]{1,0:T(8,128)(2,1)S(1)}, u32[]{:S(2)}, u32[]{:S(2)}) collective-permute-start(bf16[1152,256]{1,0:T(8,128)(2,1)S(1)} %get-tuple-element.15), channel_id=1, source_target_pairs={{0,480},{32,0},{64,32},{96,64},{128,96},{160,128},{192,160},{224,1... | collective-permute-start | bytes 1769480 | tf_op jit(solution)/shard_map/ppermute | solution.py:223
  62.8 27.3 %copy-start.7 = (f32[128]{0:T(128)}, f32[128]{0:T(128)S(1)}, u32[]{:S(2)}) copy-start(f32[128]{0:T(128)S(1)} %compare_select_fusion) | copy-start | bytes 1540
  63.5 14.8 %all-to-all-start.2 = ((f32[8,1,128]{2,1,0:T(1,128)}), f32[8,1,128]{2,1,0:T(1,128)S(1)}, u32[]{:S(2)}, u32[]{:S(2)}) async-start(f32[8,1,128]{2,1,0:T(1,128)} %broadcast_in_dim.42), calls=%async_computation.2 | async-start | bytes 8192 | tf_op jit(solution)/shard_map/all_to_all | solution.py:218
  78.9 32.2 %all-to-all-start.3 = ((f32[8,1,128]{2,1,0:T(1,128)}), f32[8,1,128]{2,1,0:T(1,128)S(1)}, u32[]{:S(2)}, u32[]{:S(2)}) async-start(f32[8,1,128]{2,1,0:T(1,128)} %broadcast_in_dim.43), calls=%async_computation.3 | async-start | bytes 8192 | tf_op jit(solution)/shard_map/all_to_all | solution.py:218
  90.1 14.6 %collective-permute-start.5 = (bf16[640,256]{1,0:T(8,128)(2,1)S(1)}, bf16[640,256]{1,0:T(8,128)(2,1)S(1)}, u32[]{:S(2)}, u32[]{:S(2)}) collective-permute-start(bf16[640,256]{1,0:T(8,128)(2,1)S(1)} %slice.44), channel_id=1, source_target_pairs={{0,32},{32,64},{64,96},{96,128},{128,160},{160,192},{192,224},{224... | collective-permute-start | bytes 983048 | tf_op jit(solution)/shard_map/ppermute | solution.py:223
  92.1 12.6 %collective-permute-start.7 = (bf16[512,256]{1,0:T(8,128)(2,1)S(1)}, bf16[512,256]{1,0:T(8,128)(2,1)S(1)}, u32[]{:S(2)}, u32[]{:S(2)}) collective-permute-start(bf16[512,256]{1,0:T(8,128)(2,1)S(1)} %slice.46), channel_id=1, source_target_pairs={{0,480},{32,0},{64,32},{96,64},{128,96},{160,128},{192,160},{224,1... | collective-permute-start | bytes 786440 | tf_op jit(solution)/shard_map/ppermute | solution.py:223
  104.7 11.4 %copy-start.6 = (f32[16]{0:T(128)S(1)}, f32[16]{0:T(128)}, u32[]{:S(2)}) copy-start(f32[16]{0:T(128)} %param.13) | copy-start | bytes 196
  111.1 14.4 %all-to-all-start = ((bf16[4,128,640]{2,1,0:T(8,128)(2,1)}), bf16[4,128,640]{2,1,0:T(8,128)(2,1)S(1)}, u32[]{:S(2)}, u32[]{:S(2)}) async-start(bf16[4,128,640]{2,1,0:T(8,128)(2,1)} %attend.5), calls=%async_computation | async-start | bytes 1310720 | tf_op jit(solution)/shard_map/all_to_all | solution.py:287
  125.5 0.8 copy-start.2

commit v3 on v2

--- a/solution.py
+++ b/solution.py
@@ -12,7 +12,7 @@
 HEADS = 4
 ROWS_DEV = 128
 PLANE = 4
-TILE = 256
+TILE = 512
 SCALE = 1.0 / math.sqrt(HD)
 LOG2E = 1.4426950408889634
 Z = ("zh", "zl")
@@ -21,17 +21,22 @@
 MIB = 1 << 20
 
 
-def logit_kernel(token_ref, base_ref, logits_ref, out_ref, stat_ref):
+def logit_kernel(token_ref, base_ref, logits_ref, out_ref, stat_ref, target_ref):
     step = pl.program_id(0)
-    rows = logits_ref.shape[0]
-    width = logits_ref.shape[1]
+    rows, width = logits_ref.shape
+
+    @pl.when(step == 0)
+    def _():
+        wanted = jnp.broadcast_to(token_ref[...].astype(jnp.float32), target_ref.shape)
+        target_ref[...] = wanted.T.astype(jnp.int32) - base_ref[0]
+
     here = pl.ds(pl.multiple_of(step * rows, rows), rows)
     wide = logits_ref[...].astype(jnp.float32)
     peak = jnp.max(wide, axis=1, keepdims=True)
     total = jnp.sum(jnp.exp(wide - peak), axis=1, keepdims=True)
-    target = token_ref[...] - base_ref[0]
     columns = lax.broadcasted_iota(jnp.int32, (rows, width), 1)
-    picked = jnp.sum(jnp.where(columns == target, wide, 0.0), axis=1, keepdims=True)
+    matches = columns == target_ref[here, :1]
+    picked = jnp.sum(jnp.where(matches, wide, 0.0), axis=1, keepdims=True)
     lane = lax.broadcasted_iota(jnp.int32, (rows, 128), 1)
     stat_ref[here, :] = jnp.where(
         lane == 0, peak, jnp.where(lane == 1, total, picked)
@@ -39,29 +44,29 @@
 
     @pl.when(step == pl.num_programs(0) - 1)
     def _():
-        out_ref[...] = stat_ref[...].T[:8]
-
-
-def logit_stats(logits, token_ids, vocab_base):
+        out_ref[...] = jnp.broadcast_to(stat_ref[...].T[None, :8], out_ref.shape)
+
+
+def logit_stats(logits, token_ids, vocab_base, copies):
     rows, width = logits.shape
     block = 32
     return pl.pallas_call(
         logit_kernel,
         grid=(rows // block,),
         in_specs=[
-            pl.BlockSpec((block, 1), lambda i: (i, 0)),
+            pl.BlockSpec((1, rows), lambda i: (0, 0)),
             pl.BlockSpec(memory_space=pltpu.SMEM),
             pl.BlockSpec((block, width), lambda i: (i, 0)),
         ],
-        out_specs=pl.BlockSpec((8, 128), lambda i: (0, 0)),
-        out_shape=jax.ShapeDtypeStruct((8, 128), jnp.float32),
-        scratch_shapes=[pltpu.VMEM((rows, 128), jnp.float32)],
+        out_specs=pl.BlockSpec((copies, 8, rows), lambda i: (0, 0, 0)),
+        out_shape=jax.ShapeDtypeStruct((copies, 8, rows), jnp.float32),
+        scratch_shapes=[pltpu.VMEM((rows, 128), jnp.float32), pltpu.VMEM((rows, 128), jnp.int32)],
         compiler_params=pltpu.CompilerParams(vmem_limit_bytes=32 * MIB),
         cost_estimate=pl.CostEstimate(
             flops=8 * rows * width, bytes_accessed=2 * rows * width, transcendentals=rows * width
         ),
         name="logit_stats",
-    )(token_ids.reshape(rows, 1), vocab_base, logits)
+    )(token_ids.reshape(1, rows), vocab_base, logits)
 
 
 def nt(a, b):
@@ -185,31 +190,34 @@
 
 
 def combine_kernel(parts_ref, out_ref):
+    tops = []
+    for j in range(PLANE):
+        bits = parts_ref[j, :, HEADS * HD :].astype(jnp.float32)
+        tops.append(bits + pltpu.roll(bits, HD - 1, 1) + pltpu.roll(bits, HD - 2, 1))
+    top = jnp.maximum(jnp.maximum(tops[0], tops[1]), jnp.maximum(tops[2], tops[3]))
+    weights = [jnp.exp(x - top) for x in tops]
+    share = 1.0 / (weights[0] + weights[1] + weights[2] + weights[3])
+    weights = [x * share for x in weights]
+    heads = []
     for h in range(HEADS):
         lanes = slice(h * HD, (h + 1) * HD)
-        lse = []
-        for j in range(PLANE):
-            base = HEADS * HD + 3 * h
-            bits = parts_ref[j, :, HEADS * HD :].astype(jnp.float32)
-            lse.append(
-                bits[:, 3 * h : 3 * h + 1] + bits[:, 3 * h + 1 : 3 * h + 2] + bits[:, 3 * h + 2 : 3 * h + 3]
+        heads.append(
+            sum(
+                weights[j][:, 3 * h : 3 * h + 1] * parts_ref[j, :, lanes].astype(jnp.float32)
+                for j in range(PLANE)
             )
-        top = jnp.maximum(jnp.maximum(lse[0], lse[1]), jnp.maximum(lse[2], lse[3]))
-        weights = [jnp.exp(x - top) for x in lse]
-        share = 1.0 / (weights[0] + weights[1] + weights[2] + weights[3])
-        total = sum(
-            (weights[j] * share) * parts_ref[j, :, lanes].astype(jnp.float32) for j in range(PLANE)
         )
-        out_ref[:, lanes] = total.astype(jnp.bfloat16)
+    out_ref[...] = jnp.stack(heads, axis=1).astype(jnp.bfloat16)
 
 
 def combine(parts):
-    vmem = pl.BlockSpec(memory_space=pltpu.VMEM)
+    rows = 32
     return pl.pallas_call(
         combine_kernel,
-        in_specs=[vmem],
-        out_specs=vmem,
-        out_shape=jax.ShapeDtypeStruct((ROWS_DEV, HEADS * HD), jnp.bfloat16),
+        grid=(ROWS_DEV // rows,),
+        in_specs=[pl.BlockSpec((PLANE, rows, HEADS * HD + HD), lambda i: (0, i, 0))],
+        out_specs=pl.BlockSpec((rows, HEADS, HD), lambda i: (i, 0, 0)),
+        out_shape=jax.ShapeDtypeStruct((ROWS_DEV, HEADS, HD), jnp.bfloat16),
         name="combine",
     )(parts)
 
@@ -236,12 +244,26 @@
     )
     plus4 = shift(own, 4)
     minus4 = shift(own[:pb], -4)
-    q = lax.all_gather(queries.reshape(ROWS_DEV, HEADS * HD), PLANE_AXES, axis=0)
-    eight_a = shift(minus4[: pb // 2], -4)
-    eight_b = shift(plus4[pb // 2 : pb], 4)
+    q = to_all(queries.reshape(ROWS_DEV, HEADS * HD), PLANE_AXES, PLANE)
 
     vocab_base = (lax.axis_index("tp") * logits.shape[1]).astype(jnp.int32).reshape(1)
-    stats = to_all(logit_stats(logits, token_ids, vocab_base), "tp", lax.axis_size("tp"))
+    stats = logit_stats(logits, token_ids, vocab_base, lax.axis_size("tp"))
+    stats, q = lax.optimization_barrier((stats, q))
+    stats = lax.all_to_all(stats, "tp", 0, 0)
+    def place(*planes):
+        first_keys = [((p + depth) % depth * PLANE + spot) * rb for p in planes]
+        return jnp.stack([z * PLANE * ROWS_DEV] + first_keys).astype(jnp.int32)
+
+    send_right = jnp.concatenate([own[:pb], plus4[:pb], own[pb:], minus4], axis=0)
+    send_left = jnp.concatenate([own[:pb], minus4, plus4[pb:], plus4[:pb]], axis=0)
+    stats, *_ = lax.optimization_barrier((stats, send_right, send_left))
+    right = shift(send_right, 1)
+    left = shift(send_left, -1)
+    half_a, half_b, *_ = lax.optimization_barrier(
+        (minus4[: pb // 2], plus4[pb // 2 : pb], send_right, send_left)
+    )
+    eight_a = shift(half_a, -4)
+    eight_b = shift(half_b, 4)
     peaks, sums, picks = stats[:, 0], stats[:, 1], stats[:, 2]
     peak = jnp.max(peaks, axis=0)
     spread = jnp.sum(sums * jnp.exp(peaks - peak), axis=0)
@@ -253,39 +275,37 @@
     members = segment[:, None] == jnp.arange(128, dtype=jnp.int32)[None, :]
     part = jnp.sum(jnp.where(members, token_logprob[:, None], 0.0), axis=0)
     part = jnp.sum(to_all(part[None], ("zl",) + PLANE_AXES, 8)[:, 0], axis=0)
+
+    whole = ((0, 2 * pb, False), (2 * pb, 2 * pb + rb, True), (2 * pb + rb, 3 * pb + rb, False))
+    state = attend(
+        lengths, place(z, z - 4), q, [send_right, plus4], [whole, ((pb, pb + rb, True),)], (), False
+    )
+    part, _ = lax.optimization_barrier((part, state[1]))
+    eight = jnp.concatenate([eight_a, eight_b], axis=0)
+    right2 = shift(jnp.concatenate([right[: 2 * pb + rb], eight], axis=0), 1)
+    left2 = shift(jnp.concatenate([left[: 2 * pb], eight], axis=0), -1)
     part = jnp.sum(to_all(part[None], "zh", 8)[:, 0], axis=0)
+    state = attend(
+        lengths,
+        place(z - 1, z - 3),
+        q,
+        [right, left, eight],
+        [whole, whole, ((0, pb, False),)],
+        state,
+        False,
+    )
+    partial = attend(
+        lengths, place(z - 2), q, [right2, left2], [whole, ((0, 3 * pb, False),)], state, True
+    )
+    exchanged = lax.all_to_all(partial, PLANE_AXES, 0, 0)
+    context = combine(exchanged)
+
     response_sum = part[:responses]
     length_float = lengths.astype(jnp.float32)
     adjusted = rewards - 0.5 * length_float / 2048
     advantage = adjusted - jnp.mean(adjusted)
     response_objective = -advantage * response_sum / length_float
 
-    def place(*planes):
-        first_keys = [((p + depth) % depth * PLANE + spot) * rb for p in planes]
-        return jnp.stack([z * PLANE * ROWS_DEV] + first_keys).astype(jnp.int32)
-
-    send_right = jnp.concatenate(
-        [own[:pb], plus4[:pb], own[pb:], minus4, eight_a, eight_b], axis=0
-    )
-    send_left = jnp.concatenate(
-        [own[:pb], minus4, plus4[pb:], plus4[:pb], eight_a, eight_b], axis=0
-    )
-    right = shift(send_right, 1)
-    left = shift(send_left, -1)
-    whole = ((0, 2 * pb, False), (2 * pb, 2 * pb + rb, True), (2 * pb + rb, 4 * pb + rb, False))
-    state = attend(
-        lengths, place(z, z - 4), q, [send_right, plus4], [whole, ((pb, pb + rb, True),)], (), False
-    )
-    right2 = shift(right[: 2 * pb + rb], 1)
-    left2 = shift(left[: 2 * pb], -1)
-    state = attend(
-        lengths, place(z - 1, z - 3), q, [right, left], [whole, whole], state, False
-    )
-    partial = attend(
-        lengths, place(z - 2), q, [right2, left2], [whole[:2], whole[:1]], state, True
-    )
-    exchanged = lax.all_to_all(partial, PLANE_AXES, 0, 0)
-    context = combine(exchanged).reshape(ROWS_DEV, HEADS, HD)
     return (context, token_logprob, response_objective)
 
 

time: 131 us -> 132 us (level)
  starting transfers between devices: 63.3 us -> 75.9 us
  blocking collectives: 7.67 us -> 0 us
  waiting for transfers between devices: 22.8 us -> 17.1 us
  local copies, waits for them, and re-layouts: 8.92 us -> 6.87 us
  other arithmetic: 1.82 us -> 3.43 us
  Pallas kernels: 24.5 us -> 25.9 us
    ppermute x8, starting transfers between devices: 38.7 us -> 47.9 us  [shift(): lax.ppermute(x, Z, [(i, (i + distance) % depth) for i in range(depth)])]
    all_to_all x3, waiting for transfers between devices: 7.92 us -> 0.01 us  [to_all(): lax.all_to_all(jnp.broadcast_to(x[None], (count,) + x.shape), axes, 0, 0)]
    all_gather x1 -> x0, blocking collectives: 7.67 us -> none  [shards(): lax.all_gather(queries.reshape(ROWS_DEV, HEADS * HD), PLANE_AXES, axis=0)]
    all_to_all x0 -> x1, starting transfers between devices: none -> 6.66 us  [shards(): stats = lax.all_to_all(stats, 'tp', 0, 0)]
    all_to_all x0 -> x1, waiting for transfers between devices: none -> 6.58 us  [shards(): stats = lax.all_to_all(stats, 'tp', 0, 0)]
    ppermute x8, waiting for transfers between devices: 7.27 us -> 2.91 us  [shift(): lax.ppermute(x, Z, [(i, (i + distance) % depth) for i in range(depth)])]
    all_to_all x3, starting transfers between devices: 19.6 us -> 16.4 us  [to_all(): lax.all_to_all(jnp.broadcast_to(x[None], (count,) + x.shape), axes, 0, 0)]
    reshape x2 -> x0, local copies, waits for them, and re-layouts: 2.36 us -> none  [the longest x1 1.59 us: shards(): context = combine(exchanged).reshape(ROWS_DEV, HEADS, HD)]
  transfers between devices with their start and end apart: 12 -> 13, of which waited for: 4 -> 4; matrix products, arithmetic and copies ran while one was open for 4% -> 6% of each run, Pallas kernels for 17% -> 17%
where the time goes in v3:
time: 132 us; the launch traced here: 131 us
  starting transfers between devices  75.9 us (58%)
  Pallas kernels  25.9 us (20%)
  waiting for transfers between devices  17.1 us (13%)
  local copies, waits for them, and re-layouts  6.87 us (5%)
  other arithmetic  3.43 us (3%)
  between operations  1.59 us (1%)
    ppermute x8, starting transfers between devices, shift(): lax.ppermute(x, Z, [(i, (i + distance) % depth) for i in range(depth)])  47.9 us
    pallas_call x3, Pallas kernels, attend(): pl.pallas_call(functools.partial(attend_kernel, pieces, not state, last),...  19.2 us
    all_to_all x3, starting transfers between devices, to_all(): lax.all_to_all(jnp.broadcast_to(x[None], (count,) + x.shape), axes, 0, 0)  16.4 us
    all_to_all x1, waiting for transfers between devices, shards(): exchanged = lax.all_to_all(partial, PLANE_AXES, 0, 0)  7.59 us
    all_to_all x1, starting transfers between devices, shards(): stats = lax.all_to_all(stats, 'tp', 0, 0)  6.66 us
    all_to_all x1, waiting for transfers between devices, shards(): stats = lax.all_to_all(stats, 'tp', 0, 0)  6.58 us
    all_to_all x1, starting transfers between devices, shards(): exchanged = lax.all_to_all(partial, PLANE_AXES, 0, 0)  4.92 us
    unnamed x19, local copies, waits for them, and re-layouts  4.69 us
  transfers between devices with their start and end apart: 13, of which 4 were waited for; matrix products, arithmetic and copies ran while one was open for 6% of the time, Pallas kernels for 17%

profile of v3, /device:TPU:1, one launch (start us, length us, event | category | flops | bytes accessed | tf_op | source)
XLA Modules:
  0.0 130.7 jit_solution(13424467355567235787)
XLA Ops:
  0.6 0.0 copy-start.1
  0.6 0.0 copy-start.2
  0.7 0.0 copy-start
  0.7 1.1 copy.26
  1.7 13.3 %collective-permute-start.1 = (bf16[256,256]{1,0:T(8,128)(2,1)S(1)}, bf16[256,256]{1,0:T(8,128)(2,1)S(1)}, u32[]{:S(2)}, u32[]{:S(2)}) collective-permute-start(bf16[256,256]{1,0:T(8,128)(2,1)S(1)} %bitcast.38), channel_id=1, source_target_pairs={{0,384},{32,416},{64,448},{96,480},{128,0},{160,32},{192,64},{224,... | collective-permute-start | bytes 393224 | tf_op jit(solution)/shard_map/ppermute | solution.py:231
  15.0 0.9 copy.28
  15.9 0.7 pad_maximum_fusion.4
  16.6 1.9 %collective-permute-start = (bf16[384,256]{1,0:T(8,128)(2,1)}, bf16[384,256]{1,0:T(8,128)(2,1)S(1)}, u32[]{:S(2)}, u32[]{:S(2)}) collective-permute-start(bf16[384,256]{1,0:T(8,128)(2,1)} %pad_maximum_fusion.4), channel_id=1, source_target_pairs={{0,128},{32,160},{64,192},{96,224},{128,256},{160,288},{192,320},{... | collective-permute-start | bytes 589832 | tf_op jit(solution)/shard_map/ppermute | solution.py:231
  18.5 0.9 copy.27
  19.4 0.8 broadcast_in_dim.40
  20.2 4.9 %all-to-all-start = ((bf16[4,128,512]{2,1,0:T(8,128)(2,1)}), bf16[4,128,512]{2,1,0:T(8,128)(2,1)S(1)}, u32[]{:S(2)}, u32[]{:S(2)}) async-start(bf16[4,128,512]{2,1,0:T(8,128)(2,1)} %broadcast_in_dim.40), calls=%async_computation | async-start | bytes 1048576 | tf_op jit(solution)/shard_map/all_to_all | solution.py:226
  25.1 0.1 pad_add_fusion.refs_1_
  25.2 0.1 pad_add_fusion.2.refs_1_
  25.3 0.0 copy-done.1
  25.3 0.1 copy.16
  25.4 0.1 reduce.4
  25.5 0.0 copy-done.2
  25.5 0.0 copy-done
  25.5 3.1 %logit_stats.1 = f32[8,8,128]{2,1,0:T(8,128)} custom-call(s32[1,128]{1,0:T(1,128)S(1)} %bitcast.37, s32[1]{0:T(128)} %bitcast.3.base_ref, bf16[128,9600]{1,0:T(8,128)(2,1)S(1)} %copy-done), custom_call_target="tpu_custom_call" | custom-call | flops 9830400 | bytes 2457600 | tf_op jit(solution)/shard_map/logit_stats/pallas_call | solution.py:53
  28.6 0.1 convert_reduce_fusion
  28.7 0.0 collective-permute-done.1
  28.7 2.7 %collective-permute-done.refs_4_ = bf16[384,256]{1,0:T(8,128)(2,1)S(1)} collective-permute-done((bf16[384,256]{1,0:T(8,128)(2,1)}, bf16[384,256]{1,0:T(8,128)(2,1)S(1)}, u32[]{:S(2)}, u32[]{:S(2)}) %collective-permute-start) | collective-permute-done | bytes 196640 | tf_op jit(solution)/shard_map/ppermute | solution.py:231
  31.4 0.9 fusion.3
  32.3 4.4 %collective-permute-start.3 = (bf16[128,256]{1,0:T(8,128)(2,1)S(1)}, bf16[128,256]{1,0:T(8,128)(2,1)S(1)}, u32[]{:S(2)}, u32[]{:S(2)}) collective-permute-start(bf16[128,256]{1,0:T(8,128)(2,1)S(1)} %slice.43), channel_id=1, source_target_pairs={{0,384},{32,416},{64,448},{96,480},{128,0},{160,32},{192,64},{224,... | collective-permute-start | bytes 196616 | tf_op jit(solution)/shard_map/ppermute | solution.py:231
  36.7 4.8 %collective-permute-start.4 = (bf16[128,256]{1,0:T(8,128)(2,1)S(1)}, bf16[128,256]{1,0:T(8,128)(2,1)S(1)}, u32[]{:S(2)}, u32[]{:S(2)}) collective-permute-start(bf16[128,256]{1,0:T(8,128)(2,1)S(1)} %get-tuple-element.15), channel_id=1, source_target_pairs={{0,128},{32,160},{64,192},{96,224},{128,256},{160,288},{192,320},{... | collective-permute-start | bytes 196616 | tf_op jit(solution)/shard_map/ppermute | solution.py:231
  41.5 0.1 pad_add_fusion.1.refs_1_
  41.6 7.8 %collective-permute-start.2 = (bf16[896,256]{1,0:T(8,128)(2,1)S(1)}, bf16[896,256]{1,0:T(8,128)(2,1)S(1)}, u32[]{:S(2)}, u32[]{:S(2)}) collective-permute-start(bf16[896,256]{1,0:T(8,128)(2,1)S(1)} %get-tuple-element.24.refs_3_), channel_id=1, source_target_pairs={{0,32},{32,64},{64,96},{96,128},{128,160},{160,192},{192,224},{224... | collective-permute-start | bytes 1376264 | tf_op jit(solution)/shard_map/ppermute | solution.py:231
  49.3 7.9 %collective-permute-start.6 = (bf16[896,256]{1,0:T(8,128)(2,1)}, bf16[896,256]{1,0:T(8,128)(2,1)S(1)}, u32[]{:S(2)}, u32[]{:S(2)}) collective-permute-start(bf16[896,256]{1,0:T(8,128)(2,1)} %get-tuple-element.23), channel_id=1, source_target_pairs={{0,480},{32,0},{64,32},{96,64},{128,96},{160,128},{192,160},{224,1... | collective-permute-start | bytes 1376264 | tf_op jit(solution)/shard_map/ppermute | solution.py:231
  57.2 0.0 all-to-all-done.refs_2_
  57.2 6.7 %all-to-all-start.2 = ((f32[8,8,128]{2,1,0:T(8,128)}), f32[8,8,128]{2,1,0:T(8,128)S(1)}, u32[]{:S(2)}, u32[]{:S(2)}) async-start(f32[8,8,128]{2,1,0:T(8,128)} %logit_stats.1), calls=%async_computation.2 | async-start | bytes 65536 | tf_op jit(solution)/shard_map/all_to_all | solution.py:252
  63.9 0.0 collective-permute-done.3
  63.9 0.0 collective-permute-done.4
  63.9 6.6 %all-to-all-done.2 = f32[8,8,128]{2,1,0:T(8,128)S(1)} async-done(((f32[8,8,128]{2,1,0:T(8,128)}), f32[8,8,128]{2,1,0:T(8,128)S(1)}, u32[]{:S(2)}, u32[]{:S(2)}) %all-to-all-start.2) | async-done | bytes 32800 | tf_op jit(solution)/shard_map/all_to_all | solution.py:252
  70.6 0.0 copy-start.7
  70.6 0.1 select_reduce_fusion
  70.7 0.6 broadcast_in_dim.44
  71.3 6.5 %all-to-all-start.3 = ((f32[8,1,128]{2,1,0:T(1,128)}), f32[8,1,128]{2,1,0:T(1,128)S(1)}, u32[]{:S(2)}, u32[]{:S(2)}) async-start(f32[8,1,128]{2,1,0:T(1,128)} %broadcast_in_dim.44), calls=%async_computation.3 | async-start | bytes 8192 | tf_op jit(solution)/shard_map/all_to_all | solution.py:226
  77.8 4.1 %attend.3 = (f32[4,128,512]{2,1,0:T(8,128)S(1)}, f32[4,128,128]{2,1,0:T(8,128)S(1)}) custom-call(s32[16]{0:T(128)S(1)} %copy-done.1, s32[3]{0:T(128)S(1)} %pad_add_fusion.2.refs_1_, bf16[4,128,512]{2,1,0:T(8,128)(2,1)S(1)} %all-to-all-done.refs_2_, bf16[896,256]{1,0:T(8,128)(2,1)S(1)} %get-tuple-element.24.refs_3_, ...), custom_call_target="tpu_custom_call" | custom-call | flops 2147483648 | bytes 2621440 | tf_op jit(solution)/shard_map/attend/pallas_call | solution.py:178
  81.9 0.0 copy-done.7
  81.9 0.0 copy-start.3
  81.9 1.0 copy-done.3
  82.9 0.0 all-to-all-done.3
  82.9 0.6 broadcast_in_dim.45
  83.5 5.0 %all-to-all-start.4 = ((f32[8,1,128]{2,1,0:T(1,128)}), f32[8,1,128]{2,1,0:T(1,128)S(1)}, u32[]{:S(2)}, u32[]{:S(2)}) async-start(f32[8,1,128]{2,1,0:T(1,128)} %broadcast_in_dim.45), calls=%async_computation.4 | async-start | bytes 8192 | tf_op jit(solution)/shard_map/all_to_all | solution.py:226
  88.5 0.0 copy-start.4
  88.5 0.0 collective-permute-done.2.refs_3_
  88.6 3.4 %collective-permute-start.5 = (bf16[896,256]{1,0:T(8,128)(2,1)S(1)}, bf16[896,256]{1,0:T(8,128)(2,1)S(1)}, u32[]{:S(2)}, u32[]{:S(2)}) collective-permute-start(bf16[896,256]{1,0:T(8,128)(2,1)S(1)} %pad_maximum_fusion.2), channel_id=1, source_target_pairs={{0,32},{32,64},{64,96},{96,128},{128,160},{160,192},{192,224},{224... | collective-permute-start | bytes 1376264 | tf_op jit(solution)/shard_map/ppermute | solution.py:231
  92.0 0.0 collective-permute-done.6.refs_4_
  92.1 4.5 %collective-permute-start.7 = (bf16[768,256]{1,0:T(8,128)(2,1)S(1)}, bf16[768,256]{1,0:T(8,128)(2,1)S(1)}, u32[]{:S(2)}, u32[]{:S(2)}) collective-permute-start(bf16[768,256]{1,0:T(8,128)(2,1)S(1)} %pad_maximum_fusion.3), channel_id=1, source_target_pairs={{0,480},{32,0},{64,32},{96,64},{128,96},{160,128},{192,160},{224,1... | collective-permute-start | bytes 1179656 | tf_op jit(solution)/shard_map/ppermute | solution.py:231
  96.6 0.0 copy-done.4
  96.6 7.6 %attend.4 = (f32[4,128,512]{2,1,0:T(8,128)S(1)}, f32[4,128,128]{2,1,0:T(8,128)S(1)}) custom-call(s32[16]{0:T(128)S(1)} %copy-done.1, s32[3]{0:T(128)S(1)} %pad_add_fusion.1.refs_1_, bf16[4,128,512]{2,1,0:T(8,128)(2,1)S(1)} %all-to-all-done.refs_2_, bf16[896,256]{1,0:T(8,128)(2,1)S(1)} %collective-permute-done.2.refs_3_, ...), custom_call_target="tpu_custom_call" | custom-call | flops 4294967296 | bytes 3145728 | tf_op jit(solution)/shard_map/attend/pallas_call | solution.py:178
  104.2 0.0 collective-permute-done.7.refs_4_
  104.2 0.2 collective-permute-done.5.refs_3_
  104.5 0.0 copy-start.6
  104.5 7.5 %attend.5 = bf16[4,128,640]{2,1,0:T(8,128)(2,1)} custom-call(s32[16]{0:T(128)S(1)} %copy-done.1, s32[2]{0:T(128)S(1)} %pad_add_fusion.refs_1_, bf16[4,128,512]{2,1,0:T(8,128)(2,1)S(1)} %all-to-all-done.refs_2_, bf16[896,256]{1,0:T(8,128)(2,1)S(1)} %collective-permute-done.5.refs_3_, bf16[768,256]{1,0:T(8,128)(2,1)S(1)} %collective-permute-done.7.refs_4_, ...), custom_call_target="tpu_custom_call" | custom-call | flops 3489660928 | bytes 2949120 | tf_op jit(solution)/shard_map/attend/pallas_call | solution.py:178
  111.9 0.0 all-to-all-done.4
  112.0 4.9 %all-to-all-start.1 = ((bf16[4,128,640]{2,1,0:T(8,128)(2,1)}), bf16[4,128,640]{2,1,0:T(8,128)(2,1)S(1)}, u32[]{:S(2)}, u32[]{:S(2)}) async-start(bf16[4,128,640]{2,1,0:T(8,128)(2,1)} %attend.5), calls=%async_computation.1 | async-start | bytes 1310720 | tf_op jit(solution)/shard_map/all_to_all | solution.py:300
  116.9 0.0 copy-done.6
  116.9 0.6 fusion.7
  118.1 0.5 multiply_divide_fusion
  118.7 7.6 %all-to-all-done.1.parts_ref = bf16[4,128,640]{2,1,0:T(8,128)(2,1)S(1)} async-done(((bf16[4,128,640]{2,1,0:T(8,128)(2,1)}), bf16[4,128,640]{2,1,0:T(8,128)(2,1)S(1)}, u32[]{:S(2)}, u32[]{:S(2)}) %all-to-all-start.1) | async-done | bytes 655392 | tf_op jit(solution)/shard_map/all_to_all | solution.py:300
  126.3 0.0 copy-start.5
  126.3 0.8 copy-done.5
  127.1 3.6 %combine.1 = bf16[128,4,128]{2,1,0:T(4,128)(2,1)} custom-call(bf16[4,128,640]{2,1,0:T(8,128)(2,1)} %copy-done.5), custom_call_target="tpu_custom_call" | custom-call | tf_op jit(solution)/shard_map/combine/pallas_call | solution.py:215
  (17 shorter events, 0.3 us)
Async XLA Ops:
  0.6 24.6 %copy-start.1 = (s32[16]{0:T(128)S(1)}, s32[16]{0:T(128)}, u32[]{:S(2)}) copy-start(s32[16]{0:T(128)} %refs_0_.5) | copy-start | bytes 196
  0.6 24.9 %copy-start.2 = (s32[128]{0:T(128)S(1)}, s32[128]{0:T(128)}, u32[]{:S(2)}) copy-start(s32[128]{0:T(128)} %param.11) | copy-start | bytes 1540
  0.7 24.9 %copy-start = (bf16[128,9600]{1,0:T(8,128)(2,1)S(1)}, bf16[128,9600]{1,0:T(8,128)(2,1)}, u32[]{:S(2)}) copy-start(bf16[128,9600]{1,0:T(8,128)(2,1)} %logits_ref.1) | copy-start | bytes 7372804
  1.7 27.0 %collective-permute-start.1 = (bf16[256,256]{1,0:T(8,128)(2,1)S(1)}, bf16[256,256]{1,0:T(8,128)(2,1)S(1)}, u32[]{:S(2)}, u32[]{:S(2)}) collective-permute-start(bf16[256,256]{1,0:T(8,128)(2,1)S(1)} %bitcast.38), channel_id=1, source_target_pairs={{0,384},{32,416},{64,448},{96,480},{128,0},{160,32},{192,64},{224,... | collective-permute-start | bytes 393224 | tf_op jit(solution)/shard_map/ppermute | solution.py:231
  16.6 14.8 %collective-permute-start = (bf16[384,256]{1,0:T(8,128)(2,1)}, bf16[384,256]{1,0:T(8,128)(2,1)S(1)}, u32[]{:S(2)}, u32[]{:S(2)}) collective-permute-start(bf16[384,256]{1,0:T(8,128)(2,1)} %pad_maximum_fusion.4), channel_id=1, source_target_pairs={{0,128},{32,160},{64,192},{96,224},{128,256},{160,288},{192,320},{... | collective-permute-start | bytes 589832 | tf_op jit(solution)/shard_map/ppermute | solution.py:231
  20.2 37.0 %all-to-all-start = ((bf16[4,128,512]{2,1,0:T(8,128)(2,1)}), bf16[4,128,512]{2,1,0:T(8,128)(2,1)S(1)}, u32[]{:S(2)}, u32[]{:S(2)}) async-start(bf16[4,128,512]{2,1,0:T(8,128)(2,1)} %broadcast_in_dim.40), calls=%async_computation | async-start | bytes 1048576 | tf_op jit(solution)/shard_map/all_to_all | solution.py:226
  32.3 31.6 %collective-permute-start.3 = (bf16[128,256]{1,0:T(8,128)(2,1)S(1)}, bf16[128,256]{1,0:T(8,128)(2,1)S(1)}, u32[]{:S(2)}, u32[]{:S(2)}) collective-permute-start(bf16[128,256]{1,0:T(8,128)(2,1)S(1)} %slice.43), channel_id=1, source_target_pairs={{0,384},{32,416},{64,448},{96,480},{128,0},{160,32},{192,64},{224,... | collective-permute-start | bytes 196616 | tf_op jit(solution)/shard_map/ppermute | solution.py:231
  36.7 27.2 %collective-permute-start.4 = (bf16[128,256]{1,0:T(8,128)(2,1)S(1)}, bf16[128,256]{1,0:T(8,128)(2,1)S(1)}, u32[]{:S(2)}, u32[]{:S(2)}) collective-permute-start(bf16[128,256]{1,0:T(8,128)(2,1)S(1)} %get-tuple-element.15), channel_id=1, source_target_pairs={{0,128},{32,160},{64,192},{96,224},{128,256},{160,288},{192,320},{... | collective-permute-start | bytes 196616 | tf_op jit(solution)/shard_map/ppermute | solution.py:231
  41.6 47.0 %collective-permute-start.2 = (bf16[896,256]{1,0:T(8,128)(2,1)S(1)}, bf16[896,256]{1,0:T(8,128)(2,1)S(1)}, u32[]{:S(2)}, u32[]{:S(2)}) collective-permute-start(bf16[896,256]{1,0:T(8,128)(2,1)S(1)} %get-tuple-element.24.refs_3_), channel_id=1, source_target_pairs={{0,32},{32,64},{64,96},{96,128},{128,160},{160,192},{192,224},{224... | collective-permute-start | bytes 1376264 | tf_op jit(solution)/shard_map/ppermute | solution.py:231
  49.3 42.7 %collective-permute-start.6 = (bf16[896,256]{1,0:T(8,128)(2,1)}, bf16[896,256]{1,0:T(8,128)(2,1)S(1)}, u32[]{:S(2)}, u32[]{:S(2)}) collective-permute-start(bf16[896,256]{1,0:T(8,128)(2,1)} %get-tuple-element.23), channel_id=1, source_target_pairs={{0,480},{32,0},{64,32},{96,64},{128,96},{160,128},{192,160},{224,1... | collective-permute-start | bytes 1376264 | tf_op jit(solution)/shard_map/ppermute | solution.py:231
  57.2 13.3 %all-to-all-start.2 = ((f32[8,8,128]{2,1,0:T(8,128)}), f32[8,8,128]{2,1,0:T(8,128)S(1)}, u32[]{:S(2)}, u32[]{:S(2)}) async-start(f32[8,8,128]{2,1,0:T(8,128)} %logit_stats.1), calls=%async_computation.2 | async-start | bytes 65536 | tf_op jit(solution)/shard_map/all_to_all | solution.py:252
  70.6 11.3 %copy-start.7 = (f32[128]{0:T(128)}, f32[128]{0:T(128)S(1)}, u32[]{:S(2)}) copy-start(f32[128]{0:T(128)S(1)} %compare_select_fusion) | copy-start | bytes 1540
  71.3 11.6 %all-to-all-start.3 = ((f32[8,1,128]{2,1,0:T(1,128)}), f32[8,1,128]{2,1,0:T(1,128)S(1)}, u32[]{:S(2)}, u32[]{:S(2)}) async-start(f32[8,1,128]{2,1,0:T(1,128)} %broadcast_in_dim.44), calls=%async_computation.3 | async-start | bytes 8192 | tf_op jit(solution)/shard_map/all_to_all | solution.py:226
  81.9 1.0 copy-start.3
  83.5 28.5 %all-to-all-start.4 = ((f32[8,1,128]{2,1,0:T(1,128)}), f32[8,1,128]{2,1,0:T(1,128)S(1)}, u32[]{:S(2)}, u32[]{:S(2)}) async-start(f32[8,1,128]{2,1,0:T(1,128)} %broadcast_in_dim.45), calls=%async_computation.4 | async-start | bytes 8192 | tf_op jit(solution)/shard_map/all_to_all | solution.py:226
  88.5 8.1 %copy-start.4 = (f32[4,128,512]{2,1,0:T(8,128)S(1)}, f32[4,128,512]{2,1,0:T(8,128)}, u32[]{:S(2)}) copy-start(f32[4,128,512]{2,1,0:T(8,128)} %copy-done.3) | copy-start | bytes 3145732
  88.6 15.8 %collective-permute-start.5 = (bf16[896,256]{1,0:T(8,128)(2,1)S(1)}, bf16[896,256]{1,0:T(8,128)(2,1)S(1)}, u32[]{:S(2)}, u32[]{:S(2)}) collective-permute-start(bf16[896,256]{1,0:T(8,128)(2,1)S(1)} %pad_maximum_fusion.2), channel_id=1, source_target_pairs={{0,32},{32,64},{64,96},{96,128},{128,160},{160,192},{192,224},{224... | collective-permute-start | bytes 1376264 | tf_op jit(solution)/shard_map/ppermute | solution.py:231
  92.1 12.1 %collective-permute-start.7 = (bf16[768,256]{1,0:T(8,128)(2,1)S(1)}, bf16[768,256]{1,0:T(8,128)(2,1)S(1)}, u32[]{:S(2)}, u32[]{:S(2)}) collective-permute-start(bf16[768,256]{1,0:T(8,128)(2,1)S(1)} %pad_maximum_fusion.3), channel_id=1, source_target_pairs={{0,480},{32,0},{64,32},{96,64},{128,96},{160,128},{192,160},{224,1... | collective-permute-start | bytes 1179656 | tf_op jit(solution)/shard_map/ppermute | solution.py:231
  104.5 12.4 %copy-start.6 = (f32[16]{0:T(128)S(1)}, f32[16]{0:T(128)}, u32[]{:S(2)}) copy-start(f32[16]{0:T(128)} %param.13) | copy-start | bytes 196
  112.0 14.3 %all-to-all-start.1 = ((bf16[4,128,640]{2,1,0:T(8,128)(2,1)}), bf16[4,128,640]{2,1,0:T(8,128)(2,1)S(1)}, u32[]{:S(2)}, u32[]{:S(2)}) async-start(bf16[4,128,640]{2,1,0:T(8,128)(2,1)} %attend.5), calls=%async_computation.1 | async-start | bytes 1310720 | tf_op jit(solution)/shard_map/all_to_all | solution.py:300
  126.3 0.8 copy-start.5

commit v4 on v3

--- a/solution.py
+++ b/solution.py
@@ -17,7 +17,7 @@
 LOG2E = 1.4426950408889634
 Z = ("zh", "zl")
 CTX = Z + ("yl", "core")
-PLANE_AXES = ("yl", "core")
+SHARE = ("zl", "yl")
 MIB = 1 << 20
 
 
@@ -95,7 +95,9 @@
     per = TILE // ROWS_DEV
 
     def row_tile(t, carry):
-        rows = place_ref[0] + t * TILE + lax.broadcasted_iota(jnp.int32, (TILE, 1), 0)
+        index = t * TILE + lax.broadcasted_iota(jnp.int32, (TILE, 1), 0)
+        planes, spots = index // (2 * ROWS_DEV), index // ROWS_DEV % 2
+        rows = place_ref[0] + (planes * PLANE + spots * 2) * ROWS_DEV + index % ROWS_DEV
         start = jnp.zeros((TILE, 1), jnp.int32)
         edge = jnp.int32(0)
         for r in range(lengths_ref.shape[0]):
@@ -117,9 +119,9 @@
                     s = nt(q, kv_ref[low:high, :HD])
                     if masked:
                         answer += 1
-                        keys = place_ref[answer] + lax.broadcasted_iota(
-                            jnp.int32, (TILE, high - low), 1
-                        )
+                        column = lax.broadcasted_iota(jnp.int32, (TILE, high - low), 1)
+                        keys = place_ref[answer] + column % ROWS_DEV
+                        keys = keys - column // ROWS_DEV * (2 * PLANE * ROWS_DEV)
                         s = jnp.where((keys >= start) & (keys <= rows), s, -1e30)
                     tops.append(jnp.max(s, axis=1, keepdims=True))
                     scores.append((s, v_ref, low, high))
@@ -226,86 +228,59 @@
     return lax.all_to_all(jnp.broadcast_to(x[None], (count,) + x.shape), axes, 0, 0)
 
 
-def shift(x, distance):
-    depth = lax.axis_size("zh") * lax.axis_size("zl")
-    return lax.ppermute(x, Z, [(i, (i + distance) % depth) for i in range(depth)])
-
-
 def shards(queries, prompt_kv, response_kv, logits, token_ids, lengths, rewards):
+    pair = lax.axis_index("zh")
     z = lax.axis_index(Z)
-    spot = lax.axis_index(PLANE_AXES)
-    depth = lax.axis_size("zh") * lax.axis_size("zl")
+    row = lax.axis_index("yl")
+    core = lax.axis_index("core")
+    pairs = lax.axis_size("zh")
     responses = lengths.shape[0]
     pb = prompt_kv.shape[0]
     rb = response_kv.shape[0]
 
-    own = jnp.concatenate(
-        [prompt_kv.reshape(pb, 2 * HD), response_kv.reshape(rb, 2 * HD)], axis=0
-    )
-    plus4 = shift(own, 4)
-    minus4 = shift(own[:pb], -4)
-    q = to_all(queries.reshape(ROWS_DEV, HEADS * HD), PLANE_AXES, PLANE)
+    prompt = lax.all_gather(prompt_kv.reshape(pb, 2 * HD), ("zh", "core"), axis=0, tiled=True)
+    q = lax.all_gather(queries.reshape(ROWS_DEV, HEADS * HD), SHARE, axis=0)
 
     vocab_base = (lax.axis_index("tp") * logits.shape[1]).astype(jnp.int32).reshape(1)
     stats = logit_stats(logits, token_ids, vocab_base, lax.axis_size("tp"))
-    stats, q = lax.optimization_barrier((stats, q))
     stats = lax.all_to_all(stats, "tp", 0, 0)
-    def place(*planes):
-        first_keys = [((p + depth) % depth * PLANE + spot) * rb for p in planes]
-        return jnp.stack([z * PLANE * ROWS_DEV] + first_keys).astype(jnp.int32)
-
-    send_right = jnp.concatenate([own[:pb], plus4[:pb], own[pb:], minus4], axis=0)
-    send_left = jnp.concatenate([own[:pb], minus4, plus4[pb:], plus4[:pb]], axis=0)
-    stats, *_ = lax.optimization_barrier((stats, send_right, send_left))
-    right = shift(send_right, 1)
-    left = shift(send_left, -1)
-    half_a, half_b, *_ = lax.optimization_barrier(
-        (minus4[: pb // 2], plus4[pb // 2 : pb], send_right, send_left)
-    )
-    eight_a = shift(half_a, -4)
-    eight_b = shift(half_b, 4)
+
+    own = response_kv.reshape(rb, 2 * HD)
+    before = [
+        lax.ppermute(own, "zh", [(i, (i + d) % pairs) for i in range(pairs)]) for d in (1, 2)
+    ]
+    mine = jnp.concatenate([own] + before, axis=0)
+    other = lax.ppermute(mine, "core", [(0, 1), (1, 0)])
+
     peaks, sums, picks = stats[:, 0], stats[:, 1], stats[:, 2]
     peak = jnp.max(peaks, axis=0)
     spread = jnp.sum(sums * jnp.exp(peaks - peak), axis=0)
     logprob = jnp.sum(picks, axis=0) - peak - jnp.log(spread)
     ends_at = jnp.cumsum(lengths)
-    rows = (z * PLANE + spot) * ROWS_DEV + jnp.arange(ROWS_DEV, dtype=jnp.int32)
+    block = z * PLANE + row * 2
+    rows = (block + core) * ROWS_DEV + jnp.arange(ROWS_DEV, dtype=jnp.int32)
     segment = jnp.sum((rows[:, None] >= ends_at[None, :]).astype(jnp.int32), axis=1)
     token_logprob = jnp.where(segment < responses, logprob, 0.0)
     members = segment[:, None] == jnp.arange(128, dtype=jnp.int32)[None, :]
     part = jnp.sum(jnp.where(members, token_logprob[:, None], 0.0), axis=0)
-    part = jnp.sum(to_all(part[None], ("zl",) + PLANE_AXES, 8)[:, 0], axis=0)
-
-    whole = ((0, 2 * pb, False), (2 * pb, 2 * pb + rb, True), (2 * pb + rb, 3 * pb + rb, False))
-    state = attend(
-        lengths, place(z, z - 4), q, [send_right, plus4], [whole, ((pb, pb + rb, True),)], (), False
-    )
-    part, _ = lax.optimization_barrier((part, state[1]))
-    eight = jnp.concatenate([eight_a, eight_b], axis=0)
-    right2 = shift(jnp.concatenate([right[: 2 * pb + rb], eight], axis=0), 1)
-    left2 = shift(jnp.concatenate([left[: 2 * pb], eight], axis=0), -1)
-    part = jnp.sum(to_all(part[None], "zh", 8)[:, 0], axis=0)
-    state = attend(
-        lengths,
-        place(z - 1, z - 3),
-        q,
-        [right, left, eight],
-        [whole, whole, ((0, pb, False),)],
-        state,
-        False,
-    )
-    partial = attend(
-        lengths, place(z - 2), q, [right2, left2], [whole, ((0, 3 * pb, False),)], state, True
-    )
-    exchanged = lax.all_to_all(partial, PLANE_AXES, 0, 0)
-    context = combine(exchanged)
-
+    part = jnp.sum(to_all(part[None], CTX, 64)[:, 0], axis=0)
     response_sum = part[:responses]
     length_float = lengths.astype(jnp.float32)
     adjusted = rewards - 0.5 * length_float / 2048
     advantage = adjusted - jnp.mean(adjusted)
     response_objective = -advantage * response_sum / length_float
 
+    first_row = (pair * 2 * PLANE + core) * ROWS_DEV
+    place = jnp.stack(
+        [first_row, (block + core) * ROWS_DEV, (block + 1 - core) * ROWS_DEV]
+    ).astype(jnp.int32)
+    masked = ((0, 3 * rb, True),)
+    state = attend(lengths, place, q, [mine, other], [masked, masked], (), False)
+    half = prompt.shape[0] // 2
+    spans = ((0, half, False), (half, 2 * half, False))
+    partial = attend(lengths, place, q, [prompt], [spans], state, True)
+    exchanged = lax.all_to_all(partial, SHARE, 0, 0)
+    context = combine(exchanged)
     return (context, token_logprob, response_objective)
 
 

time: 132 us -> 113 us (0.86)
  starting transfers between devices: 75.9 us -> 39.9 us
  blocking collectives: 0 us -> 14.6 us
  between operations: 1.59 us -> 14.9 us
  waiting for transfers between devices: 17.1 us -> 7.39 us
  other arithmetic: 3.43 us -> 1.67 us
    ppermute x8 -> x3, starting transfers between devices: 47.9 us -> 20.7 us  [the longest x2 14.5 us: shards(): lax.ppermute(own, 'zh', [(i, (i + d) % pairs) for i in range(pairs)])]
    all_gather x0 -> x1, blocking collectives: none -> 14.6 us  [shards(): q = lax.all_gather(queries.reshape(ROWS_DEV, HEADS * HD), SHARE, axis=0)]
    all_to_all x3 -> x1, starting transfers between devices: 16.4 us -> 9.03 us  [to_all(): lax.all_to_all(jnp.broadcast_to(x[None], (count,) + x.shape), axes, 0, 0)]
    all_to_all x1, waiting for transfers between devices: 6.58 us -> 0.01 us  [shards(): stats = lax.all_to_all(stats, 'tp', 0, 0)]
    ppermute x8 -> x3, waiting for transfers between devices: 2.91 us -> 0.01 us  [the longest x2 0.01 us: shards(): lax.ppermute(own, 'zh', [(i, (i + d) % pairs) for i in range(pairs)])]
    unnamed x19 -> x22, local copies, waits for them, and re-layouts: 4.69 us -> 7.28 us
    concatenate x5 -> x0, other arithmetic: 1.61 us -> none  [the longest x1 0.85 us: shards(): jnp.concatenate([own[:pb], minus4, plus4[pb:], plus4[:pb]], axis=0)]
    all_to_all x1, starting transfers between devices: 4.92 us -> 3.48 us  [shards(): exchanged = lax.all_to_all(partial, SHARE, 0, 0)]
  transfers between devices with their start and end apart: 13 -> 7, of which waited for: 4 -> 2; matrix products, arithmetic and copies ran while one was open for 6% -> 3% of each run, Pallas kernels for 17% -> 19%
where the time goes in v4:
time: 113 us; the launch traced here: 112 us
  starting transfers between devices  39.9 us (35%)
  Pallas kernels  25.1 us (22%)
  between operations  14.9 us (13%)
  blocking collectives  14.6 us (13%)
  local copies, waits for them, and re-layouts  8.06 us (7%)
  waiting for transfers between devices  7.39 us (7%)
  other arithmetic  1.67 us (1%)
    pallas_call x2, Pallas kernels, attend(): pl.pallas_call(functools.partial(attend_kernel, pieces, not state, last),...  18.4 us
    all_gather x1, blocking collectives, shards(): q = lax.all_gather(queries.reshape(ROWS_DEV, HEADS * HD), SHARE, axis=0)  14.6 us
    ppermute x2, starting transfers between devices, shards(): lax.ppermute(own, 'zh', [(i, (i + d) % pairs) for i in range(pairs)])  14.5 us
    all_to_all x1, starting transfers between devices, to_all(): lax.all_to_all(jnp.broadcast_to(x[None], (count,) + x.shape), axes, 0, 0)  9.03 us
    unnamed x22, local copies, waits for them, and re-layouts  7.28 us
    all_to_all x1, waiting for transfers between devices, shards(): exchanged = lax.all_to_all(partial, SHARE, 0, 0)  7.15 us
    all_to_all x1, starting transfers between devices, shards(): stats = lax.all_to_all(stats, 'tp', 0, 0)  6.65 us
    ppermute x1, starting transfers between devices, shards(): other = lax.ppermute(mine, 'core', [(0, 1), (1, 0)])  6.18 us
  transfers between devices with their start and end apart: 7, of which 2 were waited for; matrix products, arithmetic and copies ran while one was open for 3% of the time, Pallas kernels for 19%

profile of v4, /device:TPU:1, one launch (start us, length us, event | category | flops | bytes accessed | tf_op | source)
XLA Modules:
  0.0 111.6 jit_solution(8682451982083297797)
XLA Ops:
  7.2 0.0 copy-start.5
  7.2 0.0 copy-start.1
  7.2 0.0 copy-start.6
  7.2 0.0 all-gather.2.cloned.1.call-start
  7.2 1.6 %copy.28 = bf16[32,8,2,128]{3,1,2,0:T(8,128)(2,1)} copy(bf16[32,8,2,128]{3,2,1,0:T(2,128)(2,1)} %bitcast.30) | data formatting | bytes 262144
  8.9 0.0 all-gather.2.cloned.1.call-update
  8.9 0.9 copy.29
  9.7 9.6 %collective-permute-start.1 = (bf16[128,256]{1,0:T(8,128)(2,1)S(1)}, bf16[128,256]{1,0:T(8,128)(2,1)S(1)}, u32[]{:S(2)}, u32[]{:S(2)}) collective-permute-start(bf16[128,256]{1,0:T(8,128)(2,1)S(1)} %bitcast.32), channel_id=1, source_target_pairs={{0,128},{64,192},{128,256},{192,320},{256,384},{320,448},{384,0},{... | collective-permute-start | bytes 196616 | tf_op jit(solution)/shard_map/ppermute | solution.py:250
  19.4 4.9 %collective-permute-start = (bf16[128,256]{1,0:T(8,128)(2,1)S(1)}, bf16[128,256]{1,0:T(8,128)(2,1)S(1)}, u32[]{:S(2)}, u32[]{:S(2)}) collective-permute-start(bf16[128,256]{1,0:T(8,128)(2,1)S(1)} %bitcast.33), channel_id=1, source_target_pairs={{0,64},{64,128},{128,192},{192,256},{256,320},{320,384},{384,448},... | collective-permute-start | bytes 196616 | tf_op jit(solution)/shard_map/ppermute | solution.py:250
  24.3 0.0 copy-start
  24.3 1.7 %copy-done = bf16[128,9600]{1,0:T(8,128)(2,1)S(1)} copy-done((bf16[128,9600]{1,0:T(8,128)(2,1)S(1)}, bf16[128,9600]{1,0:T(8,128)(2,1)}, u32[]{:S(2)}) %copy-start) | copy-done | bytes 2457624
  26.0 0.0 copy-start.2
  26.0 0.7 copy-done.2
  26.7 3.1 %logit_stats.1 = f32[8,8,128]{2,1,0:T(8,128)} custom-call(s32[1,128]{1,0:T(1,128)S(1)} %bitcast.26, s32[1]{0:T(128)} %bitcast.5.base_ref, bf16[128,9600]{1,0:T(8,128)(2,1)S(1)} %copy-done), custom_call_target="tpu_custom_call" | custom-call | flops 9830400 | bytes 2457600 | tf_op jit(solution)/shard_map/logit_stats/pallas_call | solution.py:53
  29.7 6.7 %all-to-all-start.1 = ((f32[8,8,128]{2,1,0:T(8,128)}), f32[8,8,128]{2,1,0:T(8,128)S(1)}, u32[]{:S(2)}, u32[]{:S(2)}) async-start(f32[8,8,128]{2,1,0:T(8,128)} %logit_stats.1), calls=%async_computation.1 | async-start | bytes 65536 | tf_op jit(solution)/shard_map/all_to_all | solution.py:246
  36.4 0.0 copy-done.1
  36.4 0.1 copy.18
  36.5 0.1 reduce.3
  36.6 0.0 copy-done.6
  36.6 0.1 all_gather_reshape.3
  36.7 0.1 convert_reduce_fusion
  36.8 14.6 %all_gather.6.refs_2_ = bf16[4,128,512]{2,1,0:T(8,128)(2,1)S(1)} all-gather(bf16[1,128,512]{2,1,0:T(8,128)(2,1)S(1)} %all_gather_reshape.3), channel_id=1, replica_groups=mesh['zh'=8,'zl'=2,'yl'=2,'core'=2,'tp'=8] {'zl','yl'}, dimensions={0}, use_global_device_ids=true | all-gather | bytes 655360 | tf_op jit(solution)/shard_map/all_gather | solution.py:242
  51.4 0.0 copy-done.5
  51.4 0.1 pad_add_fusion.refs_1_
  51.5 0.0 all-to-all-done.1
  51.5 0.0 collective-permute-done
  51.6 0.0 collective-permute-done.1
  51.6 6.2 %collective-permute-start.2 = (bf16[384,256]{1,0:T(8,128)(2,1)S(1)}, bf16[384,256]{1,0:T(8,128)(2,1)S(1)}, u32[]{:S(2)}, u32[]{:S(2)}) collective-permute-start(bf16[384,256]{1,0:T(8,128)(2,1)S(1)} %constant_dynamic-update-slice_fusion.refs_3_), channel_id=1, source_target_pairs={{0,8},{8,0},{1,9},{9,1},{2,10},{10,2},{3,11},{11,3},{4,12},{12,4},... | collective-permute-start | bytes 589832 | tf_op jit(solution)/shard_map/ppermute | solution.py:253
  57.8 0.0 copy-start.8
  57.8 0.1 select_reduce_fusion
  57.9 0.6 broadcast_in_dim.30
  58.5 9.0 %all-to-all-start.2 = ((f32[64,1,128]{2,1,0:T(1,128)}), f32[64,1,128]{2,1,0:T(1,128)S(1)}, u32[]{:S(2)}, u32[]{:S(2)}) async-start(f32[64,1,128]{2,1,0:T(1,128)} %broadcast_in_dim.30), calls=%async_computation.2 | async-start | bytes 65536 | tf_op jit(solution)/shard_map/all_to_all | solution.py:228
  67.6 0.0 collective-permute-done.2.refs_4_
  67.6 3.8 %attend.2 = (f32[4,128,512]{2,1,0:T(8,128)S(1)}, f32[4,128,128]{2,1,0:T(8,128)S(1)}) custom-call(s32[16]{0:T(128)S(1)} %copy-done.1, s32[3]{0:T(128)S(1)} %pad_add_fusion.refs_1_, bf16[4,128,512]{2,1,0:T(8,128)(2,1)S(1)} %all_gather.6.refs_2_, bf16[384,256]{1,0:T(8,128)(2,1)S(1)} %constant_dynamic-update-slice_fusion.refs_3_, ...), custom_call_target="tpu_custom_call" | custom-call | flops 1610612736 | bytes 2490368 | tf_op jit(solution)/shard_map/attend/pallas_call | solution.py:180
  71.4 0.0 copy-done.8
  71.4 0.2 all-gather.2.cloned.1.call-done.refs_3_
  71.6 0.0 copy-start.3
  71.6 1.6 %copy-done.3 = bf16[4096,256]{1,0:T(8,128)(2,1)S(1)} copy-done((bf16[4096,256]{1,0:T(8,128)(2,1)S(1)}, bf16[4096,256]{1,0:T(8,128)(2,1)}, u32[]{:S(2)}) %copy-start.3) | copy-done | bytes 2097176
  73.2 0.0 copy-start.7
  73.2 14.6 %attend.3 = bf16[4,128,640]{2,1,0:T(8,128)(2,1)} custom-call(s32[16]{0:T(128)S(1)} %copy-done.1, s32[3]{0:T(128)S(1)} %pad_add_fusion.refs_1_, bf16[4,128,512]{2,1,0:T(8,128)(2,1)S(1)} %all_gather.6.refs_2_, bf16[4096,256]{1,0:T(8,128)(2,1)S(1)} %copy-done.3, f32[4,128,512]{2,1,0:T(8,128)S(1)} %get-tuple-element.5.refs_4_, ...), custom_call_target="tpu_custom_call" | custom-call | flops 8589934592 | bytes 4194304 | tf_op jit(solution)/shard_map/attend/pallas_call | solution.py:180
  87.8 0.0 all-to-all-done.2
  87.8 3.5 %all-to-all-start = ((bf16[4,128,640]{2,1,0:T(8,128)(2,1)}), bf16[4,128,640]{2,1,0:T(8,128)(2,1)S(1)}, u32[]{:S(2)}, u32[]{:S(2)}) async-start(bf16[4,128,640]{2,1,0:T(8,128)(2,1)} %attend.3), calls=%async_computation | async-start | bytes 1310720 | tf_op jit(solution)/shard_map/all_to_all | solution.py:282
  91.3 0.0 copy-done.7
  91.3 0.6 fusion
  92.6 0.5 multiply_divide_fusion
  93.1 7.2 %all-to-all-done.parts_ref = bf16[4,128,640]{2,1,0:T(8,128)(2,1)S(1)} async-done(((bf16[4,128,640]{2,1,0:T(8,128)(2,1)}), bf16[4,128,640]{2,1,0:T(8,128)(2,1)S(1)}, u32[]{:S(2)}, u32[]{:S(2)}) %all-to-all-start) | async-done | bytes 655392 | tf_op jit(solution)/shard_map/all_to_all | solution.py:282
  100.2 0.0 copy-start.4
  100.3 0.8 copy-done.4
  101.1 3.6 %combine.1 = bf16[128,4,128]{2,1,0:T(4,128)(2,1)} custom-call(bf16[4,128,640]{2,1,0:T(8,128)(2,1)} %copy-done.4), custom_call_target="tpu_custom_call" | custom-call | tf_op jit(solution)/shard_map/combine/pallas_call | solution.py:217
  (10 shorter events, 0.2 us)
Async XLA Ops:
  7.2 44.2 %copy-start.5 = (bf16[128,2,1,128]{3,1,2,0:T(2,128)(2,1)S(1)}, bf16[128,2,1,128]{3,1,2,0:T(2,128)(2,1)}, u32[]{:S(2)}) copy-start(bf16[128,2,1,128]{3,1,2,0:T(2,128)(2,1)} %param.9) | copy-start | bytes 196612
  7.2 29.2 %copy-start.1 = (s32[16]{0:T(128)S(1)}, s32[16]{0:T(128)}, u32[]{:S(2)}) copy-start(s32[16]{0:T(128)} %refs_0_.3) | copy-start | bytes 196
  7.2 29.4 %copy-start.6 = (bf16[128,4,128]{2,1,0:T(4,128)(2,1)S(1)}, bf16[128,4,128]{2,1,0:T(4,128)(2,1)}, u32[]{:S(2)}) copy-start(bf16[128,4,128]{2,1,0:T(4,128)(2,1)} %param.7) | copy-start | bytes 393220
  7.2 64.4 %all-gather.2.cloned.1.call-start = ((), (), s32[]{:S(2)}) async-start(), calls=%async_computation.3 | async-start | bytes 2228224 | tf_op jit(solution)/shard_map/all_gather | solution.py:241
  9.7 41.8 %collective-permute-start.1 = (bf16[128,256]{1,0:T(8,128)(2,1)S(1)}, bf16[128,256]{1,0:T(8,128)(2,1)S(1)}, u32[]{:S(2)}, u32[]{:S(2)}) collective-permute-start(bf16[128,256]{1,0:T(8,128)(2,1)S(1)} %bitcast.32), channel_id=1, source_target_pairs={{0,128},{64,192},{128,256},{192,320},{256,384},{320,448},{384,0},{... | collective-permute-start | bytes 196616 | tf_op jit(solution)/shard_map/ppermute | solution.py:250
  19.4 32.1 %collective-permute-start = (bf16[128,256]{1,0:T(8,128)(2,1)S(1)}, bf16[128,256]{1,0:T(8,128)(2,1)S(1)}, u32[]{:S(2)}, u32[]{:S(2)}) collective-permute-start(bf16[128,256]{1,0:T(8,128)(2,1)S(1)} %bitcast.33), channel_id=1, source_target_pairs={{0,64},{64,128},{128,192},{192,256},{256,320},{320,384},{384,448},... | collective-permute-start | bytes 196616 | tf_op jit(solution)/shard_map/ppermute | solution.py:250
  24.3 1.7 %copy-start = (bf16[128,9600]{1,0:T(8,128)(2,1)S(1)}, bf16[128,9600]{1,0:T(8,128)(2,1)}, u32[]{:S(2)}) copy-start(bf16[128,9600]{1,0:T(8,128)(2,1)} %logits_ref.1) | copy-start | bytes 7372804
  26.0 0.7 copy-start.2
  29.7 21.7 %all-to-all-start.1 = ((f32[8,8,128]{2,1,0:T(8,128)}), f32[8,8,128]{2,1,0:T(8,128)S(1)}, u32[]{:S(2)}, u32[]{:S(2)}) async-start(f32[8,8,128]{2,1,0:T(8,128)} %logit_stats.1), calls=%async_computation.1 | async-start | bytes 65536 | tf_op jit(solution)/shard_map/all_to_all | solution.py:246
  51.6 16.0 %collective-permute-start.2 = (bf16[384,256]{1,0:T(8,128)(2,1)S(1)}, bf16[384,256]{1,0:T(8,128)(2,1)S(1)}, u32[]{:S(2)}, u32[]{:S(2)}) collective-permute-start(bf16[384,256]{1,0:T(8,128)(2,1)S(1)} %constant_dynamic-update-slice_fusion.refs_3_), channel_id=1, source_target_pairs={{0,8},{8,0},{1,9},{9,1},{2,10},{10,2},{3,11},{11,3},{4,12},{12,4},... | collective-permute-start | bytes 589832 | tf_op jit(solution)/shard_map/ppermute | solution.py:253
  57.8 13.6 %copy-start.8 = (f32[128]{0:T(128)}, f32[128]{0:T(128)S(1)}, u32[]{:S(2)}) copy-start(f32[128]{0:T(128)S(1)} %compare_select_fusion) | copy-start | bytes 1540
  58.5 29.3 %all-to-all-start.2 = ((f32[64,1,128]{2,1,0:T(1,128)}), f32[64,1,128]{2,1,0:T(1,128)S(1)}, u32[]{:S(2)}, u32[]{:S(2)}) async-start(f32[64,1,128]{2,1,0:T(1,128)} %broadcast_in_dim.30), calls=%async_computation.2 | async-start | bytes 65536 | tf_op jit(solution)/shard_map/all_to_all | solution.py:228
  71.6 1.6 %copy-start.3 = (bf16[4096,256]{1,0:T(8,128)(2,1)S(1)}, bf16[4096,256]{1,0:T(8,128)(2,1)}, u32[]{:S(2)}) copy-start(bf16[4096,256]{1,0:T(8,128)(2,1)} %all-gather.2.cloned.1.call-done.refs_3_) | copy-start | bytes 6291460
  73.2 18.1 %copy-start.7 = (f32[16]{0:T(128)S(1)}, f32[16]{0:T(128)}, u32[]{:S(2)}) copy-start(f32[16]{0:T(128)} %param.13) | copy-start | bytes 196
  87.8 12.5 %all-to-all-start = ((bf16[4,128,640]{2,1,0:T(8,128)(2,1)}), bf16[4,128,640]{2,1,0:T(8,128)(2,1)S(1)}, u32[]{:S(2)}, u32[]{:S(2)}) async-start(bf16[4,128,640]{2,1,0:T(8,128)(2,1)} %attend.3), calls=%async_computation | async-start | bytes 1310720 | tf_op jit(solution)/shard_map/all_to_all | solution.py:282
  100.2 0.8 copy-start.4
Sparse Core Ops, SparseCore 0:
  10.7 60.8 all-gather.1

commit v5 on v4

--- a/solution.py
+++ b/solution.py
@@ -13,6 +13,7 @@
 ROWS_DEV = 128
 PLANE = 4
 TILE = 512
+CHUNK = 512
 SCALE = 1.0 / math.sqrt(HD)
 LOG2E = 1.4426950408889634
 Z = ("zh", "zl")
@@ -191,6 +192,88 @@
     )(lengths, place, q, *blocks, *state)
 
 
+def finish_kernel(
+    place_ref, q_ref, prompt_ref, acc_ref, stat_ref, out_ref, key_ref, value_ref, sems
+):
+    chunks = key_ref.shape[0] // CHUNK
+    half = -(-chunks // 2)
+    copies = []
+    for i in range(chunks):
+        source = pl.ds(pl.multiple_of(lax.rem(place_ref[3] + 1 + i, chunks + 1) * CHUNK, CHUNK), CHUNK)
+        target = pl.ds(i * CHUNK, CHUNK)
+        copies.append(
+            (
+                pltpu.make_async_copy(
+                    prompt_ref.at[source, pl.ds(0, HD)], key_ref.at[target, :], sems.at[2 * i]
+                ),
+                pltpu.make_async_copy(
+                    prompt_ref.at[source, pl.ds(HD, HD)],
+                    value_ref.at[target, pl.ds(0, HD)],
+                    sems.at[2 * i + 1],
+                ),
+            )
+        )
+    for key_copy, value_copy in copies:
+        key_copy.start()
+        value_copy.start()
+    value_ref[:, HD:] = jnp.ones((value_ref.shape[0], HD), jnp.bfloat16)
+    lane = lax.broadcasted_iota(jnp.int32, (TILE, HD), 1)
+    stat = stat_ref[...].reshape(TILE, HD)
+    packed = jnp.zeros((TILE, HD), jnp.float32)
+    for pair_copies in copies:
+        for copy in pair_copies:
+            copy.wait()
+    for h in range(HEADS):
+        lanes = slice(h * HD, (h + 1) * HD)
+        q = q_ref[:, :, lanes].reshape(TILE, HD)
+        m = stat[:, h : h + 1]
+        weighted = acc_ref[:, :, lanes].reshape(TILE, HD)
+        denominator = stat[:, HEADS + h : HEADS + h + 1]
+        for low, high in ((0, half * CHUNK), (half * CHUNK, chunks * CHUNK)):
+            s = nt(q, key_ref[low:high, :])
+            raised = jnp.maximum(m, jnp.max(s, axis=1, keepdims=True))
+            shrink = jnp.exp2((m - raised) * (SCALE * LOG2E))
+            p = jnp.exp2((s - raised) * (SCALE * LOG2E)).astype(jnp.bfloat16)
+            acc = jnp.dot(p, value_ref[low:high, :], preferred_element_type=jnp.float32)
+            weighted = weighted * shrink + acc[:, :HD]
+            denominator = denominator * shrink + acc[:, HD:]
+            m = raised
+        out_ref[:, :, lanes] = (
+            (weighted / denominator).astype(jnp.bfloat16).reshape(PLANE, ROWS_DEV, HD)
+        )
+        lse = m * SCALE + jnp.log(denominator)
+        high_part = lse.astype(jnp.bfloat16).astype(jnp.float32)
+        middle = (lse - high_part).astype(jnp.bfloat16).astype(jnp.float32)
+        low_part = lse - high_part - middle
+        packed = jnp.where(lane == 3 * h, high_part, packed)
+        packed = jnp.where(lane == 3 * h + 1, middle, packed)
+        packed = jnp.where(lane == 3 * h + 2, low_part, packed)
+    out_ref[:, :, HEADS * HD :] = packed.astype(jnp.bfloat16).reshape(PLANE, ROWS_DEV, HD)
+
+
+def finish(place, q, prompt, state):
+    vmem = pl.BlockSpec(memory_space=pltpu.VMEM)
+    smem = pl.BlockSpec(memory_space=pltpu.SMEM)
+    keys = prompt.shape[0] - CHUNK
+    pairs = PLANE * ROWS_DEV * HEADS * keys
+    return pl.pallas_call(
+        finish_kernel,
+        in_specs=[smem, vmem, pl.BlockSpec(memory_space=pltpu.HBM), vmem, vmem],
+        out_specs=vmem,
+        out_shape=jax.ShapeDtypeStruct((PLANE, ROWS_DEV, HEADS * HD + HD), jnp.bfloat16),
+        scratch_shapes=[
+            pltpu.VMEM((keys, HD), jnp.bfloat16),
+            pltpu.VMEM((keys, 2 * HD), jnp.bfloat16),
+            pltpu.SemaphoreType.DMA((2 * (keys // CHUNK),)),
+        ],
+        compiler_params=pltpu.CompilerParams(vmem_limit_bytes=61 * MIB),
+        cost_estimate=pl.CostEstimate(
+            flops=8 * HD * pairs, bytes_accessed=512 * keys + 2 * MIB, transcendentals=pairs
+        ),
+        name="finish",
+    )(place, q, prompt, *state)
+
+
 def combine_kernel(parts_ref, out_ref):
     tops = []
     for j in range(PLANE):
@@ -213,7 +296,7 @@
 
 
 def combine(parts):
-    rows = 32
+    rows = 64
     return pl.pallas_call(
         combine_kernel,
         grid=(ROWS_DEV // rows,),
@@ -238,8 +321,9 @@
     pb = prompt_kv.shape[0]
     rb = response_kv.shape[0]
 
-    prompt = lax.all_gather(prompt_kv.reshape(pb, 2 * HD), ("zh", "core"), axis=0, tiled=True)
-    q = lax.all_gather(queries.reshape(ROWS_DEV, HEADS * HD), SHARE, axis=0)
+    own_prompt = prompt_kv.reshape(pb, 2 * HD)
+    prompt = lax.all_gather(own_prompt, ("zh", "core"), axis=0, tiled=True)
+    q = to_all(queries.reshape(ROWS_DEV, HEADS * HD), SHARE, PLANE)
 
     vocab_base = (lax.axis_index("tp") * logits.shape[1]).astype(jnp.int32).reshape(1)
     stats = logit_stats(logits, token_ids, vocab_base, lax.axis_size("tp"))
@@ -249,7 +333,7 @@
     before = [
         lax.ppermute(own, "zh", [(i, (i + d) % pairs) for i in range(pairs)]) for d in (1, 2)
     ]
-    mine = jnp.concatenate([own] + before, axis=0)
+    mine = jnp.concatenate([own_prompt, own] + before, axis=0)
     other = lax.ppermute(mine, "core", [(0, 1), (1, 0)])
 
     peaks, sums, picks = stats[:, 0], stats[:, 1], stats[:, 2]
@@ -272,13 +356,11 @@
 
     first_row = (pair * 2 * PLANE + core) * ROWS_DEV
     place = jnp.stack(
-        [first_row, (block + core) * ROWS_DEV, (block + 1 - core) * ROWS_DEV]
+        [first_row, (block + core) * ROWS_DEV, (block + 1 - core) * ROWS_DEV, pair]
     ).astype(jnp.int32)
-    masked = ((0, 3 * rb, True),)
-    state = attend(lengths, place, q, [mine, other], [masked, masked], (), False)
-    half = prompt.shape[0] // 2
-    spans = ((0, half, False), (half, 2 * half, False))
-    partial = attend(lengths, place, q, [prompt], [spans], state, True)
+    spans = ((0, pb, False), (pb, pb + 3 * rb, True))
+    state = attend(lengths, place, q, [mine, other], [spans, spans], (), False)
+    partial = finish(place, q, prompt, state)
     exchanged = lax.all_to_all(partial, SHARE, 0, 0)
     context = combine(exchanged)
     return (context, token_logprob, response_objective)

time: 113 us -> 121 us (1.071)
  blocking collectives: 14.6 us -> 0 us
  waiting for transfers between devices: 7.39 us -> 21.2 us
  starting transfers between devices: 39.9 us -> 48.3 us
    pallas_call x0 -> x1, Pallas kernels: none -> 15.1 us  [finish(): pl.pallas_call(finish_kernel, in_specs=[smem, vmem, pl.BlockSpec(memory_s...]
    all_gather x1 -> x0, blocking collectives: 14.6 us -> none  [shards(): q = lax.all_gather(queries.reshape(ROWS_DEV, HEADS * HD), SHARE, axis=0)]
    pallas_call x2 -> x1, Pallas kernels: 18.4 us -> 5.05 us  [attend(): pl.pallas_call(functools.partial(attend_kernel, pieces, not state, last),...]
    all_to_all x1 -> x2, starting transfers between devices: 9.03 us -> 18.9 us  [to_all(): lax.all_to_all(jnp.broadcast_to(x[None], (count,) + x.shape), axes, 0, 0)]
    all_to_all x1 -> x2, waiting for transfers between devices: 0.01 us -> 7.7 us  [to_all(): lax.all_to_all(jnp.broadcast_to(x[None], (count,) + x.shape), axes, 0, 0)]
    all_to_all x1, waiting for transfers between devices: 0.01 us -> 6.31 us  [shards(): stats = lax.all_to_all(stats, 'tp', 0, 0)]
    ppermute x1, starting transfers between devices: 6.18 us -> 4.57 us  [shards(): other = lax.ppermute(mine, 'core', [(0, 1), (1, 0)])]
    pallas_call x1, Pallas kernels: 3.64 us -> 2.41 us  [combine(): pl.pallas_call(combine_kernel, grid=(ROWS_DEV // rows,), in_specs=[pl.Blo...]
  transfers between devices with their start and end apart: 7 -> 8, of which waited for: 2 -> 3; matrix products, arithmetic and copies ran while one was open for 3% -> 3% of each run, Pallas kernels for 19% -> 19%
where the time goes in v5:
time: 121 us
  starting transfers between devices  48.3 us (40%)
  Pallas kernels  25.6 us (21%)
  waiting for transfers between devices  21.2 us (18%)
  between operations  14.9 us (12%)
  local copies, waits for them, and re-layouts  9.05 us (7%)
  other arithmetic  1.67 us (1%)
    all_to_all x2, starting transfers between devices, to_all(): lax.all_to_all(jnp.broadcast_to(x[None], (count,) + x.shape), axes, 0, 0)  18.9 us
    pallas_call x1, Pallas kernels, finish(): pl.pallas_call(finish_kernel, in_specs=[smem, vmem, pl.BlockSpec(memory_s...  15.1 us
    ppermute x2, starting transfers between devices, shards(): lax.ppermute(own, 'zh', [(i, (i + d) % pairs) for i in range(pairs)])  14.5 us
    all_to_all x2, waiting for transfers between devices, to_all(): lax.all_to_all(jnp.broadcast_to(x[None], (count,) + x.shape), axes, 0, 0)  7.7 us
    unnamed x32, local copies, waits for them, and re-layouts  7.47 us
    all_to_all x1, waiting for transfers between devices, shards(): exchanged = lax.all_to_all(partial, SHARE, 0, 0)  7.12 us
    all_to_all x1, starting transfers between devices, shards(): stats = lax.all_to_all(stats, 'tp', 0, 0)  6.65 us
    all_to_all x1, waiting for transfers between devices, shards(): stats = lax.all_to_all(stats, 'tp', 0, 0)  6.31 us
  transfers between devices with their start and end apart: 8, of which 3 were waited for; matrix products, arithmetic and copies ran while one was open for 3% of the time, Pallas kernels for 19%

profile of v5, /device:TPU:1, one launch (start us, length us, event | category | flops | bytes accessed | tf_op | source)
XLA Modules:
  0.0 120.7 jit_solution(12327607743179567494)
XLA Ops:
  7.2 0.0 copy-start.10
  7.2 0.0 copy-start.2
  7.2 0.0 all-gather.2.cloned.1.call-start
  7.2 1.6 %copy.30 = bf16[32,8,2,128]{3,1,2,0:T(8,128)(2,1)} copy(bf16[32,8,2,128]{3,2,1,0:T(2,128)(2,1)} %bitcast.35) | data formatting | bytes 262144
  8.8 0.0 copy-start.8
  8.8 0.0 all-gather.2.cloned.1.call-update
  8.8 0.0 copy-start.9
  8.9 0.9 copy.32
  9.8 5.7 %collective-permute-start = (bf16[128,256]{1,0:T(8,128)(2,1)S(1)}, bf16[128,256]{1,0:T(8,128)(2,1)S(1)}, u32[]{:S(2)}, u32[]{:S(2)}) collective-permute-start(bf16[128,256]{1,0:T(8,128)(2,1)S(1)} %bitcast.42), channel_id=1, source_target_pairs={{0,64},{64,128},{128,192},{192,256},{256,320},{320,384},{384,448},... | collective-permute-start | bytes 196616 | tf_op jit(solution)/shard_map/ppermute | solution.py:334
  15.5 8.8 %collective-permute-start.1 = (bf16[128,256]{1,0:T(8,128)(2,1)S(1)}, bf16[128,256]{1,0:T(8,128)(2,1)S(1)}, u32[]{:S(2)}, u32[]{:S(2)}) collective-permute-start(bf16[128,256]{1,0:T(8,128)(2,1)S(1)} %bitcast.43), channel_id=1, source_target_pairs={{0,128},{64,192},{128,256},{192,320},{256,384},{320,448},{384,0},{... | collective-permute-start | bytes 196616 | tf_op jit(solution)/shard_map/ppermute | solution.py:334
  24.3 0.0 copy-start
  24.4 1.7 %copy-done = bf16[128,9600]{1,0:T(8,128)(2,1)S(1)} copy-done((bf16[128,9600]{1,0:T(8,128)(2,1)S(1)}, bf16[128,9600]{1,0:T(8,128)(2,1)}, u32[]{:S(2)}) %copy-start) | copy-done | bytes 2457624
  26.0 0.0 copy-start.3
  26.0 0.7 copy-done.3
  26.7 3.1 %logit_stats.1 = f32[8,8,128]{2,1,0:T(8,128)} custom-call(s32[1,128]{1,0:T(1,128)S(1)} %bitcast.33, s32[1]{0:T(128)} %bitcast.6.base_ref, bf16[128,9600]{1,0:T(8,128)(2,1)S(1)} %copy-done), custom_call_target="tpu_custom_call" | custom-call | flops 9830400 | bytes 2457600 | tf_op jit(solution)/shard_map/logit_stats/pallas_call | solution.py:54
  29.8 6.7 %all-to-all-start.2 = ((f32[8,8,128]{2,1,0:T(8,128)}), f32[8,8,128]{2,1,0:T(8,128)S(1)}, u32[]{:S(2)}, u32[]{:S(2)}) async-start(f32[8,8,128]{2,1,0:T(8,128)} %logit_stats.1), calls=%async_computation.2 | async-start | bytes 65536 | tf_op jit(solution)/shard_map/all_to_all | solution.py:330
  36.4 0.0 copy-done.10
  36.5 0.0 copy-done.2
  36.5 0.1 copy.16
  36.6 0.1 reduce.3
  36.7 6.3 %all-to-all-done.2 = f32[8,8,128]{2,1,0:T(8,128)S(1)} async-done(((f32[8,8,128]{2,1,0:T(8,128)}), f32[8,8,128]{2,1,0:T(8,128)S(1)}, u32[]{:S(2)}, u32[]{:S(2)}) %all-to-all-start.2) | async-done | bytes 32800 | tf_op jit(solution)/shard_map/all_to_all | solution.py:330
  43.0 0.8 broadcast_in_dim.35
  43.9 3.5 %all-to-all-start = ((bf16[4,128,512]{2,1,0:T(8,128)(2,1)}), bf16[4,128,512]{2,1,0:T(8,128)(2,1)S(1)}, u32[]{:S(2)}, u32[]{:S(2)}) async-start(bf16[4,128,512]{2,1,0:T(8,128)(2,1)} %broadcast_in_dim.35), calls=%async_computation | async-start | bytes 1048576 | tf_op jit(solution)/shard_map/all_to_all | solution.py:311
  47.3 0.1 pad_add_fusion.refs_1_.place_ref
  47.4 0.0 copy-start.4
  47.4 0.1 convert_reduce_fusion
  47.5 0.0 copy-done.8
  47.5 0.0 copy-done.9
  47.6 0.0 collective-permute-done
  47.6 0.0 collective-permute-done.1
  47.7 4.6 %collective-permute-start.2 = (bf16[640,256]{1,0:T(8,128)(2,1)S(1)}, bf16[640,256]{1,0:T(8,128)(2,1)S(1)}, u32[]{:S(2)}, u32[]{:S(2)}) collective-permute-start(bf16[640,256]{1,0:T(8,128)(2,1)S(1)} %constant_dynamic-update-slice_fusion.refs_3_), channel_id=1, source_target_pairs={{0,8},{8,0},{1,9},{9,1},{2,10},{10,2},{3,11},{11,3},{4,12},{12,4},... | collective-permute-start | bytes 983048 | tf_op jit(solution)/shard_map/ppermute | solution.py:337
  52.3 0.0 copy-start.12
  52.3 0.1 select_reduce_fusion
  52.4 7.7 %all-to-all-done.refs_2_.q_ref = bf16[4,128,512]{2,1,0:T(8,128)(2,1)S(1)} async-done(((bf16[4,128,512]{2,1,0:T(8,128)(2,1)}), bf16[4,128,512]{2,1,0:T(8,128)(2,1)S(1)}, u32[]{:S(2)}, u32[]{:S(2)}) %all-to-all-start) | async-done | bytes 524320 | tf_op jit(solution)/shard_map/all_to_all | solution.py:311
  60.1 0.0 copy-start.1
  60.1 0.7 broadcast_in_dim.39
  60.8 15.4 %all-to-all-start.3 = ((f32[64,1,128]{2,1,0:T(1,128)}), f32[64,1,128]{2,1,0:T(1,128)S(1)}, u32[]{:S(2)}, u32[]{:S(2)}) async-start(f32[64,1,128]{2,1,0:T(1,128)} %broadcast_in_dim.39), calls=%async_computation.3 | async-start | bytes 65536 | tf_op jit(solution)/shard_map/all_to_all | solution.py:311
  76.2 0.0 collective-permute-done.2.refs_4_
  76.2 5.0 %attend.1 = (f32[4,128,512]{2,1,0:T(8,128)S(1)}, f32[4,128,128]{2,1,0:T(8,128)S(1)}) custom-call(s32[16]{0:T(128)S(1)} %copy-done.2, s32[4]{0:T(128)S(1)} %pad_add_fusion.refs_1_.place_ref, bf16[4,128,512]{2,1,0:T(8,128)(2,1)S(1)} %all-to-all-done.refs_2_.q_ref, bf16[640,256]{1,0:T(8,128)(2,1)S(1)} %constant_dynamic-update-slice_fusion.refs_3_, ...), custom_call_target="tpu_custom_call" | custom-call | flops 2684354560 | bytes 2752512 | tf_op jit(solution)/shard_map/attend/pallas_call | solution.py:181
  81.3 0.0 copy-done.4
  81.3 0.0 copy-done.12
  81.3 0.0 copy-done.1
  81.3 0.0 copy-start.5
  81.3 1.0 copy-done.5
  82.3 0.0 copy-start.6
  82.3 0.7 copy-done.6
  83.0 0.0 all-gather.2.cloned.1.call-done.prompt_ref
  83.0 0.0 copy-start.11
  83.0 15.1 %finish.1 = bf16[4,128,640]{2,1,0:T(8,128)(2,1)} custom-call(s32[4]{0:T(128)} %copy-done.4, bf16[4,128,512]{2,1,0:T(8,128)(2,1)} %copy-done.1, bf16[4096,256]{1,0:T(8,128)(2,1)} %all-gather.2.cloned.1.call-done.prompt_ref, f32[4,128,512]{2,1,0:T(8,128)} %copy-done.5, f32[4,128,128]{2,1,0:T(8,128)} %copy-done.6), custom_call_target="tpu_custom_call" | custom-call | flops 7516192768 | bytes 3932160 | tf_op jit(solution)/shard_map/finish/pallas_call | solution.py:259
  98.1 0.0 all-to-all-done.3
  98.1 3.6 %all-to-all-start.1 = ((bf16[4,128,640]{2,1,0:T(8,128)(2,1)}), bf16[4,128,640]{2,1,0:T(8,128)(2,1)S(1)}, u32[]{:S(2)}, u32[]{:S(2)}) async-start(bf16[4,128,640]{2,1,0:T(8,128)(2,1)} %finish.1), calls=%async_computation.1 | async-start | bytes 1310720 | tf_op jit(solution)/shard_map/all_to_all | solution.py:364
  101.7 0.0 copy-done.11
  101.7 0.6 fusion
  103.0 0.5 multiply_divide_fusion
  103.5 7.1 %all-to-all-done.1.parts_ref = bf16[4,128,640]{2,1,0:T(8,128)(2,1)S(1)} async-done(((bf16[4,128,640]{2,1,0:T(8,128)(2,1)}), bf16[4,128,640]{2,1,0:T(8,128)(2,1)S(1)}, u32[]{:S(2)}, u32[]{:S(2)}) %all-to-all-start.1) | async-done | bytes 655392 | tf_op jit(solution)/shard_map/all_to_all | solution.py:364
  110.6 0.0 copy-start.7
  110.6 0.8 copy-done.7
  111.5 2.4 %combine.1 = bf16[128,4,128]{2,1,0:T(4,128)(2,1)} custom-call(bf16[4,128,640]{2,1,0:T(8,128)(2,1)} %copy-done.7), custom_call_target="tpu_custom_call" | custom-call | tf_op jit(solution)/shard_map/combine/pallas_call | solution.py:300
  (12 shorter events, 0.2 us)
Async XLA Ops:
  7.2 29.3 %copy-start.10 = (bf16[128,4,128]{2,1,0:T(4,128)(2,1)S(1)}, bf16[128,4,128]{2,1,0:T(4,128)(2,1)}, u32[]{:S(2)}) copy-start(bf16[128,4,128]{2,1,0:T(4,128)(2,1)} %param.7) | copy-start | bytes 393220
  7.2 29.3 %copy-start.2 = (s32[16]{0:T(128)S(1)}, s32[16]{0:T(128)}, u32[]{:S(2)}) copy-start(s32[16]{0:T(128)} %refs_0_.1) | copy-start | bytes 196
  7.2 75.8 %all-gather.2.cloned.1.call-start = ((), (), s32[]{:S(2)}) async-start(), calls=%async_computation.4 | async-start | bytes 2228224 | tf_op jit(solution)/shard_map/all_gather | solution.py:325
  8.8 38.7 %copy-start.8 = (bf16[256,2,1,128]{3,1,2,0:T(2,128)(2,1)S(1)}, bf16[256,2,1,128]{3,1,2,0:T(2,128)(2,1)}, u32[]{:S(2)}) copy-start(bf16[256,2,1,128]{3,1,2,0:T(2,128)(2,1)} %param.8) | copy-start | bytes 393220
  8.8 38.7 %copy-start.9 = (bf16[128,2,1,128]{3,1,2,0:T(2,128)(2,1)S(1)}, bf16[128,2,1,128]{3,1,2,0:T(2,128)(2,1)}, u32[]{:S(2)}) copy-start(bf16[128,2,1,128]{3,1,2,0:T(2,128)(2,1)} %param.9) | copy-start | bytes 196612
  9.8 37.9 %collective-permute-start = (bf16[128,256]{1,0:T(8,128)(2,1)S(1)}, bf16[128,256]{1,0:T(8,128)(2,1)S(1)}, u32[]{:S(2)}, u32[]{:S(2)}) collective-permute-start(bf16[128,256]{1,0:T(8,128)(2,1)S(1)} %bitcast.42), channel_id=1, source_target_pairs={{0,64},{64,128},{128,192},{192,256},{256,320},{320,384},{384,448},... | collective-permute-start | bytes 196616 | tf_op jit(solution)/shard_map/ppermute | solution.py:334
  15.5 32.1 %collective-permute-start.1 = (bf16[128,256]{1,0:T(8,128)(2,1)S(1)}, bf16[128,256]{1,0:T(8,128)(2,1)S(1)}, u32[]{:S(2)}, u32[]{:S(2)}) collective-permute-start(bf16[128,256]{1,0:T(8,128)(2,1)S(1)} %bitcast.43), channel_id=1, source_target_pairs={{0,128},{64,192},{128,256},{192,320},{256,384},{320,448},{384,0},{... | collective-permute-start | bytes 196616 | tf_op jit(solution)/shard_map/ppermute | solution.py:334
  24.3 1.7 %copy-start = (bf16[128,9600]{1,0:T(8,128)(2,1)S(1)}, bf16[128,9600]{1,0:T(8,128)(2,1)}, u32[]{:S(2)}) copy-start(bf16[128,9600]{1,0:T(8,128)(2,1)} %logits_ref.1) | copy-start | bytes 7372804
  26.0 0.7 copy-start.3
  29.8 13.3 %all-to-all-start.2 = ((f32[8,8,128]{2,1,0:T(8,128)}), f32[8,8,128]{2,1,0:T(8,128)S(1)}, u32[]{:S(2)}, u32[]{:S(2)}) async-start(f32[8,8,128]{2,1,0:T(8,128)} %logit_stats.1), calls=%async_computation.2 | async-start | bytes 65536 | tf_op jit(solution)/shard_map/all_to_all | solution.py:330
  43.9 16.2 %all-to-all-start = ((bf16[4,128,512]{2,1,0:T(8,128)(2,1)}), bf16[4,128,512]{2,1,0:T(8,128)(2,1)S(1)}, u32[]{:S(2)}, u32[]{:S(2)}) async-start(bf16[4,128,512]{2,1,0:T(8,128)(2,1)} %broadcast_in_dim.35), calls=%async_computation | async-start | bytes 1048576 | tf_op jit(solution)/shard_map/all_to_all | solution.py:311
  47.4 33.9 %copy-start.4 = (s32[4]{0:T(128)}, s32[4]{0:T(128)S(1)}, u32[]{:S(2)}) copy-start(s32[4]{0:T(128)S(1)} %pad_add_fusion.refs_1_.place_ref) | copy-start | bytes 52
  47.7 28.5 %collective-permute-start.2 = (bf16[640,256]{1,0:T(8,128)(2,1)S(1)}, bf16[640,256]{1,0:T(8,128)(2,1)S(1)}, u32[]{:S(2)}, u32[]{:S(2)}) collective-permute-start(bf16[640,256]{1,0:T(8,128)(2,1)S(1)} %constant_dynamic-update-slice_fusion.refs_3_), channel_id=1, source_target_pairs={{0,8},{8,0},{1,9},{9,1},{2,10},{10,2},{3,11},{11,3},{4,12},{12,4},... | collective-permute-start | bytes 983048 | tf_op jit(solution)/shard_map/ppermute | solution.py:337
  52.3 29.0 %copy-start.12 = (f32[128]{0:T(128)}, f32[128]{0:T(128)S(1)}, u32[]{:S(2)}) copy-start(f32[128]{0:T(128)S(1)} %compare_select_fusion) | copy-start | bytes 1540
  60.1 21.2 %copy-start.1 = (bf16[4,128,512]{2,1,0:T(8,128)(2,1)}, bf16[4,128,512]{2,1,0:T(8,128)(2,1)S(1)}, u32[]{:S(2)}) copy-start(bf16[4,128,512]{2,1,0:T(8,128)(2,1)S(1)} %all-to-all-done.refs_2_.q_ref) | copy-start | bytes 1572868
  60.8 37.4 %all-to-all-start.3 = ((f32[64,1,128]{2,1,0:T(1,128)}), f32[64,1,128]{2,1,0:T(1,128)S(1)}, u32[]{:S(2)}, u32[]{:S(2)}) async-start(f32[64,1,128]{2,1,0:T(1,128)} %broadcast_in_dim.39), calls=%async_computation.3 | async-start | bytes 65536 | tf_op jit(solution)/shard_map/all_to_all | solution.py:311
  81.3 1.0 copy-start.5
  82.3 0.7 copy-start.6
  83.0 18.7 %copy-start.11 = (f32[16]{0:T(128)S(1)}, f32[16]{0:T(128)}, u32[]{:S(2)}) copy-start(f32[16]{0:T(128)} %param.13) | copy-start | bytes 196
  98.1 12.5 %all-to-all-start.1 = ((bf16[4,128,640]{2,1,0:T(8,128)(2,1)}), bf16[4,128,640]{2,1,0:T(8,128)(2,1)S(1)}, u32[]{:S(2)}, u32[]{:S(2)}) async-start(bf16[4,128,640]{2,1,0:T(8,128)(2,1)} %finish.1), calls=%async_computation.1 | async-start | bytes 1310720 | tf_op jit(solution)/shard_map/all_to_all | solution.py:364
  110.6 0.8 copy-start.7
Sparse Core Ops, SparseCore 0:
  10.7 61.6 all-gather.1

commit v6 on v4

--- a/solution.py
+++ b/solution.py
@@ -111,8 +111,14 @@
         for h in range(HEADS):
             lanes = slice(h * HD, (h + 1) * HD)
             q = q_ref[devs, :, lanes].reshape(TILE, HD)
-            tops = [] if first else [stat[:, h : h + 1]]
-            scores = []
+            if first:
+                m = jnp.full((TILE, 1), -1e30, jnp.float32)
+                weighted = jnp.zeros((TILE, HD), jnp.float32)
+                denominator = jnp.zeros((TILE, HD), jnp.float32)
+            else:
+                m = stat[:, h : h + 1]
+                weighted = acc_in[devs, :, lanes].reshape(TILE, HD)
+                denominator = stat[:, HEADS + h : HEADS + h + 1]
             answer = 0
             for kv_ref, v_ref, spans in zip(kv_refs, v_refs, pieces):
                 for low, high, masked in spans:
@@ -123,20 +129,13 @@
                         keys = place_ref[answer] + column % ROWS_DEV
                         keys = keys - column // ROWS_DEV * (2 * PLANE * ROWS_DEV)
                         s = jnp.where((keys >= start) & (keys <= rows), s, -1e30)
-                    tops.append(jnp.max(s, axis=1, keepdims=True))
-                    scores.append((s, v_ref, low, high))
-            m = tops[0]
-            for top in tops[1:]:
-                m = jnp.maximum(m, top)
-            acc = 0.0
-            for s, v_ref, low, high in scores:
-                p = jnp.exp2((s - m) * (SCALE * LOG2E)).astype(jnp.bfloat16)
-                acc = acc + jnp.dot(p, v_ref[low:high, :], preferred_element_type=jnp.float32)
-            weighted, denominator = acc[:, :HD], acc[:, HD:]
-            if not first:
-                shrink = jnp.exp2((tops[0] - m) * (SCALE * LOG2E))
-                weighted = weighted + shrink * acc_in[devs, :, lanes].reshape(TILE, HD)
-                denominator = denominator + shrink * stat[:, HEADS + h : HEADS + h + 1]
+                    raised = jnp.maximum(m, jnp.max(s, axis=1, keepdims=True))
+                    shrink = jnp.exp2((m - raised) * (SCALE * LOG2E))
+                    p = jnp.exp2((s - raised) * (SCALE * LOG2E)).astype(jnp.bfloat16)
+                    acc = jnp.dot(p, v_ref[low:high, :], preferred_element_type=jnp.float32)
+                    weighted = weighted * shrink + acc[:, :HD]
+                    denominator = denominator * shrink + acc[:, HD:]
+                    m = raised
             if last:
                 out_ref[devs, :, lanes] = (
                     (weighted / denominator).astype(jnp.bfloat16).reshape(per, ROWS_DEV, HD)
@@ -213,7 +212,7 @@
 
 
 def combine(parts):
-    rows = 32
+    rows = 64
     return pl.pallas_call(
         combine_kernel,
         grid=(ROWS_DEV // rows,),
@@ -239,10 +238,11 @@
     rb = response_kv.shape[0]
 
     prompt = lax.all_gather(prompt_kv.reshape(pb, 2 * HD), ("zh", "core"), axis=0, tiled=True)
-    q = lax.all_gather(queries.reshape(ROWS_DEV, HEADS * HD), SHARE, axis=0)
+    q = to_all(queries.reshape(ROWS_DEV, HEADS * HD), SHARE, PLANE)
 
     vocab_base = (lax.axis_index("tp") * logits.shape[1]).astype(jnp.int32).reshape(1)
     stats = logit_stats(logits, token_ids, vocab_base, lax.axis_size("tp"))
+    stats, q = lax.optimization_barrier((stats, q))
     stats = lax.all_to_all(stats, "tp", 0, 0)
 
     own = response_kv.reshape(rb, 2 * HD)
@@ -263,12 +263,7 @@
     token_logprob = jnp.where(segment < responses, logprob, 0.0)
     members = segment[:, None] == jnp.arange(128, dtype=jnp.int32)[None, :]
     part = jnp.sum(jnp.where(members, token_logprob[:, None], 0.0), axis=0)
-    part = jnp.sum(to_all(part[None], CTX, 64)[:, 0], axis=0)
-    response_sum = part[:responses]
-    length_float = lengths.astype(jnp.float32)
-    adjusted = rewards - 0.5 * length_float / 2048
-    advantage = adjusted - jnp.mean(adjusted)
-    response_objective = -advantage * response_sum / length_float
+    part = jnp.sum(to_all(part[None], ("zl", "yl", "core"), 8)[:, 0], axis=0)
 
     first_row = (pair * 2 * PLANE + core) * ROWS_DEV
     place = jnp.stack(
@@ -277,10 +272,18 @@
     masked = ((0, 3 * rb, True),)
     state = attend(lengths, place, q, [mine, other], [masked, masked], (), False)
     half = prompt.shape[0] // 2
+    part, _ = lax.optimization_barrier((part, state[1]))
+    part = jnp.sum(to_all(part[None], "zh", pairs)[:, 0], axis=0)
     spans = ((0, half, False), (half, 2 * half, False))
     partial = attend(lengths, place, q, [prompt], [spans], state, True)
     exchanged = lax.all_to_all(partial, SHARE, 0, 0)
     context = combine(exchanged)
+
+    response_sum = part[:responses]
+    length_float = lengths.astype(jnp.float32)
+    adjusted = rewards - 0.5 * length_float / 2048
+    advantage = adjusted - jnp.mean(adjusted)
+    response_objective = -advantage * response_sum / length_float
     return (context, token_logprob, response_objective)
 
 

time: 113 us -> 112 us (level)
  the two profiles are of different devices: /device:TPU:1 before, /device:TPU:30 now
where the time goes in v6:
time: 112 us
  starting transfers between devices  41.3 us (37%)
  Pallas kernels  23.2 us (21%)
  waiting for transfers between devices  22.5 us (20%)
  between operations  14.9 us (13%)
  local copies, waits for them, and re-layouts  8.13 us (7%)
  other arithmetic  1.68 us (2%)
    pallas_call x2, Pallas kernels, attend(): pl.pallas_call(functools.partial(attend_kernel, pieces, not state, last),...  17.8 us
    ppermute x2, starting transfers between devices, shards(): lax.ppermute(own, 'zh', [(i, (i + d) % pairs) for i in range(pairs)])  14.3 us
    all_to_all x3, starting transfers between devices, to_all(): lax.all_to_all(jnp.broadcast_to(x[None], (count,) + x.shape), axes, 0, 0)  11.4 us
    all_to_all x1, waiting for transfers between devices, shards(): exchanged = lax.all_to_all(partial, SHARE, 0, 0)  7.74 us
    all_to_all x1, starting transfers between devices, shards(): stats = lax.all_to_all(stats, 'tp', 0, 0)  7.17 us
    ppermute x2, waiting for transfers between devices, shards(): lax.ppermute(own, 'zh', [(i, (i + d) % pairs) for i in range(pairs)])  7.09 us
    all_to_all x1, starting transfers between devices, shards(): exchanged = lax.all_to_all(partial, SHARE, 0, 0)  6.47 us
    all_gather x1, waiting for transfers between devices, shards(): lax.all_gather(prompt_kv.reshape(pb, 2 * HD), ('zh', 'core'), axis=0, til...  6.23 us
  transfers between devices with their start and end apart: 9, of which 4 were waited for; matrix products, arithmetic and copies ran while one was open for 5% of the time, Pallas kernels for 19%

profile of v6, /device:TPU:30, one launch (start us, length us, event | category | flops | bytes accessed | tf_op | source)
XLA Modules:
  0.0 111.7 jit_solution(15800199635885820628)
XLA Ops:
  7.2 0.0 copy-start.1
  7.2 0.0 copy-start.2
  7.2 0.0 copy-start
  7.2 0.0 all-gather.2.cloned.1.call-start
  7.2 1.7 %copy.29 = bf16[32,8,2,128]{3,1,2,0:T(8,128)(2,1)} copy(bf16[32,8,2,128]{3,2,1,0:T(2,128)(2,1)} %bitcast.36) | data formatting | bytes 262144
  9.0 0.0 copy-start.5
  9.0 0.0 all-gather.2.cloned.1.call-update
  9.0 1.0 copy.30
  10.0 0.8 broadcast_in_dim.40
  10.8 4.6 %all-to-all-start = ((bf16[4,128,512]{2,1,0:T(8,128)(2,1)}), bf16[4,128,512]{2,1,0:T(8,128)(2,1)S(1)}, u32[]{:S(2)}, u32[]{:S(2)}) async-start(bf16[4,128,512]{2,1,0:T(8,128)(2,1)} %broadcast_in_dim.40), calls=%async_computation | async-start | bytes 1048576 | tf_op jit(solution)/shard_map/all_to_all | solution.py:227
  15.4 0.8 copy.31
  16.3 5.2 %collective-permute-start = (bf16[128,256]{1,0:T(8,128)(2,1)S(1)}, bf16[128,256]{1,0:T(8,128)(2,1)S(1)}, u32[]{:S(2)}, u32[]{:S(2)}) collective-permute-start(bf16[128,256]{1,0:T(8,128)(2,1)S(1)} %bitcast.38), channel_id=1, source_target_pairs={{0,64},{64,128},{128,192},{192,256},{256,320},{320,384},{384,448},... | collective-permute-start | bytes 196616 | tf_op jit(solution)/shard_map/ppermute | solution.py:250
  21.5 9.1 %collective-permute-start.1 = (bf16[128,256]{1,0:T(8,128)(2,1)S(1)}, bf16[128,256]{1,0:T(8,128)(2,1)S(1)}, u32[]{:S(2)}, u32[]{:S(2)}) collective-permute-start(bf16[128,256]{1,0:T(8,128)(2,1)S(1)} %bitcast.39), channel_id=1, source_target_pairs={{0,128},{64,192},{128,256},{192,320},{256,384},{320,448},{384,0},{... | collective-permute-start | bytes 196616 | tf_op jit(solution)/shard_map/ppermute | solution.py:250
  30.6 0.0 copy-done.1
  30.6 0.1 copy.16
  30.7 0.1 reduce.4
  30.9 0.0 copy-done.2
  30.9 0.0 copy-done
  30.9 3.1 %logit_stats.1 = f32[8,8,128]{2,1,0:T(8,128)} custom-call(s32[1,128]{1,0:T(1,128)S(1)} %bitcast.31, s32[1]{0:T(128)} %bitcast.4.base_ref, bf16[128,9600]{1,0:T(8,128)(2,1)S(1)} %copy-done), custom_call_target="tpu_custom_call" | custom-call | flops 9830400 | bytes 2457600 | tf_op jit(solution)/shard_map/logit_stats/pallas_call | solution.py:53
  34.0 0.1 convert_reduce_fusion
  34.0 0.0 copy-done.5
  34.1 0.1 pad_add_fusion.refs_1_
  34.1 7.1 %collective-permute-done = bf16[128,256]{1,0:T(8,128)(2,1)S(1)} collective-permute-done((bf16[128,256]{1,0:T(8,128)(2,1)S(1)}, bf16[128,256]{1,0:T(8,128)(2,1)S(1)}, u32[]{:S(2)}, u32[]{:S(2)}) %collective-permute-start) | collective-permute-done | bytes 65568 | tf_op jit(solution)/shard_map/ppermute | solution.py:250
  41.2 0.0 all-to-all-done.refs_2_
  41.2 7.2 %all-to-all-start.2 = ((f32[8,8,128]{2,1,0:T(8,128)}), f32[8,8,128]{2,1,0:T(8,128)S(1)}, u32[]{:S(2)}, u32[]{:S(2)}) async-start(f32[8,8,128]{2,1,0:T(8,128)} %logit_stats.1), calls=%async_computation.2 | async-start | bytes 65536 | tf_op jit(solution)/shard_map/all_to_all | solution.py:246
  48.4 0.0 collective-permute-done.1
  48.4 1.9 %collective-permute-start.2 = (bf16[384,256]{1,0:T(8,128)(2,1)S(1)}, bf16[384,256]{1,0:T(8,128)(2,1)S(1)}, u32[]{:S(2)}, u32[]{:S(2)}) collective-permute-start(bf16[384,256]{1,0:T(8,128)(2,1)S(1)} %constant_dynamic-update-slice_fusion.refs_3_), channel_id=1, source_target_pairs={{0,8},{8,0},{1,9},{9,1},{2,10},{10,2},{3,11},{11,3},{4,12},{12,4},... | collective-permute-start | bytes 589832 | tf_op jit(solution)/shard_map/ppermute | solution.py:253
  50.4 1.4 %all-to-all-done.2 = f32[8,8,128]{2,1,0:T(8,128)S(1)} async-done(((f32[8,8,128]{2,1,0:T(8,128)}), f32[8,8,128]{2,1,0:T(8,128)S(1)}, u32[]{:S(2)}, u32[]{:S(2)}) %all-to-all-start.2) | async-done | bytes 32800 | tf_op jit(solution)/shard_map/all_to_all | solution.py:246
  51.9 0.0 copy-start.7
  51.9 0.1 select_reduce_fusion
  52.0 0.6 broadcast_in_dim.44
  52.6 3.3 %all-to-all-start.3 = ((f32[8,1,128]{2,1,0:T(1,128)}), f32[8,1,128]{2,1,0:T(1,128)S(1)}, u32[]{:S(2)}, u32[]{:S(2)}) async-start(f32[8,1,128]{2,1,0:T(1,128)} %broadcast_in_dim.44), calls=%async_computation.3 | async-start | bytes 8192 | tf_op jit(solution)/shard_map/all_to_all | solution.py:227
  55.9 0.0 collective-permute-done.2.refs_4_
  55.9 4.1 %attend.2 = (f32[4,128,512]{2,1,0:T(8,128)S(1)}, f32[4,128,128]{2,1,0:T(8,128)S(1)}) custom-call(s32[16]{0:T(128)S(1)} %copy-done.1, s32[3]{0:T(128)S(1)} %pad_add_fusion.refs_1_, bf16[4,128,512]{2,1,0:T(8,128)(2,1)S(1)} %all-to-all-done.refs_2_, bf16[384,256]{1,0:T(8,128)(2,1)S(1)} %constant_dynamic-update-slice_fusion.refs_3_, ...), custom_call_target="tpu_custom_call" | custom-call | flops 1610612736 | bytes 2490368 | tf_op jit(solution)/shard_map/attend/pallas_call | solution.py:179
  60.0 0.0 copy-done.7
  60.0 0.0 all-to-all-done.3
  60.1 0.6 broadcast_in_dim.45
  60.7 3.4 %all-to-all-start.4 = ((f32[8,1,128]{2,1,0:T(1,128)}), f32[8,1,128]{2,1,0:T(1,128)S(1)}, u32[]{:S(2)}, u32[]{:S(2)}) async-start(f32[8,1,128]{2,1,0:T(1,128)} %broadcast_in_dim.45), calls=%async_computation.4 | async-start | bytes 8192 | tf_op jit(solution)/shard_map/all_to_all | solution.py:227
  64.1 6.2 %all-gather.2.cloned.1.call-done.refs_3_ = bf16[4096,256]{1,0:T(8,128)(2,1)} async-done(((bf16[256,256]{1,0:T(8,128)(2,1)}), bf16[4096,256]{1,0:T(8,128)(2,1)}) %all-gather.2.cloned.1.call-update) | async-done | bytes 2097168 | tf_op jit(solution)/shard_map/all_gather | solution.py:240
  70.4 0.0 copy-start.3
  70.4 1.6 %copy-done.3 = bf16[4096,256]{1,0:T(8,128)(2,1)S(1)} copy-done((bf16[4096,256]{1,0:T(8,128)(2,1)S(1)}, bf16[4096,256]{1,0:T(8,128)(2,1)}, u32[]{:S(2)}) %copy-start.3) | copy-done | bytes 2097176
  71.9 0.0 copy-start.6
  72.0 13.6 %attend.3 = bf16[4,128,640]{2,1,0:T(8,128)(2,1)} custom-call(s32[16]{0:T(128)S(1)} %copy-done.1, s32[3]{0:T(128)S(1)} %pad_add_fusion.refs_1_, bf16[4,128,512]{2,1,0:T(8,128)(2,1)S(1)} %all-to-all-done.refs_2_, bf16[4096,256]{1,0:T(8,128)(2,1)S(1)} %copy-done.3, f32[4,128,512]{2,1,0:T(8,128)S(1)} %get-tuple-element.9.refs_4_, ...), custom_call_target="tpu_custom_call" | custom-call | flops 8589934592 | bytes 4194304 | tf_op jit(solution)/shard_map/attend/pallas_call | solution.py:179
  85.6 0.0 all-to-all-done.4
  85.6 6.5 %all-to-all-start.1 = ((bf16[4,128,640]{2,1,0:T(8,128)(2,1)}), bf16[4,128,640]{2,1,0:T(8,128)(2,1)S(1)}, u32[]{:S(2)}, u32[]{:S(2)}) async-start(bf16[4,128,640]{2,1,0:T(8,128)(2,1)} %attend.3), calls=%async_computation.1 | async-start | bytes 1310720 | tf_op jit(solution)/shard_map/all_to_all | solution.py:279
  92.1 0.0 copy-done.6
  92.1 0.6 fusion
  93.3 0.5 multiply_divide_fusion
  93.8 7.7 %all-to-all-done.1.parts_ref = bf16[4,128,640]{2,1,0:T(8,128)(2,1)S(1)} async-done(((bf16[4,128,640]{2,1,0:T(8,128)(2,1)}), bf16[4,128,640]{2,1,0:T(8,128)(2,1)S(1)}, u32[]{:S(2)}, u32[]{:S(2)}) %all-to-all-start.1) | async-done | bytes 655392 | tf_op jit(solution)/shard_map/all_to_all | solution.py:279
  101.6 0.0 copy-start.4
  101.6 0.8 copy-done.4
  102.4 2.4 %combine.1 = bf16[128,4,128]{2,1,0:T(4,128)(2,1)} custom-call(bf16[4,128,640]{2,1,0:T(8,128)(2,1)} %copy-done.4), custom_call_target="tpu_custom_call" | custom-call | tf_op jit(solution)/shard_map/combine/pallas_call | solution.py:216
  (11 shorter events, 0.2 us)
Async XLA Ops:
  7.2 23.4 %copy-start.1 = (s32[16]{0:T(128)S(1)}, s32[16]{0:T(128)}, u32[]{:S(2)}) copy-start(s32[16]{0:T(128)} %refs_0_.3) | copy-start | bytes 196
  7.2 23.7 %copy-start.2 = (s32[128]{0:T(128)S(1)}, s32[128]{0:T(128)}, u32[]{:S(2)}) copy-start(s32[128]{0:T(128)} %param.11) | copy-start | bytes 1540
  7.2 23.7 %copy-start = (bf16[128,9600]{1,0:T(8,128)(2,1)S(1)}, bf16[128,9600]{1,0:T(8,128)(2,1)}, u32[]{:S(2)}) copy-start(bf16[128,9600]{1,0:T(8,128)(2,1)} %logits_ref.1) | copy-start | bytes 7372804
  7.2 63.2 %all-gather.2.cloned.1.call-start = ((), (), s32[]{:S(2)}) async-start(), calls=%async_computation.5 | async-start | bytes 2228224 | tf_op jit(solution)/shard_map/all_gather | solution.py:240
  9.0 25.1 %copy-start.5 = (bf16[128,2,1,128]{3,1,2,0:T(2,128)(2,1)S(1)}, bf16[128,2,1,128]{3,1,2,0:T(2,128)(2,1)}, u32[]{:S(2)}) copy-start(bf16[128,2,1,128]{3,1,2,0:T(2,128)(2,1)} %param.9) | copy-start | bytes 196612
  10.8 30.4 %all-to-all-start = ((bf16[4,128,512]{2,1,0:T(8,128)(2,1)}), bf16[4,128,512]{2,1,0:T(8,128)(2,1)S(1)}, u32[]{:S(2)}, u32[]{:S(2)}) async-start(bf16[4,128,512]{2,1,0:T(8,128)(2,1)} %broadcast_in_dim.40), calls=%async_computation | async-start | bytes 1048576 | tf_op jit(solution)/shard_map/all_to_all | solution.py:227
  16.3 24.9 %collective-permute-start = (bf16[128,256]{1,0:T(8,128)(2,1)S(1)}, bf16[128,256]{1,0:T(8,128)(2,1)S(1)}, u32[]{:S(2)}, u32[]{:S(2)}) collective-permute-start(bf16[128,256]{1,0:T(8,128)(2,1)S(1)} %bitcast.38), channel_id=1, source_target_pairs={{0,64},{64,128},{128,192},{192,256},{256,320},{320,384},{384,448},... | collective-permute-start | bytes 196616 | tf_op jit(solution)/shard_map/ppermute | solution.py:250
  21.5 26.9 %collective-permute-start.1 = (bf16[128,256]{1,0:T(8,128)(2,1)S(1)}, bf16[128,256]{1,0:T(8,128)(2,1)S(1)}, u32[]{:S(2)}, u32[]{:S(2)}) collective-permute-start(bf16[128,256]{1,0:T(8,128)(2,1)S(1)} %bitcast.39), channel_id=1, source_target_pairs={{0,128},{64,192},{128,256},{192,320},{256,384},{320,448},{384,0},{... | collective-permute-start | bytes 196616 | tf_op jit(solution)/shard_map/ppermute | solution.py:250
  41.2 10.6 %all-to-all-start.2 = ((f32[8,8,128]{2,1,0:T(8,128)}), f32[8,8,128]{2,1,0:T(8,128)S(1)}, u32[]{:S(2)}, u32[]{:S(2)}) async-start(f32[8,8,128]{2,1,0:T(8,128)} %logit_stats.1), calls=%async_computation.2 | async-start | bytes 65536 | tf_op jit(solution)/shard_map/all_to_all | solution.py:246
  48.4 7.5 %collective-permute-start.2 = (bf16[384,256]{1,0:T(8,128)(2,1)S(1)}, bf16[384,256]{1,0:T(8,128)(2,1)S(1)}, u32[]{:S(2)}, u32[]{:S(2)}) collective-permute-start(bf16[384,256]{1,0:T(8,128)(2,1)S(1)} %constant_dynamic-update-slice_fusion.refs_3_), channel_id=1, source_target_pairs={{0,8},{8,0},{1,9},{9,1},{2,10},{10,2},{3,11},{11,3},{4,12},{12,4},... | collective-permute-start | bytes 589832 | tf_op jit(solution)/shard_map/ppermute | solution.py:253
  51.9 8.2 %copy-start.7 = (f32[128]{0:T(128)}, f32[128]{0:T(128)S(1)}, u32[]{:S(2)}) copy-start(f32[128]{0:T(128)S(1)} %compare_select_fusion) | copy-start | bytes 1540
  52.6 7.5 %all-to-all-start.3 = ((f32[8,1,128]{2,1,0:T(1,128)}), f32[8,1,128]{2,1,0:T(1,128)S(1)}, u32[]{:S(2)}, u32[]{:S(2)}) async-start(f32[8,1,128]{2,1,0:T(1,128)} %broadcast_in_dim.44), calls=%async_computation.3 | async-start | bytes 8192 | tf_op jit(solution)/shard_map/all_to_all | solution.py:227
  60.7 24.9 %all-to-all-start.4 = ((f32[8,1,128]{2,1,0:T(1,128)}), f32[8,1,128]{2,1,0:T(1,128)S(1)}, u32[]{:S(2)}, u32[]{:S(2)}) async-start(f32[8,1,128]{2,1,0:T(1,128)} %broadcast_in_dim.45), calls=%async_computation.4 | async-start | bytes 8192 | tf_op jit(solution)/shard_map/all_to_all | solution.py:227
  70.4 1.6 %copy-start.3 = (bf16[4096,256]{1,0:T(8,128)(2,1)S(1)}, bf16[4096,256]{1,0:T(8,128)(2,1)}, u32[]{:S(2)}) copy-start(bf16[4096,256]{1,0:T(8,128)(2,1)} %all-gather.2.cloned.1.call-done.refs_3_) | copy-start | bytes 6291460
  71.9 20.1 %copy-start.6 = (f32[16]{0:T(128)S(1)}, f32[16]{0:T(128)}, u32[]{:S(2)}) copy-start(f32[16]{0:T(128)} %param.13) | copy-start | bytes 196
  85.6 16.0 %all-to-all-start.1 = ((bf16[4,128,640]{2,1,0:T(8,128)(2,1)}), bf16[4,128,640]{2,1,0:T(8,128)(2,1)S(1)}, u32[]{:S(2)}, u32[]{:S(2)}) async-start(bf16[4,128,640]{2,1,0:T(8,128)(2,1)} %attend.3), calls=%async_computation.1 | async-start | bytes 1310720 | tf_op jit(solution)/shard_map/all_to_all | solution.py:279
  101.6 0.8 copy-start.4
Sparse Core Ops, SparseCore 0:
  10.7 59.5 all-gather.1

commit v7 on v6

--- a/solution.py
+++ b/solution.py
@@ -246,9 +246,9 @@
     stats = lax.all_to_all(stats, "tp", 0, 0)
 
     own = response_kv.reshape(rb, 2 * HD)
-    before = [
-        lax.ppermute(own, "zh", [(i, (i + d) % pairs) for i in range(pairs)]) for d in (1, 2)
-    ]
+    route = [(i, (i + 1) % pairs) for i in range(pairs)]
+    once = lax.ppermute(own, "zh", route)
+    before = [once, lax.ppermute(once, "zh", route)]
     mine = jnp.concatenate([own] + before, axis=0)
     other = lax.ppermute(mine, "core", [(0, 1), (1, 0)])
 

time: 112 us -> 110 us (0.982)
  the two profiles are of different devices: /device:TPU:30 before, /device:TPU:1 now
where the time goes in v7:
time: 110 us; the launch traced here: 109 us
  starting transfers between devices  39.9 us (36%)
  Pallas kernels  23.2 us (21%)
  waiting for transfers between devices  21.3 us (19%)
  between operations  14.9 us (14%)
  local copies, waits for them, and re-layouts  8.13 us (7%)
  other arithmetic  1.68 us (2%)
    all_to_all x3, starting transfers between devices, to_all(): lax.all_to_all(jnp.broadcast_to(x[None], (count,) + x.shape), axes, 0, 0)  18.9 us
    pallas_call x2, Pallas kernels, attend(): pl.pallas_call(functools.partial(attend_kernel, pieces, not state, last),...  17.8 us
    ppermute x1, waiting for transfers between devices, shards(): once = lax.ppermute(own, 'zh', route)  8.66 us
    all_to_all x1, waiting for transfers between devices, shards(): exchanged = lax.all_to_all(partial, SHARE, 0, 0)  7.22 us
    all_to_all x1, starting transfers between devices, shards(): stats = lax.all_to_all(stats, 'tp', 0, 0)  6.66 us
    unnamed x21, local copies, waits for them, and re-layouts  6 us
    ppermute x1, starting transfers between devices, shards(): once = lax.ppermute(own, 'zh', route)  4.9 us
    all_to_all x1, starting transfers between devices, shards(): exchanged = lax.all_to_all(partial, SHARE, 0, 0)  4.15 us
  transfers between devices with their start and end apart: 9, of which 6 were waited for; matrix products, arithmetic and copies ran while one was open for 5% of the time, Pallas kernels for 19%

profile of v7, /device:TPU:1, one launch (start us, length us, event | category | flops | bytes accessed | tf_op | source)
XLA Modules:
  0.0 109.1 jit_solution(10599670335693858995)
XLA Ops:
  7.2 0.0 copy-start.1
  7.2 0.0 copy-start.2
  7.2 0.0 copy-start
  7.2 0.0 all-gather.2.cloned.1.call-start
  7.2 1.7 %copy.29 = bf16[32,8,2,128]{3,1,2,0:T(8,128)(2,1)} copy(bf16[32,8,2,128]{3,2,1,0:T(2,128)(2,1)} %bitcast.36) | data formatting | bytes 262144
  9.0 0.0 copy-start.5
  9.0 0.0 all-gather.2.cloned.1.call-update
  9.0 1.0 copy.30
  10.0 0.8 broadcast_in_dim.40
  10.8 4.7 %all-to-all-start = ((bf16[4,128,512]{2,1,0:T(8,128)(2,1)}), bf16[4,128,512]{2,1,0:T(8,128)(2,1)S(1)}, u32[]{:S(2)}, u32[]{:S(2)}) async-start(bf16[4,128,512]{2,1,0:T(8,128)(2,1)} %broadcast_in_dim.40), calls=%async_computation | async-start | bytes 1048576 | tf_op jit(solution)/shard_map/all_to_all | solution.py:227
  15.5 0.8 copy.31
  16.4 4.9 %collective-permute-start = (bf16[128,256]{1,0:T(8,128)(2,1)S(1)}, bf16[128,256]{1,0:T(8,128)(2,1)S(1)}, u32[]{:S(2)}, u32[]{:S(2)}) collective-permute-start(bf16[128,256]{1,0:T(8,128)(2,1)S(1)} %bitcast.38), channel_id=1, source_target_pairs={{0,64},{64,128},{128,192},{192,256},{256,320},{320,384},{384,448},... | collective-permute-start | bytes 196616 | tf_op jit(solution)/shard_map/ppermute | solution.py:250
  21.3 0.0 copy-done.1
  21.3 0.1 copy.16
  21.4 0.1 reduce.4
  21.6 0.0 copy-done.2
  21.6 0.0 copy-done
  21.6 3.1 %logit_stats.1 = f32[8,8,128]{2,1,0:T(8,128)} custom-call(s32[1,128]{1,0:T(1,128)S(1)} %bitcast.31, s32[1]{0:T(128)} %bitcast.4.base_ref, bf16[128,9600]{1,0:T(8,128)(2,1)S(1)} %copy-done), custom_call_target="tpu_custom_call" | custom-call | flops 9830400 | bytes 2457600 | tf_op jit(solution)/shard_map/logit_stats/pallas_call | solution.py:53
  24.7 0.1 convert_reduce_fusion
  24.8 0.0 copy-done.5
  24.8 0.1 pad_add_fusion.refs_1_
  24.9 8.7 %collective-permute-done = bf16[128,256]{1,0:T(8,128)(2,1)S(1)} collective-permute-done((bf16[128,256]{1,0:T(8,128)(2,1)S(1)}, bf16[128,256]{1,0:T(8,128)(2,1)S(1)}, u32[]{:S(2)}, u32[]{:S(2)}) %collective-permute-start) | collective-permute-done | bytes 65568 | tf_op jit(solution)/shard_map/ppermute | solution.py:250
  33.5 1.9 %collective-permute-start.1 = (bf16[128,256]{1,0:T(8,128)(2,1)S(1)}, bf16[128,256]{1,0:T(8,128)(2,1)S(1)}, u32[]{:S(2)}, u32[]{:S(2)}) collective-permute-start(bf16[128,256]{1,0:T(8,128)(2,1)S(1)} %collective-permute-done), channel_id=1, source_target_pairs={{0,64},{64,128},{128,192},{192,256},{256,320},{320,384},{384,448},... | collective-permute-start | bytes 196616 | tf_op jit(solution)/shard_map/ppermute | solution.py:251
  35.5 0.0 all-to-all-done.refs_2_
  35.5 6.7 %all-to-all-start.2 = ((f32[8,8,128]{2,1,0:T(8,128)}), f32[8,8,128]{2,1,0:T(8,128)S(1)}, u32[]{:S(2)}, u32[]{:S(2)}) async-start(f32[8,8,128]{2,1,0:T(8,128)} %logit_stats.1), calls=%async_computation.2 | async-start | bytes 65536 | tf_op jit(solution)/shard_map/all_to_all | solution.py:246
  42.1 0.4 collective-permute-done.1
  42.5 3.3 %collective-permute-start.2 = (bf16[384,256]{1,0:T(8,128)(2,1)S(1)}, bf16[384,256]{1,0:T(8,128)(2,1)S(1)}, u32[]{:S(2)}, u32[]{:S(2)}) collective-permute-start(bf16[384,256]{1,0:T(8,128)(2,1)S(1)} %constant_dynamic-update-slice_fusion.refs_3_), channel_id=1, source_target_pairs={{0,8},{8,0},{1,9},{9,1},{2,10},{10,2},{3,11},{11,3},{4,12},{12,4},... | collective-permute-start | bytes 589832 | tf_op jit(solution)/shard_map/ppermute | solution.py:253
  45.9 2.9 %all-to-all-done.2 = f32[8,8,128]{2,1,0:T(8,128)S(1)} async-done(((f32[8,8,128]{2,1,0:T(8,128)}), f32[8,8,128]{2,1,0:T(8,128)S(1)}, u32[]{:S(2)}, u32[]{:S(2)}) %all-to-all-start.2) | async-done | bytes 32800 | tf_op jit(solution)/shard_map/all_to_all | solution.py:246
  48.8 0.0 copy-start.7
  48.8 0.1 select_reduce_fusion
  48.9 0.6 broadcast_in_dim.44
  49.5 6.1 %all-to-all-start.3 = ((f32[8,1,128]{2,1,0:T(1,128)}), f32[8,1,128]{2,1,0:T(1,128)S(1)}, u32[]{:S(2)}, u32[]{:S(2)}) async-start(f32[8,1,128]{2,1,0:T(1,128)} %broadcast_in_dim.44), calls=%async_computation.3 | async-start | bytes 8192 | tf_op jit(solution)/shard_map/all_to_all | solution.py:227
  55.7 0.0 collective-permute-done.2.refs_4_
  55.7 4.1 %attend.2 = (f32[4,128,512]{2,1,0:T(8,128)S(1)}, f32[4,128,128]{2,1,0:T(8,128)S(1)}) custom-call(s32[16]{0:T(128)S(1)} %copy-done.1, s32[3]{0:T(128)S(1)} %pad_add_fusion.refs_1_, bf16[4,128,512]{2,1,0:T(8,128)(2,1)S(1)} %all-to-all-done.refs_2_, bf16[384,256]{1,0:T(8,128)(2,1)S(1)} %constant_dynamic-update-slice_fusion.refs_3_, ...), custom_call_target="tpu_custom_call" | custom-call | flops 1610612736 | bytes 2490368 | tf_op jit(solution)/shard_map/attend/pallas_call | solution.py:179
  59.8 0.0 copy-done.7
  59.8 0.1 all-to-all-done.3
  59.9 0.6 broadcast_in_dim.45
  60.5 8.0 %all-to-all-start.4 = ((f32[8,1,128]{2,1,0:T(1,128)}), f32[8,1,128]{2,1,0:T(1,128)S(1)}, u32[]{:S(2)}, u32[]{:S(2)}) async-start(f32[8,1,128]{2,1,0:T(1,128)} %broadcast_in_dim.45), calls=%async_computation.4 | async-start | bytes 8192 | tf_op jit(solution)/shard_map/all_to_all | solution.py:227
  68.6 2.0 %all-gather.2.cloned.1.call-done.refs_3_ = bf16[4096,256]{1,0:T(8,128)(2,1)} async-done(((bf16[256,256]{1,0:T(8,128)(2,1)}), bf16[4096,256]{1,0:T(8,128)(2,1)}) %all-gather.2.cloned.1.call-update) | async-done | bytes 2097168 | tf_op jit(solution)/shard_map/all_gather | solution.py:240
  70.6 0.0 copy-start.3
  70.6 1.6 %copy-done.3 = bf16[4096,256]{1,0:T(8,128)(2,1)S(1)} copy-done((bf16[4096,256]{1,0:T(8,128)(2,1)S(1)}, bf16[4096,256]{1,0:T(8,128)(2,1)}, u32[]{:S(2)}) %copy-start.3) | copy-done | bytes 2097176
  72.2 0.0 copy-start.6
  72.2 13.6 %attend.3 = bf16[4,128,640]{2,1,0:T(8,128)(2,1)} custom-call(s32[16]{0:T(128)S(1)} %copy-done.1, s32[3]{0:T(128)S(1)} %pad_add_fusion.refs_1_, bf16[4,128,512]{2,1,0:T(8,128)(2,1)S(1)} %all-to-all-done.refs_2_, bf16[4096,256]{1,0:T(8,128)(2,1)S(1)} %copy-done.3, f32[4,128,512]{2,1,0:T(8,128)S(1)} %get-tuple-element.9.refs_4_, ...), custom_call_target="tpu_custom_call" | custom-call | flops 8589934592 | bytes 4194304 | tf_op jit(solution)/shard_map/attend/pallas_call | solution.py:179
  85.8 0.0 all-to-all-done.4
  85.8 4.1 %all-to-all-start.1 = ((bf16[4,128,640]{2,1,0:T(8,128)(2,1)}), bf16[4,128,640]{2,1,0:T(8,128)(2,1)S(1)}, u32[]{:S(2)}, u32[]{:S(2)}) async-start(bf16[4,128,640]{2,1,0:T(8,128)(2,1)} %attend.3), calls=%async_computation.1 | async-start | bytes 1310720 | tf_op jit(solution)/shard_map/all_to_all | solution.py:279
  90.0 0.0 copy-done.6
  90.0 0.6 fusion
  91.2 0.5 multiply_divide_fusion
  91.8 7.2 %all-to-all-done.1.parts_ref = bf16[4,128,640]{2,1,0:T(8,128)(2,1)S(1)} async-done(((bf16[4,128,640]{2,1,0:T(8,128)(2,1)}), bf16[4,128,640]{2,1,0:T(8,128)(2,1)S(1)}, u32[]{:S(2)}, u32[]{:S(2)}) %all-to-all-start.1) | async-done | bytes 655392 | tf_op jit(solution)/shard_map/all_to_all | solution.py:279
  99.0 0.0 copy-start.4
  99.0 0.8 copy-done.4
  99.8 2.4 %combine.1 = bf16[128,4,128]{2,1,0:T(4,128)(2,1)} custom-call(bf16[4,128,640]{2,1,0:T(8,128)(2,1)} %copy-done.4), custom_call_target="tpu_custom_call" | custom-call | tf_op jit(solution)/shard_map/combine/pallas_call | solution.py:216
  (11 shorter events, 0.2 us)
Async XLA Ops:
  7.2 14.2 %copy-start.1 = (s32[16]{0:T(128)S(1)}, s32[16]{0:T(128)}, u32[]{:S(2)}) copy-start(s32[16]{0:T(128)} %refs_0_.3) | copy-start | bytes 196
  7.2 14.4 %copy-start.2 = (s32[128]{0:T(128)S(1)}, s32[128]{0:T(128)}, u32[]{:S(2)}) copy-start(s32[128]{0:T(128)} %param.11) | copy-start | bytes 1540
  7.2 14.4 %copy-start = (bf16[128,9600]{1,0:T(8,128)(2,1)S(1)}, bf16[128,9600]{1,0:T(8,128)(2,1)}, u32[]{:S(2)}) copy-start(bf16[128,9600]{1,0:T(8,128)(2,1)} %logits_ref.1) | copy-start | bytes 7372804
  7.2 63.4 %all-gather.2.cloned.1.call-start = ((), (), s32[]{:S(2)}) async-start(), calls=%async_computation.5 | async-start | bytes 2228224 | tf_op jit(solution)/shard_map/all_gather | solution.py:240
  9.0 15.8 %copy-start.5 = (bf16[128,2,1,128]{3,1,2,0:T(2,128)(2,1)S(1)}, bf16[128,2,1,128]{3,1,2,0:T(2,128)(2,1)}, u32[]{:S(2)}) copy-start(bf16[128,2,1,128]{3,1,2,0:T(2,128)(2,1)} %param.9) | copy-start | bytes 196612
  10.8 24.7 %all-to-all-start = ((bf16[4,128,512]{2,1,0:T(8,128)(2,1)}), bf16[4,128,512]{2,1,0:T(8,128)(2,1)S(1)}, u32[]{:S(2)}, u32[]{:S(2)}) async-start(bf16[4,128,512]{2,1,0:T(8,128)(2,1)} %broadcast_in_dim.40), calls=%async_computation | async-start | bytes 1048576 | tf_op jit(solution)/shard_map/all_to_all | solution.py:227
  16.4 17.1 %collective-permute-start = (bf16[128,256]{1,0:T(8,128)(2,1)S(1)}, bf16[128,256]{1,0:T(8,128)(2,1)S(1)}, u32[]{:S(2)}, u32[]{:S(2)}) collective-permute-start(bf16[128,256]{1,0:T(8,128)(2,1)S(1)} %bitcast.38), channel_id=1, source_target_pairs={{0,64},{64,128},{128,192},{192,256},{256,320},{320,384},{384,448},... | collective-permute-start | bytes 196616 | tf_op jit(solution)/shard_map/ppermute | solution.py:250
  33.5 9.0 %collective-permute-start.1 = (bf16[128,256]{1,0:T(8,128)(2,1)S(1)}, bf16[128,256]{1,0:T(8,128)(2,1)S(1)}, u32[]{:S(2)}, u32[]{:S(2)}) collective-permute-start(bf16[128,256]{1,0:T(8,128)(2,1)S(1)} %collective-permute-done), channel_id=1, source_target_pairs={{0,64},{64,128},{128,192},{192,256},{256,320},{320,384},{384,448},... | collective-permute-start | bytes 196616 | tf_op jit(solution)/shard_map/ppermute | solution.py:251
  35.5 13.3 %all-to-all-start.2 = ((f32[8,8,128]{2,1,0:T(8,128)}), f32[8,8,128]{2,1,0:T(8,128)S(1)}, u32[]{:S(2)}, u32[]{:S(2)}) async-start(f32[8,8,128]{2,1,0:T(8,128)} %logit_stats.1), calls=%async_computation.2 | async-start | bytes 65536 | tf_op jit(solution)/shard_map/all_to_all | solution.py:246
  42.5 13.1 %collective-permute-start.2 = (bf16[384,256]{1,0:T(8,128)(2,1)S(1)}, bf16[384,256]{1,0:T(8,128)(2,1)S(1)}, u32[]{:S(2)}, u32[]{:S(2)}) collective-permute-start(bf16[384,256]{1,0:T(8,128)(2,1)S(1)} %constant_dynamic-update-slice_fusion.refs_3_), channel_id=1, source_target_pairs={{0,8},{8,0},{1,9},{9,1},{2,10},{10,2},{3,11},{11,3},{4,12},{12,4},... | collective-permute-start | bytes 589832 | tf_op jit(solution)/shard_map/ppermute | solution.py:253
  48.8 11.0 %copy-start.7 = (f32[128]{0:T(128)}, f32[128]{0:T(128)S(1)}, u32[]{:S(2)}) copy-start(f32[128]{0:T(128)S(1)} %compare_select_fusion) | copy-start | bytes 1540
  49.5 10.4 %all-to-all-start.3 = ((f32[8,1,128]{2,1,0:T(1,128)}), f32[8,1,128]{2,1,0:T(1,128)S(1)}, u32[]{:S(2)}, u32[]{:S(2)}) async-start(f32[8,1,128]{2,1,0:T(1,128)} %broadcast_in_dim.44), calls=%async_computation.3 | async-start | bytes 8192 | tf_op jit(solution)/shard_map/all_to_all | solution.py:227
  60.5 25.3 %all-to-all-start.4 = ((f32[8,1,128]{2,1,0:T(1,128)}), f32[8,1,128]{2,1,0:T(1,128)S(1)}, u32[]{:S(2)}, u32[]{:S(2)}) async-start(f32[8,1,128]{2,1,0:T(1,128)} %broadcast_in_dim.45), calls=%async_computation.4 | async-start | bytes 8192 | tf_op jit(solution)/shard_map/all_to_all | solution.py:227
  70.6 1.6 %copy-start.3 = (bf16[4096,256]{1,0:T(8,128)(2,1)S(1)}, bf16[4096,256]{1,0:T(8,128)(2,1)}, u32[]{:S(2)}) copy-start(bf16[4096,256]{1,0:T(8,128)(2,1)} %all-gather.2.cloned.1.call-done.refs_3_) | copy-start | bytes 6291460
  72.2 17.8 %copy-start.6 = (f32[16]{0:T(128)S(1)}, f32[16]{0:T(128)}, u32[]{:S(2)}) copy-start(f32[16]{0:T(128)} %param.13) | copy-start | bytes 196
  85.8 13.2 %all-to-all-start.1 = ((bf16[4,128,640]{2,1,0:T(8,128)(2,1)}), bf16[4,128,640]{2,1,0:T(8,128)(2,1)S(1)}, u32[]{:S(2)}, u32[]{:S(2)}) async-start(bf16[4,128,640]{2,1,0:T(8,128)(2,1)} %attend.3), calls=%async_computation.1 | async-start | bytes 1310720 | tf_op jit(solution)/shard_map/all_to_all | solution.py:279
  99.0 0.8 copy-start.4
Sparse Core Ops, SparseCore 0:
  10.7 59.8 all-gather.1

commit v8 on v7

--- a/solution.py
+++ b/solution.py
@@ -219,6 +219,7 @@
         in_specs=[pl.BlockSpec((PLANE, rows, HEADS * HD + HD), lambda i: (0, i, 0))],
         out_specs=pl.BlockSpec((rows, HEADS, HD), lambda i: (i, 0, 0)),
         out_shape=jax.ShapeDtypeStruct((ROWS_DEV, HEADS, HD), jnp.bfloat16),
+        compiler_params=pltpu.CompilerParams(vmem_limit_bytes=62 * MIB),
         name="combine",
     )(parts)
 

time: 110 us -> 110 us (level)
  no operation moved by 1% of the time
where the time goes in v8:
time: 110 us; the launch traced here: 109 us
  starting transfers between devices  39.9 us (36%)
  Pallas kernels  23.2 us (21%)
  waiting for transfers between devices  21.3 us (19%)
  between operations  14.9 us (14%)
  local copies, waits for them, and re-layouts  8.13 us (7%)
  other arithmetic  1.68 us (2%)
    all_to_all x3, starting transfers between devices, to_all(): lax.all_to_all(jnp.broadcast_to(x[None], (count,) + x.shape), axes, 0, 0)  18.9 us
    pallas_call x2, Pallas kernels, attend(): pl.pallas_call(functools.partial(attend_kernel, pieces, not state, last),...  17.8 us
    ppermute x1, waiting for transfers between devices, shards(): once = lax.ppermute(own, 'zh', route)  8.66 us
    all_to_all x1, waiting for transfers between devices, shards(): exchanged = lax.all_to_all(partial, SHARE, 0, 0)  7.22 us
    all_to_all x1, starting transfers between devices, shards(): stats = lax.all_to_all(stats, 'tp', 0, 0)  6.66 us
    unnamed x21, local copies, waits for them, and re-layouts  6 us
    ppermute x1, starting transfers between devices, shards(): once = lax.ppermute(own, 'zh', route)  4.9 us
    all_to_all x1, starting transfers between devices, shards(): exchanged = lax.all_to_all(partial, SHARE, 0, 0)  4.15 us
  transfers between devices with their start and end apart: 9, of which 6 were waited for; matrix products, arithmetic and copies ran while one was open for 5% of the time, Pallas kernels for 19%

profile of v8, /device:TPU:1, one launch (start us, length us, event | category | flops | bytes accessed | tf_op | source)
XLA Modules:
  0.0 109.1 jit_solution(7921201003318545372)
XLA Ops:
  7.2 0.0 copy-start.1
  7.2 0.0 copy-start.2
  7.2 0.0 copy-start
  7.2 0.0 all-gather.2.cloned.1.call-start
  7.2 1.7 %copy.29 = bf16[32,8,2,128]{3,1,2,0:T(8,128)(2,1)} copy(bf16[32,8,2,128]{3,2,1,0:T(2,128)(2,1)} %bitcast.36) | data formatting | bytes 262144
  9.0 0.0 copy-start.5
  9.0 0.0 all-gather.2.cloned.1.call-update
  9.0 1.0 copy.30
  10.0 0.8 broadcast_in_dim.40
  10.8 4.7 %all-to-all-start = ((bf16[4,128,512]{2,1,0:T(8,128)(2,1)}), bf16[4,128,512]{2,1,0:T(8,128)(2,1)S(1)}, u32[]{:S(2)}, u32[]{:S(2)}) async-start(bf16[4,128,512]{2,1,0:T(8,128)(2,1)} %broadcast_in_dim.40), calls=%async_computation | async-start | bytes 1048576 | tf_op jit(solution)/shard_map/all_to_all | solution.py:228
  15.5 0.8 copy.31
  16.4 4.9 %collective-permute-start = (bf16[128,256]{1,0:T(8,128)(2,1)S(1)}, bf16[128,256]{1,0:T(8,128)(2,1)S(1)}, u32[]{:S(2)}, u32[]{:S(2)}) collective-permute-start(bf16[128,256]{1,0:T(8,128)(2,1)S(1)} %bitcast.38), channel_id=1, source_target_pairs={{0,64},{64,128},{128,192},{192,256},{256,320},{320,384},{384,448},... | collective-permute-start | bytes 196616 | tf_op jit(solution)/shard_map/ppermute | solution.py:251
  21.3 0.0 copy-done.1
  21.3 0.1 copy.16
  21.4 0.1 reduce.4
  21.6 0.0 copy-done.2
  21.6 0.0 copy-done
  21.6 3.1 %logit_stats.1 = f32[8,8,128]{2,1,0:T(8,128)} custom-call(s32[1,128]{1,0:T(1,128)S(1)} %bitcast.31, s32[1]{0:T(128)} %bitcast.4.base_ref, bf16[128,9600]{1,0:T(8,128)(2,1)S(1)} %copy-done), custom_call_target="tpu_custom_call" | custom-call | flops 9830400 | bytes 2457600 | tf_op jit(solution)/shard_map/logit_stats/pallas_call | solution.py:53
  24.7 0.1 convert_reduce_fusion
  24.8 0.0 copy-done.5
  24.8 0.1 pad_add_fusion.refs_1_
  24.9 8.7 %collective-permute-done = bf16[128,256]{1,0:T(8,128)(2,1)S(1)} collective-permute-done((bf16[128,256]{1,0:T(8,128)(2,1)S(1)}, bf16[128,256]{1,0:T(8,128)(2,1)S(1)}, u32[]{:S(2)}, u32[]{:S(2)}) %collective-permute-start) | collective-permute-done | bytes 65568 | tf_op jit(solution)/shard_map/ppermute | solution.py:251
  33.5 1.9 %collective-permute-start.1 = (bf16[128,256]{1,0:T(8,128)(2,1)S(1)}, bf16[128,256]{1,0:T(8,128)(2,1)S(1)}, u32[]{:S(2)}, u32[]{:S(2)}) collective-permute-start(bf16[128,256]{1,0:T(8,128)(2,1)S(1)} %collective-permute-done), channel_id=1, source_target_pairs={{0,64},{64,128},{128,192},{192,256},{256,320},{320,384},{384,448},... | collective-permute-start | bytes 196616 | tf_op jit(solution)/shard_map/ppermute | solution.py:252
  35.5 0.0 all-to-all-done.refs_2_
  35.5 6.7 %all-to-all-start.2 = ((f32[8,8,128]{2,1,0:T(8,128)}), f32[8,8,128]{2,1,0:T(8,128)S(1)}, u32[]{:S(2)}, u32[]{:S(2)}) async-start(f32[8,8,128]{2,1,0:T(8,128)} %logit_stats.1), calls=%async_computation.2 | async-start | bytes 65536 | tf_op jit(solution)/shard_map/all_to_all | solution.py:247
  42.1 0.4 collective-permute-done.1
  42.5 3.3 %collective-permute-start.2 = (bf16[384,256]{1,0:T(8,128)(2,1)S(1)}, bf16[384,256]{1,0:T(8,128)(2,1)S(1)}, u32[]{:S(2)}, u32[]{:S(2)}) collective-permute-start(bf16[384,256]{1,0:T(8,128)(2,1)S(1)} %constant_dynamic-update-slice_fusion.refs_3_), channel_id=1, source_target_pairs={{0,8},{8,0},{1,9},{9,1},{2,10},{10,2},{3,11},{11,3},{4,12},{12,4},... | collective-permute-start | bytes 589832 | tf_op jit(solution)/shard_map/ppermute | solution.py:254
  45.9 2.9 %all-to-all-done.2 = f32[8,8,128]{2,1,0:T(8,128)S(1)} async-done(((f32[8,8,128]{2,1,0:T(8,128)}), f32[8,8,128]{2,1,0:T(8,128)S(1)}, u32[]{:S(2)}, u32[]{:S(2)}) %all-to-all-start.2) | async-done | bytes 32800 | tf_op jit(solution)/shard_map/all_to_all | solution.py:247
  48.8 0.0 copy-start.7
  48.8 0.1 select_reduce_fusion
  48.9 0.6 broadcast_in_dim.44
  49.5 6.1 %all-to-all-start.3 = ((f32[8,1,128]{2,1,0:T(1,128)}), f32[8,1,128]{2,1,0:T(1,128)S(1)}, u32[]{:S(2)}, u32[]{:S(2)}) async-start(f32[8,1,128]{2,1,0:T(1,128)} %broadcast_in_dim.44), calls=%async_computation.3 | async-start | bytes 8192 | tf_op jit(solution)/shard_map/all_to_all | solution.py:228
  55.7 0.0 collective-permute-done.2.refs_4_
  55.7 4.1 %attend.2 = (f32[4,128,512]{2,1,0:T(8,128)S(1)}, f32[4,128,128]{2,1,0:T(8,128)S(1)}) custom-call(s32[16]{0:T(128)S(1)} %copy-done.1, s32[3]{0:T(128)S(1)} %pad_add_fusion.refs_1_, bf16[4,128,512]{2,1,0:T(8,128)(2,1)S(1)} %all-to-all-done.refs_2_, bf16[384,256]{1,0:T(8,128)(2,1)S(1)} %constant_dynamic-update-slice_fusion.refs_3_, ...), custom_call_target="tpu_custom_call" | custom-call | flops 1610612736 | bytes 2490368 | tf_op jit(solution)/shard_map/attend/pallas_call | solution.py:179
  59.8 0.0 copy-done.7
  59.8 0.1 all-to-all-done.3
  59.9 0.6 broadcast_in_dim.45
  60.5 8.0 %all-to-all-start.4 = ((f32[8,1,128]{2,1,0:T(1,128)}), f32[8,1,128]{2,1,0:T(1,128)S(1)}, u32[]{:S(2)}, u32[]{:S(2)}) async-start(f32[8,1,128]{2,1,0:T(1,128)} %broadcast_in_dim.45), calls=%async_computation.4 | async-start | bytes 8192 | tf_op jit(solution)/shard_map/all_to_all | solution.py:228
  68.6 2.0 %all-gather.2.cloned.1.call-done.refs_3_ = bf16[4096,256]{1,0:T(8,128)(2,1)} async-done(((bf16[256,256]{1,0:T(8,128)(2,1)}), bf16[4096,256]{1,0:T(8,128)(2,1)}) %all-gather.2.cloned.1.call-update) | async-done | bytes 2097168 | tf_op jit(solution)/shard_map/all_gather | solution.py:241
  70.6 0.0 copy-start.3
  70.6 1.6 %copy-done.3 = bf16[4096,256]{1,0:T(8,128)(2,1)S(1)} copy-done((bf16[4096,256]{1,0:T(8,128)(2,1)S(1)}, bf16[4096,256]{1,0:T(8,128)(2,1)}, u32[]{:S(2)}) %copy-start.3) | copy-done | bytes 2097176
  72.2 0.0 copy-start.6
  72.2 13.6 %attend.3 = bf16[4,128,640]{2,1,0:T(8,128)(2,1)} custom-call(s32[16]{0:T(128)S(1)} %copy-done.1, s32[3]{0:T(128)S(1)} %pad_add_fusion.refs_1_, bf16[4,128,512]{2,1,0:T(8,128)(2,1)S(1)} %all-to-all-done.refs_2_, bf16[4096,256]{1,0:T(8,128)(2,1)S(1)} %copy-done.3, f32[4,128,512]{2,1,0:T(8,128)S(1)} %get-tuple-element.9.refs_4_, ...), custom_call_target="tpu_custom_call" | custom-call | flops 8589934592 | bytes 4194304 | tf_op jit(solution)/shard_map/attend/pallas_call | solution.py:179
  85.8 0.0 all-to-all-done.4
  85.8 4.1 %all-to-all-start.1 = ((bf16[4,128,640]{2,1,0:T(8,128)(2,1)}), bf16[4,128,640]{2,1,0:T(8,128)(2,1)S(1)}, u32[]{:S(2)}, u32[]{:S(2)}) async-start(bf16[4,128,640]{2,1,0:T(8,128)(2,1)} %attend.3), calls=%async_computation.1 | async-start | bytes 1310720 | tf_op jit(solution)/shard_map/all_to_all | solution.py:280
  90.0 0.0 copy-done.6
  90.0 0.6 fusion
  91.2 0.5 multiply_divide_fusion
  91.8 7.2 %all-to-all-done.1.parts_ref = bf16[4,128,640]{2,1,0:T(8,128)(2,1)S(1)} async-done(((bf16[4,128,640]{2,1,0:T(8,128)(2,1)}), bf16[4,128,640]{2,1,0:T(8,128)(2,1)S(1)}, u32[]{:S(2)}, u32[]{:S(2)}) %all-to-all-start.1) | async-done | bytes 655392 | tf_op jit(solution)/shard_map/all_to_all | solution.py:280
  99.0 0.0 copy-start.4
  99.0 0.8 copy-done.4
  99.8 2.4 %combine.1 = bf16[128,4,128]{2,1,0:T(4,128)(2,1)} custom-call(bf16[4,128,640]{2,1,0:T(8,128)(2,1)} %copy-done.4), custom_call_target="tpu_custom_call" | custom-call | tf_op jit(solution)/shard_map/combine/pallas_call | solution.py:216
  (11 shorter events, 0.2 us)
Async XLA Ops:
  7.2 14.2 %copy-start.1 = (s32[16]{0:T(128)S(1)}, s32[16]{0:T(128)}, u32[]{:S(2)}) copy-start(s32[16]{0:T(128)} %refs_0_.3) | copy-start | bytes 196
  7.2 14.4 %copy-start.2 = (s32[128]{0:T(128)S(1)}, s32[128]{0:T(128)}, u32[]{:S(2)}) copy-start(s32[128]{0:T(128)} %param.11) | copy-start | bytes 1540
  7.2 14.4 %copy-start = (bf16[128,9600]{1,0:T(8,128)(2,1)S(1)}, bf16[128,9600]{1,0:T(8,128)(2,1)}, u32[]{:S(2)}) copy-start(bf16[128,9600]{1,0:T(8,128)(2,1)} %logits_ref.1) | copy-start | bytes 7372804
  7.2 63.4 %all-gather.2.cloned.1.call-start = ((), (), s32[]{:S(2)}) async-start(), calls=%async_computation.5 | async-start | bytes 2228224 | tf_op jit(solution)/shard_map/all_gather | solution.py:241
  9.0 15.8 %copy-start.5 = (bf16[128,2,1,128]{3,1,2,0:T(2,128)(2,1)S(1)}, bf16[128,2,1,128]{3,1,2,0:T(2,128)(2,1)}, u32[]{:S(2)}) copy-start(bf16[128,2,1,128]{3,1,2,0:T(2,128)(2,1)} %param.9) | copy-start | bytes 196612
  10.8 24.7 %all-to-all-start = ((bf16[4,128,512]{2,1,0:T(8,128)(2,1)}), bf16[4,128,512]{2,1,0:T(8,128)(2,1)S(1)}, u32[]{:S(2)}, u32[]{:S(2)}) async-start(bf16[4,128,512]{2,1,0:T(8,128)(2,1)} %broadcast_in_dim.40), calls=%async_computation | async-start | bytes 1048576 | tf_op jit(solution)/shard_map/all_to_all | solution.py:228
  16.4 17.1 %collective-permute-start = (bf16[128,256]{1,0:T(8,128)(2,1)S(1)}, bf16[128,256]{1,0:T(8,128)(2,1)S(1)}, u32[]{:S(2)}, u32[]{:S(2)}) collective-permute-start(bf16[128,256]{1,0:T(8,128)(2,1)S(1)} %bitcast.38), channel_id=1, source_target_pairs={{0,64},{64,128},{128,192},{192,256},{256,320},{320,384},{384,448},... | collective-permute-start | bytes 196616 | tf_op jit(solution)/shard_map/ppermute | solution.py:251
  33.5 9.0 %collective-permute-start.1 = (bf16[128,256]{1,0:T(8,128)(2,1)S(1)}, bf16[128,256]{1,0:T(8,128)(2,1)S(1)}, u32[]{:S(2)}, u32[]{:S(2)}) collective-permute-start(bf16[128,256]{1,0:T(8,128)(2,1)S(1)} %collective-permute-done), channel_id=1, source_target_pairs={{0,64},{64,128},{128,192},{192,256},{256,320},{320,384},{384,448},... | collective-permute-start | bytes 196616 | tf_op jit(solution)/shard_map/ppermute | solution.py:252
  35.5 13.3 %all-to-all-start.2 = ((f32[8,8,128]{2,1,0:T(8,128)}), f32[8,8,128]{2,1,0:T(8,128)S(1)}, u32[]{:S(2)}, u32[]{:S(2)}) async-start(f32[8,8,128]{2,1,0:T(8,128)} %logit_stats.1), calls=%async_computation.2 | async-start | bytes 65536 | tf_op jit(solution)/shard_map/all_to_all | solution.py:247
  42.5 13.1 %collective-permute-start.2 = (bf16[384,256]{1,0:T(8,128)(2,1)S(1)}, bf16[384,256]{1,0:T(8,128)(2,1)S(1)}, u32[]{:S(2)}, u32[]{:S(2)}) collective-permute-start(bf16[384,256]{1,0:T(8,128)(2,1)S(1)} %constant_dynamic-update-slice_fusion.refs_3_), channel_id=1, source_target_pairs={{0,8},{8,0},{1,9},{9,1},{2,10},{10,2},{3,11},{11,3},{4,12},{12,4},... | collective-permute-start | bytes 589832 | tf_op jit(solution)/shard_map/ppermute | solution.py:254
  48.8 11.0 %copy-start.7 = (f32[128]{0:T(128)}, f32[128]{0:T(128)S(1)}, u32[]{:S(2)}) copy-start(f32[128]{0:T(128)S(1)} %compare_select_fusion) | copy-start | bytes 1540
  49.5 10.4 %all-to-all-start.3 = ((f32[8,1,128]{2,1,0:T(1,128)}), f32[8,1,128]{2,1,0:T(1,128)S(1)}, u32[]{:S(2)}, u32[]{:S(2)}) async-start(f32[8,1,128]{2,1,0:T(1,128)} %broadcast_in_dim.44), calls=%async_computation.3 | async-start | bytes 8192 | tf_op jit(solution)/shard_map/all_to_all | solution.py:228
  60.5 25.3 %all-to-all-start.4 = ((f32[8,1,128]{2,1,0:T(1,128)}), f32[8,1,128]{2,1,0:T(1,128)S(1)}, u32[]{:S(2)}, u32[]{:S(2)}) async-start(f32[8,1,128]{2,1,0:T(1,128)} %broadcast_in_dim.45), calls=%async_computation.4 | async-start | bytes 8192 | tf_op jit(solution)/shard_map/all_to_all | solution.py:228
  70.6 1.6 %copy-start.3 = (bf16[4096,256]{1,0:T(8,128)(2,1)S(1)}, bf16[4096,256]{1,0:T(8,128)(2,1)}, u32[]{:S(2)}) copy-start(bf16[4096,256]{1,0:T(8,128)(2,1)} %all-gather.2.cloned.1.call-done.refs_3_) | copy-start | bytes 6291460
  72.2 17.8 %copy-start.6 = (f32[16]{0:T(128)S(1)}, f32[16]{0:T(128)}, u32[]{:S(2)}) copy-start(f32[16]{0:T(128)} %param.13) | copy-start | bytes 196
  85.8 13.2 %all-to-all-start.1 = ((bf16[4,128,640]{2,1,0:T(8,128)(2,1)}), bf16[4,128,640]{2,1,0:T(8,128)(2,1)S(1)}, u32[]{:S(2)}, u32[]{:S(2)}) async-start(bf16[4,128,640]{2,1,0:T(8,128)(2,1)} %attend.3), calls=%async_computation.1 | async-start | bytes 1310720 | tf_op jit(solution)/shard_map/all_to_all | solution.py:280
  99.0 0.8 copy-start.4
Sparse Core Ops, SparseCore 0:
  10.7 59.8 all-gather.1
